TPU v7x, 32 devices: a whole 2x2x4 slice. The times are simulated.
32 devices in a mesh: hist: 16 (over z, y, x), batch: 2 (over core).
Axes of the slice: x: 2, y: 2, z: 4, core: 2. Of those that a mesh axis runs over, the one named last changes fastest.
Arguments:
- targets: bfloat16 [2, 4096, 512], P('batch', 'hist'), may hold values from -6 to 6
- w_query: bfloat16 [512, 1024], replicated, may hold values from -0.25 to 0.25
- keys: bfloat16 [2, 2048, 1024], P('batch', 'hist'), may hold values from -64 to 64
- values: bfloat16 [2, 2048, 1024], P('batch', 'hist'), may hold values from -12 to 12
- blocks: int32 [2, 8, 16], P('batch'), may hold values from 0 to 31, as said below
- lengths: int32 [2], P('batch'), may hold values from 1921 to 2048, as said below
- d_attended: bfloat16 [2, 4096, 1024], P('batch', 'hist'), may hold values from -6 to 6
Outputs:
- attended: bfloat16 [2, 4096, 1024], P('batch', 'hist')
- d_targets: bfloat16 [2, 4096, 512], P('batch', 'hist')
- d_query_weight: float32 [512, 1024], P(('hist', 'batch'))
Inputs may be any that keep to these rules, and one draw needn't show every extreme that they name: `lengths`: one user in every draw has the whole history of 2048 slots. Each list names 16 distinct blocks, all live. Its first entry is the block holding the user's last behavior; the others lie in the ranges of different hist indices (2 blocks a range), none in the range of that last block, so a range holds at most one block of a list.
All inputs are finite; a program needn't handle non-finite values.
Results may differ from a plain program's by a relative error of at most 0.01.
The roundings to bfloat16 on the way count: a program that leaves them out, or rounds other values in their place, can miss the bound.
Values may be sent and summed in bfloat16 or wider, within the bound.
No kernel may reach another device: no remote copies, remote signals or barrier semaphores. Data moves between devices by JAX's collectives and lax.ppermute only.
A program may use at most 64 MiB of HBM per device.

v0:
```python
import jax
import jax.numpy as jnp
from jax import lax
from jax.sharding import PartitionSpec as P

BLK = 64


def summarize(rows, live, block):
    count = rows.shape[0] // block
    kept = jnp.where(live[:, None], rows.astype(jnp.float32), 0.0)
    total = jnp.sum(kept.reshape(count, block, rows.shape[1]), axis=1)
    return (total * block ** (-0.5)).astype(jnp.bfloat16)


def attend(query, key_part, value_part, valid, grad, scale):
    scores = jnp.dot(query, key_part.T, preferred_element_type=jnp.float32) * scale
    masked = jnp.where(valid[None, :], scores, -jnp.inf)
    top = jnp.max(masked, axis=1, keepdims=True)
    expo = jnp.where(valid[None, :], jnp.exp(scores - top), 0.0)
    probs = expo / jnp.sum(expo, axis=1, keepdims=True)
    result = jnp.dot(probs.astype(jnp.bfloat16), value_part, preferred_element_type=jnp.float32)
    d_probs = jnp.dot(grad, value_part.T, preferred_element_type=jnp.float32)
    d_scores = probs * (d_probs - jnp.sum(probs * d_probs, axis=1, keepdims=True))
    d_query = (
        jnp.dot(d_scores.astype(jnp.bfloat16), key_part, preferred_element_type=jnp.float32) * scale
    )
    return (result, d_query)


def shards(targets, w_query, keys, values, blocks, lengths, d_attended):
    users, heads, topk = blocks.shape
    local_rows = keys.shape[1]
    width = keys.shape[2]
    head_dim = width // heads
    block = BLK
    blk_dev = local_rows // block
    n_hist = lax.axis_size("hist")
    rank = lax.axis_index("hist")
    scale = head_dim ** (-0.5)
    offsets = jnp.arange(local_rows, dtype=jnp.int32) + rank * local_rows
    user = 0
    live = offsets < lengths[user]
    summary_list = [
        jnp.concatenate(
            [summarize(keys[user], live, block), summarize(values[user], live, block)], axis=1
        )
    ]
    summaries = jnp.stack(summary_list)
    every_summary = lax.all_gather(summaries, "hist", axis=1, tiled=True)
    key_heads = keys.reshape(users, blk_dev, block, heads, head_dim)
    value_heads = values.reshape(users, blk_dev, block, heads, head_dim)
    paired = jnp.concatenate([key_heads, value_heads], axis=4)
    owner = blocks // blk_dev
    mine = owner == rank
    local_block = blocks - rank * blk_dev
    hits = mine[..., None] & (local_block[..., None] == jnp.arange(blk_dev, dtype=jnp.int32))
    per = heads * topk // n_hist
    sends = jnp.sum(hits.reshape(users, n_hist, per, blk_dev).astype(jnp.float32), axis=2)
    dest_head = jnp.arange(n_hist, dtype=jnp.int32) * per // topk
    head_pick = (dest_head[:, None] == jnp.arange(heads, dtype=jnp.int32)[None, :]).astype(
        jnp.float32
    )
    weights = (sends[:, :, :, None] * head_pick[None, :, None, :]).astype(jnp.bfloat16)
    outgoing = jnp.einsum(
        "udbh,ubthc->udtc", weights, paired, preferred_element_type=jnp.float32
    ).astype(jnp.bfloat16)
    incoming = lax.all_to_all(outgoing, "hist", split_axis=1, concat_axis=1, tiled=True)
    wanted = (
        lax.dynamic_slice_in_dim(blocks.reshape(users, heads * topk), rank * per, per, 1) // blk_dev
    )
    pick_owner = (wanted[..., None] == jnp.arange(n_hist, dtype=jnp.int32)).astype(jnp.bfloat16)
    owned_part = jnp.einsum(
        "ujo,uotc->ujtc", pick_owner, incoming, preferred_element_type=jnp.float32
    ).astype(jnp.bfloat16)
    fine = lax.all_gather(owned_part, "hist", axis=1, tiled=True).reshape(
        users, heads, topk, block, 2 * head_dim
    )
    summary_count = every_summary.shape[1]
    user = 0
    length = lengths[user]
    query = jnp.dot(targets[user], w_query, preferred_element_type=jnp.float32).astype(jnp.bfloat16)
    summary_live = jnp.arange(summary_count, dtype=jnp.int32) * block < length
    tokens = blocks[user][:, :, None] * block + jnp.arange(block, dtype=jnp.int32)[None, None, :]
    token_live = tokens.reshape(heads, topk * block) < length
    outs = []
    grads = []
    for head in range(heads):
        low = head * head_dim
        q_head = query[:, low : low + head_dim]
        g_head = d_attended[user][:, low : low + head_dim]
        coarse, coarse_dq = attend(
            q_head,
            every_summary[user, :, low : low + head_dim],
            every_summary[user, :, width + low : width + low + head_dim],
            summary_live,
            g_head,
            scale,
        )
        pair = fine[user, head].reshape(topk * block, 2 * head_dim)
        near, near_dq = attend(
            q_head, pair[:, :head_dim], pair[:, head_dim:], token_live[head], g_head, scale
        )
        outs.append(coarse + near)
        grads.append(coarse_dq + near_dq)
    attended_list = [jnp.concatenate(outs, axis=1).astype(jnp.bfloat16)]
    d_query = jnp.concatenate(grads, axis=1).astype(jnp.bfloat16)
    d_query_list = [d_query]
    d_target_list = [
        jnp.dot(d_query, w_query.T, preferred_element_type=jnp.float32).astype(jnp.bfloat16)
    ]
    user = 0
    part = targets[user]
    total = jnp.dot(part.T, d_query_list[user], preferred_element_type=jnp.float32)
    d_query_weight = lax.psum_scatter(total, ("hist", "batch"), scatter_dimension=0, tiled=True)
    return (jnp.stack(attended_list), jnp.stack(d_target_list), d_query_weight)


def solution(mesh):
    in_specs = (
        P("batch", "hist", None),
        P(),
        P("batch", "hist", None),
        P("batch", "hist", None),
        P("batch", None, None),
        P("batch"),
        P("batch", "hist", None),
    )
    out_specs = (P("batch", "hist", None), P("batch", "hist", None), P(("hist", "batch"), None))
    return jax.shard_map(shards, mesh=mesh, in_specs=in_specs, out_specs=out_specs, check_vma=False)
```

profile of v0, /device:TPU:0, one launch (start us, length us, event | category | flops | bytes accessed | tf_op | source)
XLA Modules:
  0.0 286.7 jit_solution(987677553336009141)
XLA Ops:
  7.2 0.8 fusion.205
  8.2 0.7 multiply_bitcast_fusion
  9.0 1.0 copy.107
  10.0 1.0 copy.106
  11.4 1.0 copy.66
  12.4 8.3 %all-to-all-start = ((bf16[1,16,64,256]{3,2,0,1:T(8,128)(2,1)}), bf16[1,16,64,256]{3,2,0,1:T(8,128)(2,1)S(1)}, u32[]{:S(2)}, u32[]{:S(2)}) async-start(bf16[1,16,64,256]{3,2,0,1:T(8,128)(2,1)} %copy.66), calls=%async_computation | async-start | bytes 1048576 | tf_op jit(solution)/shard_map/all_to_all | solution.py:68
  20.9 14.9 %all-to-all-done = bf16[1,16,64,256]{3,2,0,1:T(8,128)(2,1)S(1)} async-done(((bf16[1,16,64,256]{3,2,0,1:T(8,128)(2,1)}), bf16[1,16,64,256]{3,2,0,1:T(8,128)(2,1)S(1)}, u32[]{:S(2)}, u32[]{:S(2)}) %all-to-all-start) | async-done | bytes 524320 | tf_op jit(solution)/shard_map/all_to_all | solution.py:68
  35.8 1.1 convolution_convert_fusion.1
  38.2 39.1 %all-gather.2 = bf16[16,2,2048]{2,1,0:T(2,128)(2,1)S(1)} all-gather(bf16[1,2,2048]{2,1,0:T(2,128)(2,1)S(1)} %maximum_bitcast_fusion), channel_id=2, replica_groups=mesh['hist'=16,'batch'=2] {'hist'}, dimensions={0}, use_global_device_ids=true | all-gather | bytes 139264 | tf_op jit(solution)/shard_map/all_gather | solution.py:50
  81.8 0.9 fusion.172
  82.6 0.9 fusion.171
  83.5 0.9 fusion.173
  85.0 38.1 %all-gather.5.cloned.1.call-done = bf16[128,64,256]{2,0,1:T(8,128)(2,1)} async-done(((bf16[8,64,256]{2,0,1:T(8,128)(2,1)}), bf16[128,64,256]{2,0,1:T(8,128)(2,1)}) %all-gather.5.cloned.1.call-update) | async-done | bytes 4194320 | tf_op jit(solution)/shard_map/all_gather | solution.py:76
  123.1 2.5 fusion.248
  127.8 0.5 fusion.52
  130.0 0.5 fusion.56
  132.3 0.5 fusion.60
  133.2 0.5 multiply_reduce_fusion.2
  134.5 0.5 fusion.64
  135.5 0.5 multiply_reduce_fusion
  136.4 0.5 fusion.20
  137.3 0.7 fusion.22
  138.2 0.5 fusion.24
  138.9 0.5 fusion.26
  139.5 0.5 fusion.28
  140.1 0.5 fusion.30
  140.7 0.5 fusion.32
  141.3 0.5 fusion.34
  141.9 0.8 copy-done.17
  143.1 1.9 copy.96
  145.2 0.5 copy-done.43
  147.7 1.3 fusion.50
  149.1 0.5 fusion.48
  149.6 0.7 copy-done.10
  150.5 0.5 fusion.46
  151.0 0.7 copy-done.4
  151.9 0.5 fusion.44
  152.3 0.7 copy-done.14
  153.2 0.5 fusion.42
  153.7 0.7 copy-done.8
  154.6 0.5 fusion.40
  155.0 0.7 copy-done.16
  155.9 0.5 fusion.38
  156.4 0.7 copy-done.12
  157.3 0.5 fusion.36
  157.8 1.0 copy.84
  158.8 1.2 fusion.2
  160.0 119.9 %reduce-scatter.4.cloned.1.call-done = f32[16,1024]{1,0:T(8,128)} async-done(((f32[512,1024]{1,0:T(8,128)}), f32[16,1024]{1,0:T(8,128)}) %reduce-scatter.4.cloned.1.call-update) | async-done | bytes 65552
  (343 shorter events, 17.5 us)
Async XLA Ops:
  7.2 70.3 %copy-start = (bf16[512,1024]{1,0:T(8,128)(2,1)S(1)}, bf16[512,1024]{1,0:T(8,128)(2,1)}, u32[]{:S(2)}) copy-start(bf16[512,1024]{1,0:T(8,128)(2,1)} %param.8) | copy-start | bytes 3145732
  9.0 11.7 %copy-start.58 = (s32[1,8,16]{2,1,0:T(8,128)S(1)}, s32[1,8,16]{2,1,0:T(8,128)}, u32[]{:S(2)}) copy-start(s32[1,8,16]{2,1,0:T(8,128)} %param.11) | copy-start | bytes 1540
  11.0 26.9 %copy-start.35 = (bf16[1,128,1024]{2,1,0:T(8,128)(2,1)S(1)}, bf16[1,128,1024]{2,1,0:T(8,128)(2,1)}, u32[]{:S(2)}) copy-start(bf16[1,128,1024]{2,1,0:T(8,128)(2,1)} %param.9) | copy-start | bytes 786436
  11.0 26.9 %copy-start.36 = (bf16[1,128,1024]{2,1,0:T(8,128)(2,1)S(1)}, bf16[1,128,1024]{2,1,0:T(8,128)(2,1)}, u32[]{:S(2)}) copy-start(bf16[1,128,1024]{2,1,0:T(8,128)(2,1)} %param.10) | copy-start | bytes 786436
  11.4 66.1 %copy-start.37 = (bf16[1,256,512]{2,1,0:T(8,128)(2,1)S(1)}, bf16[1,256,512]{2,1,0:T(8,128)(2,1)}, u32[]{:S(2)}) copy-start(bf16[1,256,512]{2,1,0:T(8,128)(2,1)} %param.7) | copy-start | bytes 786436
  12.4 23.5 %all-to-all-start = ((bf16[1,16,64,256]{3,2,0,1:T(8,128)(2,1)}), bf16[1,16,64,256]{3,2,0,1:T(8,128)(2,1)S(1)}, u32[]{:S(2)}, u32[]{:S(2)}) async-start(bf16[1,16,64,256]{3,2,0,1:T(8,128)(2,1)} %copy.66), calls=%async_computation | async-start | bytes 1048576 | tf_op jit(solution)/shard_map/all_to_all | solution.py:68
  20.7 102.4 %all-gather.5.cloned.1.call-start = ((), (), s32[]{:S(2)}) async-start(), calls=%async_computation.2 | async-start | bytes 4456448 | tf_op jit(solution)/shard_map/all_gather | solution.py:76
  36.9 42.2 %copy-start.52 = (bf16[1,256,1024]{2,1,0:T(8,128)(2,1)S(1)}, bf16[1,256,1024]{2,1,0:T(8,128)(2,1)}, u32[]{:S(2)}) copy-start(bf16[1,256,1024]{2,1,0:T(8,128)(2,1)} %param.13) | copy-start | bytes 1572868
  37.0 242.9 %reduce-scatter.4.cloned.1.call-start = ((), (), s32[]{:S(2)}) async-start(), calls=%async_computation.3 | async-start | bytes 2162688
  78.1 6.4 %copy-start.42 = (f32[256,32]{0,1:T(8,128)}, f32[256,32]{0,1:T(8,128)S(1)}, u32[]{:S(2)}) copy-start(f32[256,32]{0,1:T(8,128)S(1)} %convolution_multiply_fusion.9) | copy-start | bytes 98308
  79.7 45.8 %copy-start.46 = (f32[256,32]{0,1:T(8,128)}, f32[256,32]{0,1:T(8,128)S(1)}, u32[]{:S(2)}) copy-start(f32[256,32]{0,1:T(8,128)S(1)} %convolution_multiply_fusion.11) | copy-start | bytes 98308
  79.9 45.7 %copy-start.44 = (f32[256,32]{0,1:T(8,128)}, f32[256,32]{0,1:T(8,128)S(1)}, u32[]{:S(2)}) copy-start(f32[256,32]{0,1:T(8,128)S(1)} %convolution_multiply_fusion.12) | copy-start | bytes 98308
  80.3 48.0 %copy-start.71 = (pred[1024]{0:T(1024)(128)(4,1)}, pred[1024]{0:T(1024)(128)(4,1)S(1)}, u32[]{:S(2)}) copy-start(pred[1024]{0:T(1024)(128)(4,1)S(1)} %get-tuple-element.22) | copy-start | bytes 3076
  80.3 48.4 %copy-start.68 = (pred[1024]{0:T(1024)(128)(4,1)}, pred[1024]{0:T(1024)(128)(4,1)S(1)}, u32[]{:S(2)}) copy-start(pred[1024]{0:T(1024)(128)(4,1)S(1)} %get-tuple-element.21) | copy-start | bytes 3076
  80.3 50.2 %copy-start.65 = (pred[1024]{0:T(1024)(128)(4,1)}, pred[1024]{0:T(1024)(128)(4,1)S(1)}, u32[]{:S(2)}) copy-start(pred[1024]{0:T(1024)(128)(4,1)S(1)} %get-tuple-element.20) | copy-start | bytes 3076
  80.4 50.7 %copy-start.62 = (pred[1024]{0:T(1024)(128)(4,1)}, pred[1024]{0:T(1024)(128)(4,1)S(1)}, u32[]{:S(2)}) copy-start(pred[1024]{0:T(1024)(128)(4,1)S(1)} %get-tuple-element.19) | copy-start | bytes 3076
  80.4 52.4 %copy-start.59 = (pred[1024]{0:T(1024)(128)(4,1)}, pred[1024]{0:T(1024)(128)(4,1)S(1)}, u32[]{:S(2)}) copy-start(pred[1024]{0:T(1024)(128)(4,1)S(1)} %get-tuple-element.18) | copy-start | bytes 3076
  125.8 15.5 %copy-start.19 = (bf16[1,1,16,64,256]{4,3,2,1,0:T(8,128)(2,1)}, bf16[1,1,16,64,256]{4,3,2,1,0:T(8,128)(2,1)S(1)}, u32[]{:S(2)}) copy-start(bf16[1,1,16,64,256]{4,3,2,1,0:T(8,128)(2,1)S(1)} %copy.105) | copy-start | bytes 1572868
  125.9 14.7 %copy-start.21 = (bf16[1,1,16,64,256]{4,3,2,1,0:T(8,128)(2,1)}, bf16[1,1,16,64,256]{4,3,2,1,0:T(8,128)(2,1)S(1)}, u32[]{:S(2)}) copy-start(bf16[1,1,16,64,256]{4,3,2,1,0:T(8,128)(2,1)S(1)} %copy.104) | copy-start | bytes 1572868
  126.1 14.0 %copy-start.23 = (bf16[1,1,16,64,256]{4,3,2,1,0:T(8,128)(2,1)}, bf16[1,1,16,64,256]{4,3,2,1,0:T(8,128)(2,1)S(1)}, u32[]{:S(2)}) copy-start(bf16[1,1,16,64,256]{4,3,2,1,0:T(8,128)(2,1)S(1)} %copy.103) | copy-start | bytes 1572868
  126.3 13.1 %copy-start.25 = (bf16[1,1,16,64,256]{4,3,2,1,0:T(8,128)(2,1)}, bf16[1,1,16,64,256]{4,3,2,1,0:T(8,128)(2,1)S(1)}, u32[]{:S(2)}) copy-start(bf16[1,1,16,64,256]{4,3,2,1,0:T(8,128)(2,1)S(1)} %copy.102) | copy-start | bytes 1572868
  126.5 12.3 %copy-start.27 = (bf16[1,1,16,64,256]{4,3,2,1,0:T(8,128)(2,1)}, bf16[1,1,16,64,256]{4,3,2,1,0:T(8,128)(2,1)S(1)}, u32[]{:S(2)}) copy-start(bf16[1,1,16,64,256]{4,3,2,1,0:T(8,128)(2,1)S(1)} %copy.101) | copy-start | bytes 1572868
  126.6 11.4 %copy-start.29 = (bf16[1,1,16,64,256]{4,3,2,1,0:T(8,128)(2,1)}, bf16[1,1,16,64,256]{4,3,2,1,0:T(8,128)(2,1)S(1)}, u32[]{:S(2)}) copy-start(bf16[1,1,16,64,256]{4,3,2,1,0:T(8,128)(2,1)S(1)} %copy.100) | copy-start | bytes 1572868
  126.8 10.1 %copy-start.31 = (bf16[1,1,16,64,256]{4,3,2,1,0:T(8,128)(2,1)}, bf16[1,1,16,64,256]{4,3,2,1,0:T(8,128)(2,1)S(1)}, u32[]{:S(2)}) copy-start(bf16[1,1,16,64,256]{4,3,2,1,0:T(8,128)(2,1)S(1)} %copy.99) | copy-start | bytes 1572868
  127.0 8.9 %copy-start.33 = (bf16[1,1,16,64,256]{4,3,2,1,0:T(8,128)(2,1)}, bf16[1,1,16,64,256]{4,3,2,1,0:T(8,128)(2,1)S(1)}, u32[]{:S(2)}) copy-start(bf16[1,1,16,64,256]{4,3,2,1,0:T(8,128)(2,1)S(1)} %copy.98) | copy-start | bytes 1572868
  127.4 8.6 %copy-start.5 = (f32[256,1024]{1,0:T(8,128)}, f32[256,1024]{1,0:T(8,128)S(1)}, u32[]{:S(2)}) copy-start(f32[256,1024]{1,0:T(8,128)S(1)} %get-tuple-element.62) | copy-start | bytes 3145732
  127.4 8.6 %copy-start.101 = (f32[256]{0:T(256)}, f32[256]{0:T(256)S(1)}, u32[]{:S(2)}) copy-start(f32[256]{0:T(256)S(1)} %get-tuple-element.61) | copy-start | bytes 3076
  127.8 9.1 %copy-start.1 = (f32[256,1024]{1,0:T(8,128)}, f32[256,1024]{1,0:T(8,128)S(1)}, u32[]{:S(2)}) copy-start(f32[256,1024]{1,0:T(8,128)S(1)} %get-tuple-element.64) | copy-start | bytes 3145732
  127.8 9.1 %copy-start.97 = (f32[256]{0:T(256)}, f32[256]{0:T(256)S(1)}, u32[]{:S(2)}) copy-start(f32[256]{0:T(256)S(1)} %get-tuple-element.63) | copy-start | bytes 3076
  128.3 7.7 %copy-start.126 = (f32[256]{0:T(256)}, f32[256]{0:T(256)S(1)}, u32[]{:S(2)}) copy-start(f32[256]{0:T(256)S(1)} %get-tuple-element.97) | copy-start | bytes 3076
  128.3 8.6 %copy-start.120 = (f32[256]{0:T(256)}, f32[256]{0:T(256)S(1)}, u32[]{:S(2)}) copy-start(f32[256]{0:T(256)S(1)} %get-tuple-element.98) | copy-start | bytes 3076
  129.6 8.4 %copy-start.9 = (f32[256,1024]{1,0:T(8,128)}, f32[256,1024]{1,0:T(8,128)S(1)}, u32[]{:S(2)}) copy-start(f32[256,1024]{1,0:T(8,128)S(1)} %get-tuple-element.66) | copy-start | bytes 3145732
  129.6 8.4 %copy-start.104 = (f32[256]{0:T(256)}, f32[256]{0:T(256)S(1)}, u32[]{:S(2)}) copy-start(f32[256]{0:T(256)S(1)} %get-tuple-element.65) | copy-start | bytes 3076
  130.0 8.7 %copy-start.3 = (f32[256,1024]{1,0:T(8,128)}, f32[256,1024]{1,0:T(8,128)S(1)}, u32[]{:S(2)}) copy-start(f32[256,1024]{1,0:T(8,128)S(1)} %get-tuple-element.69) | copy-start | bytes 3145732
  130.0 8.7 %copy-start.99 = (f32[256]{0:T(256)}, f32[256]{0:T(256)S(1)}, u32[]{:S(2)}) copy-start(f32[256]{0:T(256)S(1)} %get-tuple-element.68) | copy-start | bytes 3076
  130.5 7.5 %copy-start.129 = (f32[256]{0:T(256)}, f32[256]{0:T(256)S(1)}, u32[]{:S(2)}) copy-start(f32[256]{0:T(256)S(1)} %get-tuple-element.99) | copy-start | bytes 3076
  130.5 8.2 %copy-start.122 = (f32[256]{0:T(256)}, f32[256]{0:T(256)S(1)}, u32[]{:S(2)}) copy-start(f32[256]{0:T(256)S(1)} %get-tuple-element.100) | copy-start | bytes 3076
  131.8 7.6 %copy-start.13 = (f32[256,1024]{1,0:T(8,128)}, f32[256,1024]{1,0:T(8,128)S(1)}, u32[]{:S(2)}) copy-start(f32[256,1024]{1,0:T(8,128)S(1)} %get-tuple-element.71) | copy-start | bytes 3145732
  131.9 7.6 %copy-start.108 = (f32[256]{0:T(256)}, f32[256]{0:T(256)S(1)}, u32[]{:S(2)}) copy-start(f32[256]{0:T(256)S(1)} %get-tuple-element.70) | copy-start | bytes 3076
  132.2 7.9 %copy-start.7 = (f32[256,1024]{1,0:T(8,128)}, f32[256,1024]{1,0:T(8,128)S(1)}, u32[]{:S(2)}) copy-start(f32[256,1024]{1,0:T(8,128)S(1)} %get-tuple-element.73) | copy-start | bytes 3145732
  132.2 7.9 %copy-start.102 = (f32[256]{0:T(256)}, f32[256]{0:T(256)S(1)}, u32[]{:S(2)}) copy-start(f32[256]{0:T(256)S(1)} %get-tuple-element.72) | copy-start | bytes 3076
  132.8 6.7 %copy-start.131 = (f32[256]{0:T(256)}, f32[256]{0:T(256)S(1)}, u32[]{:S(2)}) copy-start(f32[256]{0:T(256)S(1)} %get-tuple-element.101) | copy-start | bytes 3076
  132.8 7.3 %copy-start.124 = (f32[256]{0:T(256)}, f32[256]{0:T(256)S(1)}, u32[]{:S(2)}) copy-start(f32[256]{0:T(256)S(1)} %get-tuple-element.102) | copy-start | bytes 3076
  134.1 6.6 %copy-start.15 = (f32[256,1024]{1,0:T(8,128)}, f32[256,1024]{1,0:T(8,128)S(1)}, u32[]{:S(2)}) copy-start(f32[256,1024]{1,0:T(8,128)S(1)} %get-tuple-element.75) | copy-start | bytes 3145732
  134.1 6.6 %copy-start.110 = (f32[256]{0:T(256)}, f32[256]{0:T(256)S(1)}, u32[]{:S(2)}) copy-start(f32[256]{0:T(256)S(1)} %get-tuple-element.74) | copy-start | bytes 3076
  134.5 6.8 %copy-start.11 = (f32[256,1024]{1,0:T(8,128)}, f32[256,1024]{1,0:T(8,128)S(1)}, u32[]{:S(2)}) copy-start(f32[256,1024]{1,0:T(8,128)S(1)} %get-tuple-element.77) | copy-start | bytes 3145732
  134.5 6.8 %copy-start.106 = (f32[256]{0:T(256)}, f32[256]{0:T(256)S(1)}, u32[]{:S(2)}) copy-start(f32[256]{0:T(256)S(1)} %get-tuple-element.76) | copy-start | bytes 3076
  135.0 6.3 %copy-start.127 = (f32[256]{0:T(256)}, f32[256]{0:T(256)S(1)}, u32[]{:S(2)}) copy-start(f32[256]{0:T(256)S(1)} %get-tuple-element.104) | copy-start | bytes 3076
  (90 other events, 201.7 us)
Sparse Core Ops, SparseCore 0:
  37.1 85.9 all-gather.4
  145.3 134.5 reduce-scatter.3
where the time goes:
time: 287 us
  waiting for transfers between devices  173 us (60%)
  blocking collectives  39.1 us (14%)
  matrix products  27.2 us (9%)
  local copies, waits for them, and re-layouts  18.4 us (6%)
  between operations  16.6 us (6%)
  starting transfers between devices  8.4 us (3%)
  other arithmetic  4.06 us (1%)
    unnamed x3, waiting for transfers between devices  120 us
    all_gather x1, blocking collectives, shards(): every_summary = lax.all_gather(summaries, 'hist', axis=1, tiled=True)  39.1 us
    all_gather x1, waiting for transfers between devices, shards(): lax.all_gather(owned_part, 'hist', axis=1, tiled=True)  38.1 us
    all_to_all x1, waiting for transfers between devices, shards(): lax.all_to_all(outgoing, 'hist', split_axis=1, concat_axis=1, tiled=True)  14.9 us
    unnamed x282, local copies, waits for them, and re-layouts  14.2 us
    all_to_all x1, starting transfers between devices, shards(): lax.all_to_all(outgoing, 'hist', split_axis=1, concat_axis=1, tiled=True)  8.31 us
    dot_general x16, matrix products, attend(): jnp.dot(d_scores.astype(jnp.bfloat16), key_part, preferred_element_type=j...  8.27 us
    dot_general x16, matrix products, attend(): jnp.dot(probs.astype(jnp.bfloat16), value_part, preferred_element_type=jn...  6.22 us
  transfers between devices with their start and end apart: 3, of which 3 were waited for; matrix products, arithmetic and copies ran while one was open for 6% of the time, Pallas kernels for 0%

commit v1 on v0

v1 whole, which is shorter than its diff:
```python
import functools

import jax
import jax.numpy as jnp
from jax import lax
from jax.experimental import pallas as pl
from jax.experimental.pallas import tpu as pltpu
from jax.sharding import PartitionSpec as P

BLK = 64
LANES = 128
QUAD = 4
DEAD = -1e30
VMEM_LIMIT = 60 * 1024 * 1024
F32 = jnp.float32
BF16 = jnp.bfloat16


def swap(array, axis, mask):
    size = lax.axis_size(axis)
    return lax.ppermute(array, axis, [(i, i ^ mask) for i in range(size)])


def select_kernel(cuts, blocks_ref, lengths_ref, keys_ref, values_ref, *outs):
    heads, topk = blocks_ref.shape[1:]
    rows, width = keys_ref.shape[1:]
    head_dim = width // heads
    blk_dev = rows // BLK
    rank = lax.axis_index("hist")
    length = lengths_ref[0]
    for out, (first, last) in zip(outs, cuts):
        for head in range(first, last):
            local = jnp.int32(0)
            for entry in range(topk):
                block = blocks_ref[0, head, entry] - rank * blk_dev
                local = jnp.where((block >= 0) & (block < blk_dev), block, local)
            low = pl.multiple_of(local * BLK, BLK)
            at = (head - first) * BLK
            columns = slice(head * head_dim, (head + 1) * head_dim)
            out[at : at + BLK, :head_dim] = keys_ref[0, pl.ds(low, BLK), columns]
            out[at : at + BLK, head_dim:] = values_ref[0, pl.ds(low, BLK), columns]
    sums = []
    for source in (keys_ref, values_ref):
        totals = []
        for block in range(blk_dev):
            part = source[0, block * BLK : (block + 1) * BLK, :].astype(F32)
            spot = lax.broadcasted_iota(jnp.int32, part.shape, 0) + (
                rank * rows + block * BLK
            )
            part = jnp.where(spot < length, part, 0.0)
            totals.append(jnp.sum(part, axis=0, keepdims=True) * BLK ** (-0.5))
        sums.append(
            jnp.concatenate(
                [
                    totals[block][:, head * head_dim : (head + 1) * head_dim]
                    for head in range(heads)
                    for block in range(blk_dev)
                ],
                axis=0,
            )
        )
    at = (cuts[0][1] - cuts[0][0]) * BLK
    count = heads * blk_dev
    outs[0][at : at + count, :head_dim] = sums[0].astype(BF16)
    outs[0][at : at + count, head_dim:] = sums[1].astype(BF16)


def attend_kernel(pieces, fine_width, scale, *refs):
    query_ref, grad_ref, bias_ref, summary_ref = refs[:4]
    piece_refs = refs[4 : 4 + pieces]
    out_ref, dq_ref = refs[-2:]
    head_dim = query_ref.shape[1]
    keys = jnp.concatenate(
        [r[:, :, :head_dim].reshape(-1, head_dim) for r in piece_refs]
        + [summary_ref[0, :, :head_dim]],
        axis=0,
    )
    values = jnp.concatenate(
        [r[:, :, head_dim:].reshape(-1, head_dim) for r in piece_refs]
        + [summary_ref[0, :, head_dim:]],
        axis=0,
    )
    bias = bias_ref[0]
    cols = (slice(0, fine_width), slice(fine_width, keys.shape[0]))
    step = min(128, query_ref.shape[0])
    contract = (((1,), (1,)), ((), ()))
    for low in range(0, query_ref.shape[0], step):
        rows = slice(low, low + step)
        query = query_ref[rows, :]
        grad = grad_ref[0, rows, :]
        scores = lax.dot_general(query, keys, contract, preferred_element_type=F32) * scale + bias
        d_probs = lax.dot_general(grad, values, contract, preferred_element_type=F32)
        probs_parts = []
        d_parts = []
        for part in cols:
            score = scores[:, part]
            expo = jnp.exp(score - jnp.max(score, axis=1, keepdims=True))
            probs = expo * (1.0 / jnp.sum(expo, axis=1, keepdims=True))
            d_prob = d_probs[:, part]
            delta = jnp.sum(probs * d_prob, axis=1, keepdims=True)
            probs_parts.append(probs.astype(BF16))
            d_parts.append((probs * (d_prob - delta)).astype(BF16))
        out = jnp.dot(jnp.concatenate(probs_parts, axis=1), values, preferred_element_type=F32)
        d_query = jnp.dot(jnp.concatenate(d_parts, axis=1), keys, preferred_element_type=F32)
        out_ref[0, rows, :] = out.astype(BF16)
        dq_ref[0, rows, :] = (d_query * scale).astype(BF16)


def attend(first, count, query, grad, bias, summary, pieces, earlier):
    rows, width = query.shape
    heads = bias.shape[0]
    head_dim = width // heads
    fine_width = sum(p.shape[0] for p in pieces) * BLK
    whole = pl.BlockSpec((1, rows, head_dim), lambda i: (0, 0, first + i))
    in_specs = [
        pl.BlockSpec((rows, head_dim), lambda i: (0, first + i)),
        whole,
        pl.BlockSpec((1,) + bias.shape[1:], lambda i: (first + i, 0, 0)),
        pl.BlockSpec((1,) + summary.shape[1:], lambda i: (first + i, 0, 0)),
    ]
    in_specs += [
        pl.BlockSpec((p.shape[0], BLK, 2 * head_dim), lambda i: (0, i, 0)) for p in pieces
    ]
    args = [query, grad, bias, summary, *pieces]
    aliases = {}
    if earlier is not None:
        aliases = {len(args): 0, len(args) + 1: 1}
        args += list(earlier)
        in_specs += [pl.BlockSpec(memory_space=pl.ANY)] * 2
    shape = jax.ShapeDtypeStruct((1, rows, width), BF16)
    columns = bias.shape[-1]
    return pl.pallas_call(
        functools.partial(attend_kernel, len(pieces), fine_width, head_dim ** (-0.5)),
        grid=(count,),
        in_specs=in_specs,
        out_specs=(whole, whole),
        out_shape=(shape, shape),
        input_output_aliases=aliases,
        compiler_params=pltpu.CompilerParams(vmem_limit_bytes=VMEM_LIMIT),
        cost_estimate=pl.CostEstimate(
            flops=8 * count * rows * columns * head_dim,
            bytes_accessed=count * (columns * 512 + rows * head_dim * 8),
            transcendentals=count * rows * columns,
        ),
        name="attend",
    )(*args)


def gather(part, sync):
    size = lax.axis_size("hist")
    if sync is not None:
        part, _ = lax.optimization_barrier((part, sync))
    column = jnp.stack(
        [part] + [swap(part, "hist", QUAD * k) for k in range(1, size // QUAD)]
    )
    half = column.shape[0] // 2
    across = swap(column, "hist", 1)
    along = swap(column, "hist", 2)
    far = (swap(across[:half], "hist", 2), swap(along[half:], "hist", 1))
    return (column, across, along) + far


def spread(total, axis, masks, weight):
    result = total[0]
    for index in range(1, masks):
        result = result + swap(total[index].astype(BF16), axis, weight * index).astype(F32)
    return result


def shards(targets, w_query, keys, values, blocks, lengths, d_attended):
    heads = blocks.shape[1]
    local_rows, width = keys.shape[1:]
    head_dim = width // heads
    blk_dev = local_rows // BLK
    n_hist = lax.axis_size("hist")
    n_batch = lax.axis_size("batch")
    rank = lax.axis_index("hist")
    lane = lax.axis_index("batch")
    rows = targets.shape[1]
    depth = targets.shape[2]

    cut = heads // 2
    cuts = ((0, cut), (cut, heads))
    sizes = [(last - first) * BLK for first, last in cuts]
    sizes[0] += heads * blk_dev
    picked = pl.pallas_call(
        functools.partial(select_kernel, cuts),
        in_specs=[
            pl.BlockSpec(memory_space=pltpu.SMEM),
            pl.BlockSpec(memory_space=pltpu.SMEM),
            pl.BlockSpec(memory_space=pltpu.VMEM),
            pl.BlockSpec(memory_space=pltpu.VMEM),
        ],
        out_specs=[pl.BlockSpec(memory_space=pltpu.VMEM)] * len(cuts),
        out_shape=[jax.ShapeDtypeStruct((size, 2 * head_dim), BF16) for size in sizes],
        name="select",
    )(blocks, lengths, keys, values)

    near = gather(picked[0], None)
    late = gather(picked[1], near[0])

    query = jnp.dot(targets[0], w_query, preferred_element_type=F32).astype(BF16)

    masks = jnp.asarray([q + QUAD * k for q in range(QUAD) for k in range(n_hist // QUAD)], jnp.int32)
    source = rank ^ masks
    owner = blocks[0] // blk_dev
    listed = jnp.max(
        jnp.where(owner[:, :, None] == source[None, None, :], blocks[0][:, :, None], -1), axis=1
    )
    spots = jnp.arange(BLK, dtype=jnp.int32)
    live = (listed[:, :, None] >= 0) & (listed[:, :, None] * BLK + spots < lengths[0])
    fine_bias = jnp.where(live, 0.0, DEAD).astype(F32).reshape(heads, -1)
    names = (source[:, None] * blk_dev + jnp.arange(blk_dev, dtype=jnp.int32)).reshape(-1)
    padded = -(-names.shape[0] // LANES) * LANES
    extra = padded - names.shape[0]
    coarse_bias = jnp.where(names * BLK < lengths[0], 0.0, DEAD).astype(F32)
    coarse_bias = jnp.pad(coarse_bias, (0, extra), constant_values=DEAD)
    bias = jnp.concatenate(
        [fine_bias, jnp.broadcast_to(coarse_bias[None], (heads, padded))], axis=1
    )[:, None, :]
    start = sizes[0] - heads * blk_dev
    summary = jnp.concatenate([p[:, start:] for p in near], axis=0)
    summary = summary.reshape(n_hist, heads, blk_dev, 2 * head_dim).transpose(1, 0, 2, 3)
    summary = summary.reshape(heads, n_hist * blk_dev, 2 * head_dim)
    summary = jnp.pad(summary, ((0, 0), (0, extra), (0, 0)))

    places = (
        (rank ^ masks)[None, :] * n_batch + (lane ^ jnp.arange(n_batch, dtype=jnp.int32))[:, None]
    ).reshape(-1)
    share = depth // (n_hist * n_batch)
    chosen = (places[:, None] * share + jnp.arange(share, dtype=jnp.int32)).reshape(-1)
    shuffle = (jnp.arange(depth, dtype=jnp.int32)[:, None] == chosen[None, :]).astype(BF16)
    ordered = jnp.dot(targets[0], shuffle, preferred_element_type=F32).astype(BF16)

    done = attend(0, cut, query, d_attended, bias, summary, near, None)
    attended, d_query = attend(cut, heads - cut, query, d_attended, bias, summary, late, done)

    total = lax.dot_general(
        ordered, d_query[0], (((0,), (0,)), ((), ())), preferred_element_type=F32
    )
    total = total.reshape(n_batch, QUAD, n_hist // QUAD, share, width)
    total = spread(total, "batch", n_batch, 1)
    total = spread(total, "hist", QUAD, 1)
    d_query_weight = spread(total, "hist", n_hist // QUAD, QUAD)
    d_targets = lax.dot_general(
        d_query[0], w_query, (((1,), (1,)), ((), ())), preferred_element_type=F32
    ).astype(BF16)
    return (attended, d_targets[None], d_query_weight)


def solution(mesh):
    in_specs = (
        P("batch", "hist", None),
        P(),
        P("batch", "hist", None),
        P("batch", "hist", None),
        P("batch", None, None),
        P("batch"),
        P("batch", "hist", None),
    )
    out_specs = (P("batch", "hist", None), P("batch", "hist", None), P(("hist", "batch"), None))
    return jax.shard_map(shards, mesh=mesh, in_specs=in_specs, out_specs=out_specs, check_vma=False)
```

time: 287 us -> 98.4 us (0.34)
  waiting for transfers between devices: 173 us -> 31.9 us
  blocking collectives: 39.1 us -> 0 us
  matrix products: 27.2 us -> 5.26 us
  starting transfers between devices: 8.4 us -> 28.6 us
  Pallas kernels: 0 us -> 18 us
  between operations: 16.6 us -> 1.64 us
  local copies, waits for them, and re-layouts: 18.4 us -> 9.03 us
    unnamed x3 -> x0, waiting for transfers between devices: 120 us -> none
    all_gather x1 -> x0, blocking collectives: 39.1 us -> none  [shards(): every_summary = lax.all_gather(summaries, 'hist', axis=1, tiled=True)]
    all_gather x1 -> x0, waiting for transfers between devices: 38.1 us -> none  [shards(): lax.all_gather(owned_part, 'hist', axis=1, tiled=True)]
    ppermute x0 -> x21, waiting for transfers between devices: none -> 31.9 us  [swap(): return lax.ppermute(array, axis, [(i, i ^ mask) for i in range(size)])]
    ppermute x0 -> x21, starting transfers between devices: none -> 28.6 us  [swap(): return lax.ppermute(array, axis, [(i, i ^ mask) for i in range(size)])]
    dot_general x69 -> x3, matrix products: 27.2 us -> 5.26 us  [the longest x1 2.18 us: shards(): jnp.dot(targets[0], w_query, preferred_element_type=F32).astype(BF16)]
    pallas_call x0 -> x3, Pallas kernels: none -> 18 us  [the longest x2 15.9 us: attend(): pl.pallas_call(functools.partial(attend_kernel, len(pieces), fine_width,...]
    all_to_all x1 -> x0, waiting for transfers between devices: 14.9 us -> none  [shards(): lax.all_to_all(outgoing, 'hist', split_axis=1, concat_axis=1, tiled=True)]
  transfers between devices with their start and end apart: 3 -> 21, of which waited for: 3 -> 10; matrix products, arithmetic and copies ran while one was open for 6% -> 14% of each run, Pallas kernels for 0% -> 8%
where the time goes in v1:
time: 98.4 us; the launch traced here: 97.8 us
  waiting for transfers between devices  31.9 us (32%)
  starting transfers between devices  28.6 us (29%)
  Pallas kernels  18 us (18%)
  local copies, waits for them, and re-layouts  9.03 us (9%)
  matrix products  5.26 us (5%)
  other arithmetic  3.47 us (4%)
  between operations  1.64 us (2%)
    ppermute x21, waiting for transfers between devices, swap(): return lax.ppermute(array, axis, [(i, i ^ mask) for i in range(size)])  31.9 us
    ppermute x21, starting transfers between devices, swap(): return lax.ppermute(array, axis, [(i, i ^ mask) for i in range(size)])  28.6 us
    pallas_call x2, Pallas kernels, attend(): pl.pallas_call(functools.partial(attend_kernel, len(pieces), fine_width,...  15.9 us
    slice x4, local copies, waits for them, and re-layouts, gather(): far = (swap(across[:half], 'hist', 2), swap(along[half:], 'hist', 1))  3.45 us
    unnamed x26, local copies, waits for them, and re-layouts  3.01 us
    dot_general x1, matrix products, shards(): jnp.dot(targets[0], w_query, preferred_element_type=F32).astype(BF16)  2.18 us
    pallas_call x1, Pallas kernels, shards(): pl.pallas_call(functools.partial(select_kernel, cuts), in_specs=[pl.Block...  2.05 us
  transfers between devices with their start and end apart: 21, of which 10 were waited for; matrix products, arithmetic and copies ran while one was open for 14% of the time, Pallas kernels for 8%

profile of v1, /device:TPU:0, one launch (start us, length us, event | category | flops | bytes accessed | tf_op | source)
XLA Modules:
  0.0 97.8 jit_solution(14014670489710913880)
XLA Ops:
  1.4 2.1 %select.22 = (bf16[272,256]{1,0:T(8,128)(2,1)}, bf16[256,256]{1,0:T(8,128)(2,1)}) custom-call(s32[1,8,16]{2,1,0:T(8,128)} %blocks_ref.1, s32[1]{0:T(128)} %copy.24.lengths_ref, bf16[1,128,1024]{2,1,0:T(8,128)(2,1)} %keys_ref.1, bf16[1,128,1024]{2,1,0:T(8,128)(2,1)} %values_ref.1), custom_call_target="tpu_custom_call" | custom-call | tf_op jit(solution)/shard_map/select/pallas_call | solution.py:186
  3.4 3.0 %collective-permute-start = (bf16[272,256]{1,0:T(8,128)(2,1)}, bf16[272,256]{1,0:T(8,128)(2,1)S(1)}, u32[]{:S(2)}, u32[]{:S(2)}) collective-permute-start(bf16[272,256]{1,0:T(8,128)(2,1)} %get-tuple-element.10), channel_id=1, source_target_pairs={{0,8},{2,10},{4,12},{6,14},{8,0},{10,2},{12,4},{14,6},{16,24},{18,... | collective-permute-start | bytes 417800 | tf_op jit(solution)/shard_map/ppermute | solution.py:21
  6.5 2.6 %collective-permute-start.1 = (bf16[272,256]{1,0:T(8,128)(2,1)}, bf16[272,256]{1,0:T(8,128)(2,1)S(1)}, u32[]{:S(2)}, u32[]{:S(2)}) collective-permute-start(bf16[272,256]{1,0:T(8,128)(2,1)} %get-tuple-element.10), channel_id=1, source_target_pairs={{0,16},{2,18},{4,20},{6,22},{8,24},{10,26},{12,28},{14,30},{16,0},... | collective-permute-start | bytes 417800 | tf_op jit(solution)/shard_map/ppermute | solution.py:21
  9.1 0.7 add_select_fusion
  9.8 0.7 broadcast_multiply_fusion.1
  10.4 0.8 select_reduce_fusion
  11.9 0.6 broadcast_in_dim.58.refs_2_
  12.7 2.2 %convolution_convert_fusion.refs_0_ = bf16[256,1024]{1,0:T(8,128)(2,1)} fusion(bf16[512,1024]{1,0:T(8,128)(2,1)S(1)} %copy-done, bf16[1,256,512]{2,1,0:T(8,128)(2,1)} %param.8), kind=kOutput, calls=%fused_computation | convolution fusion | flops 268697600 | bytes 1835008 | tf_op jit(solution)/shard_map/dot_general | solution.py:202
  14.9 5.3 %collective-permute-done.1 = bf16[272,256]{1,0:T(8,128)(2,1)S(1)} collective-permute-done((bf16[272,256]{1,0:T(8,128)(2,1)}, bf16[272,256]{1,0:T(8,128)(2,1)S(1)}, u32[]{:S(2)}, u32[]{:S(2)}) %collective-permute-start.1) | collective-permute-done | bytes 139296 | tf_op jit(solution)/shard_map/ppermute | solution.py:21
  20.2 1.6 %collective-permute-start.3 = (bf16[4,272,256]{2,1,0:T(8,128)(2,1)S(1)}, bf16[4,272,256]{2,1,0:T(8,128)(2,1)}, u32[]{:S(2)}, u32[]{:S(2)}) collective-permute-start(bf16[4,272,256]{2,1,0:T(8,128)(2,1)S(1)} %pad_maximum_fusion.refs_4_), channel_id=1, source_target_pairs={{0,2},{2,0},{4,6},{6,4},{8,10},{10,8},{12,14},{14,12},{16,18},{18,... | collective-permute-start | bytes 1671176 | tf_op jit(solution)/shard_map/ppermute | solution.py:21
  21.8 1.5 %collective-permute-start.4 = (bf16[4,272,256]{2,1,0:T(8,128)(2,1)S(1)}, bf16[4,272,256]{2,1,0:T(8,128)(2,1)}, u32[]{:S(2)}, u32[]{:S(2)}) collective-permute-start(bf16[4,272,256]{2,1,0:T(8,128)(2,1)S(1)} %pad_maximum_fusion.refs_4_), channel_id=1, source_target_pairs={{0,4},{2,6},{4,0},{6,2},{8,12},{10,14},{12,8},{14,10},{16,20},{18,... | collective-permute-start | bytes 1671176 | tf_op jit(solution)/shard_map/ppermute | solution.py:21
  23.3 3.1 %collective-permute-start.8 = (bf16[256,256]{1,0:T(8,128)(2,1)S(1)}, bf16[256,256]{1,0:T(8,128)(2,1)S(1)}, u32[]{:S(2)}, u32[]{:S(2)}) collective-permute-start(bf16[256,256]{1,0:T(8,128)(2,1)S(1)} %copy-done.8), channel_id=1, source_target_pairs={{0,16},{2,18},{4,20},{6,22},{8,24},{10,26},{12,28},{14,30},{16,0},... | collective-permute-start | bytes 393224 | tf_op jit(solution)/shard_map/ppermute | solution.py:21
  26.4 1.4 %collective-permute-start.9 = (bf16[256,256]{1,0:T(8,128)(2,1)S(1)}, bf16[256,256]{1,0:T(8,128)(2,1)S(1)}, u32[]{:S(2)}, u32[]{:S(2)}) collective-permute-start(bf16[256,256]{1,0:T(8,128)(2,1)S(1)} %copy-done.8), channel_id=1, source_target_pairs={{0,24},{2,26},{4,28},{6,30},{8,16},{10,18},{12,20},{14,22},{16,8},... | collective-permute-start | bytes 393224 | tf_op jit(solution)/shard_map/ppermute | solution.py:21
  28.0 7.1 %collective-permute-done.8 = bf16[256,256]{1,0:T(8,128)(2,1)S(1)} collective-permute-done((bf16[256,256]{1,0:T(8,128)(2,1)S(1)}, bf16[256,256]{1,0:T(8,128)(2,1)S(1)}, u32[]{:S(2)}, u32[]{:S(2)}) %collective-permute-start.8) | collective-permute-done | bytes 131104 | tf_op jit(solution)/shard_map/ppermute | solution.py:21
  35.1 0.3 collective-permute-done.7
  35.5 0.6 collective-permute-start.10
  36.1 0.5 collective-permute-start.11
  36.6 1.0 slice.88
  37.6 1.6 %collective-permute-start.5 = (bf16[2,272,256]{2,1,0:T(8,128)(2,1)S(1)}, bf16[2,272,256]{2,1,0:T(8,128)(2,1)S(1)}, u32[]{:S(2)}, u32[]{:S(2)}) collective-permute-start(bf16[2,272,256]{2,1,0:T(8,128)(2,1)S(1)} %slice.88), channel_id=1, source_target_pairs={{0,4},{2,6},{4,0},{6,2},{8,12},{10,14},{12,8},{14,10},{16,20},{18,... | collective-permute-start | bytes 835592 | tf_op jit(solution)/shard_map/ppermute | solution.py:21
  39.2 1.0 slice.90
  40.2 1.6 %collective-permute-start.6 = (bf16[2,272,256]{2,1,0:T(8,128)(2,1)S(1)}, bf16[2,272,256]{2,1,0:T(8,128)(2,1)S(1)}, u32[]{:S(2)}, u32[]{:S(2)}) collective-permute-start(bf16[2,272,256]{2,1,0:T(8,128)(2,1)S(1)} %slice.90), channel_id=1, source_target_pairs={{0,2},{2,0},{4,6},{6,4},{8,10},{10,8},{12,14},{14,12},{16,18},{18,... | collective-permute-start | bytes 835592 | tf_op jit(solution)/shard_map/ppermute | solution.py:21
  41.7 0.8 slice_dynamic-update-slice_fusion.1
  42.5 0.8 slice_dynamic-update-slice_fusion
  43.2 7.2 %collective-permute-done.10.refs_5_ = bf16[4,256,256]{2,1,0:T(8,128)(2,1)S(1)} collective-permute-done((bf16[4,256,256]{2,1,0:T(8,128)(2,1)S(1)}, bf16[4,256,256]{2,1,0:T(8,128)(2,1)S(1)}, u32[]{:S(2)}, u32[]{:S(2)}) %collective-permute-start.10) | collective-permute-done | bytes 524320 | tf_op jit(solution)/shard_map/ppermute | solution.py:21
  50.4 0.8 slice.92
  51.2 0.5 collective-permute-start.12
  51.7 0.7 slice.93
  52.4 0.8 collective-permute-start.13
  53.2 2.0 %collective-permute-done.5.refs_7_ = bf16[2,272,256]{2,1,0:T(8,128)(2,1)S(1)} collective-permute-done((bf16[2,272,256]{2,1,0:T(8,128)(2,1)S(1)}, bf16[2,272,256]{2,1,0:T(8,128)(2,1)S(1)}, u32[]{:S(2)}, u32[]{:S(2)}) %collective-permute-start.5) | collective-permute-done | bytes 278560 | tf_op jit(solution)/shard_map/ppermute | solution.py:21
  55.2 0.7 copy-done.9
  55.9 0.7 copy-done.10
  56.9 0.8 pad.9.refs_3_
  57.7 7.9 %attend.2 = (bf16[1,256,1024]{2,1,0:T(8,128)(2,1)}, bf16[1,256,1024]{2,1,0:T(8,128)(2,1)}) custom-call(bf16[256,1024]{1,0:T(8,128)(2,1)} %convolution_convert_fusion.refs_0_, bf16[1,256,1024]{2,1,0:T(8,128)(2,1)} %refs_1_.3, f32[8,1,1152]{2,1,0:T(1,128)} %broadcast_in_dim.58.refs_2_, bf16[8,128,256]{2,1,0:T(8,128)(2,1)} %pad.9.refs_3_, ...), custom_call_target="tpu_custom_call" | custom-call | flops 1207959552 | bytes 3407872 | tf_op jit(solution)/shard_map/attend/pallas_call | solution.py:132
  65.7 8.0 %attend.3 = (bf16[1,256,1024]{2,1,0:T(8,128)(2,1)}, bf16[1,256,1024]{2,1,0:T(8,128)(2,1)}) custom-call(bf16[256,1024]{1,0:T(8,128)(2,1)} %convolution_convert_fusion.refs_0_, bf16[1,256,1024]{2,1,0:T(8,128)(2,1)} %refs_1_.3, f32[8,1,1152]{2,1,0:T(1,128)} %broadcast_in_dim.58.refs_2_, ...), custom_call_target="tpu_custom_call", output_to_operand_aliasing={{0}: (9, {}), {1}: (10, {})} | custom-call | flops 1207959552 | bytes 3407872 | tf_op jit(solution)/shard_map/attend/pallas_call | solution.py:132
  73.7 1.9 %fusion = f32[512,1024]{1,0:T(8,128)S(1)} fusion(bf16[1,256,1024]{2,1,0:T(8,128)(2,1)} %get-tuple-element.16, s32[512]{0:T(512)S(1)} %add.119, bf16[1,256,512]{2,1,0:T(8,128)(2,1)S(1)} %copy-done.5), kind=kOutput, calls=%fused_computation.3 | convolution fusion | flops 403308544 | bytes 2885632 | tf_op jit(solution)/shard_map/dot_general | solution.py:238
  75.9 1.8 %collective-permute-done.14 = bf16[4,4,16,1024]{3,2,1,0:T(8,128)(2,1)S(1)} collective-permute-done((bf16[4,4,16,1024]{3,2,1,0:T(8,128)(2,1)S(1)}, bf16[4,4,16,1024]{3,2,1,0:T(8,128)(2,1)S(1)}, u32[]{:S(2)}, u32[]{:S(2)}) %collective-permute-start.14) | collective-permute-done | bytes 524320 | tf_op jit(solution)/shard_map/ppermute | solution.py:21
  77.6 0.2 fusion.25
  77.9 1.6 %collective-permute-start.15 = (bf16[4,16,1024]{2,1,0:T(8,128)(2,1)S(1)}, bf16[4,16,1024]{2,1,0:T(8,128)(2,1)S(1)}, u32[]{:S(2)}, u32[]{:S(2)}) collective-permute-start(bf16[4,16,1024]{2,1,0:T(8,128)(2,1)S(1)} %get-tuple-element.21), channel_id=1, source_target_pairs={{0,2},{2,0},{4,6},{6,4},{8,10},{10,8},{12,14},{14,12},{16,18},{18,... | collective-permute-start | bytes 393224 | tf_op jit(solution)/shard_map/ppermute | solution.py:21
  79.5 0.5 collective-permute-start.16
  80.0 1.5 %collective-permute-start.17 = (bf16[4,16,1024]{2,1,0:T(8,128)(2,1)S(1)}, bf16[4,16,1024]{2,1,0:T(8,128)(2,1)S(1)}, u32[]{:S(2)}, u32[]{:S(2)}) collective-permute-start(bf16[4,16,1024]{2,1,0:T(8,128)(2,1)S(1)} %get-tuple-element.22), channel_id=1, source_target_pairs={{0,6},{2,4},{4,2},{6,0},{8,14},{10,12},{12,10},{14,8},{16,22},{18,... | collective-permute-start | bytes 393224 | tf_op jit(solution)/shard_map/ppermute | solution.py:21
  81.5 2.4 %collective-permute-done.15 = bf16[4,16,1024]{2,1,0:T(8,128)(2,1)S(1)} collective-permute-done((bf16[4,16,1024]{2,1,0:T(8,128)(2,1)S(1)}, bf16[4,16,1024]{2,1,0:T(8,128)(2,1)S(1)}, u32[]{:S(2)}, u32[]{:S(2)}) %collective-permute-start.15) | collective-permute-done | bytes 131104 | tf_op jit(solution)/shard_map/ppermute | solution.py:21
  83.8 3.7 %collective-permute-done.16 = bf16[4,16,1024]{2,1,0:T(8,128)(2,1)S(1)} collective-permute-done((bf16[4,16,1024]{2,1,0:T(8,128)(2,1)S(1)}, bf16[4,16,1024]{2,1,0:T(8,128)(2,1)S(1)}, u32[]{:S(2)}, u32[]{:S(2)}) %collective-permute-start.16) | collective-permute-done | bytes 131104 | tf_op jit(solution)/shard_map/ppermute | solution.py:21
  87.6 3.8 %collective-permute-start.18 = (bf16[16,1024]{1,0:T(8,128)(2,1)S(1)}, bf16[16,1024]{1,0:T(8,128)(2,1)S(1)}, u32[]{:S(2)}, u32[]{:S(2)}) collective-permute-start(bf16[16,1024]{1,0:T(8,128)(2,1)S(1)} %get-tuple-element.24), channel_id=1, source_target_pairs={{0,8},{2,10},{4,12},{6,14},{8,0},{10,2},{12,4},{14,6},{16,24},{18,... | collective-permute-start | bytes 98312 | tf_op jit(solution)/shard_map/ppermute | solution.py:21
  91.5 2.4 %collective-permute-start.20 = (bf16[16,1024]{1,0:T(8,128)(2,1)S(1)}, bf16[16,1024]{1,0:T(8,128)(2,1)S(1)}, u32[]{:S(2)}, u32[]{:S(2)}) collective-permute-start(bf16[16,1024]{1,0:T(8,128)(2,1)S(1)} %get-tuple-element.25), channel_id=1, source_target_pairs={{0,24},{2,26},{4,28},{6,30},{8,16},{10,18},{12,20},{14,22},{16,8},... | collective-permute-start | bytes 98312 | tf_op jit(solution)/shard_map/ppermute | solution.py:21
  93.9 1.2 %fusion.1 = bf16[1,256,512]{2,1,0:T(8,128)(2,1)} fusion(bf16[512,1024]{1,0:T(8,128)(2,1)S(1)} %copy-done, bf16[1,256,1024]{2,1,0:T(8,128)(2,1)S(1)} %copy-done.1), kind=kOutput, calls=%fused_computation.4 | convolution fusion | flops 268566528 | bytes 1835008 | tf_op jit(solution)/shard_map/dot_general | solution.py:245
  95.1 1.2 %collective-permute-done.19 = bf16[16,1024]{1,0:T(8,128)(2,1)S(1)} collective-permute-done((bf16[16,1024]{1,0:T(8,128)(2,1)S(1)}, bf16[16,1024]{1,0:T(8,128)(2,1)S(1)}, u32[]{:S(2)}, u32[]{:S(2)}) %collective-permute-start.19) | collective-permute-done | bytes 32800 | tf_op jit(solution)/shard_map/ppermute | solution.py:21
  96.3 0.9 collective-permute-done.20
  97.2 0.6 fusion.17
  (66 shorter events, 1.7 us)
Async XLA Ops:
  0.6 12.1 %copy-start = (bf16[512,1024]{1,0:T(8,128)(2,1)S(1)}, bf16[512,1024]{1,0:T(8,128)(2,1)}, u32[]{:S(2)}) copy-start(bf16[512,1024]{1,0:T(8,128)(2,1)} %param.9) | copy-start | bytes 3145732
  3.4 16.7 %copy-start.7 = (bf16[272,256]{1,0:T(8,128)(2,1)S(1)}, bf16[272,256]{1,0:T(8,128)(2,1)}, u32[]{:S(2)}) copy-start(bf16[272,256]{1,0:T(8,128)(2,1)} %get-tuple-element.10) | copy-start | bytes 417796
  3.4 19.9 %copy-start.8 = (bf16[256,256]{1,0:T(8,128)(2,1)S(1)}, bf16[256,256]{1,0:T(8,128)(2,1)}, u32[]{:S(2)}) copy-start(bf16[256,256]{1,0:T(8,128)(2,1)} %get-tuple-element.12) | copy-start | bytes 393220
  3.4 11.4 %collective-permute-start = (bf16[272,256]{1,0:T(8,128)(2,1)}, bf16[272,256]{1,0:T(8,128)(2,1)S(1)}, u32[]{:S(2)}, u32[]{:S(2)}) collective-permute-start(bf16[272,256]{1,0:T(8,128)(2,1)} %get-tuple-element.10), channel_id=1, source_target_pairs={{0,8},{2,10},{4,12},{6,14},{8,0},{10,2},{12,4},{14,6},{16,24},{18,... | collective-permute-start | bytes 417800 | tf_op jit(solution)/shard_map/ppermute | solution.py:21
  6.5 13.7 %collective-permute-start.1 = (bf16[272,256]{1,0:T(8,128)(2,1)}, bf16[272,256]{1,0:T(8,128)(2,1)S(1)}, u32[]{:S(2)}, u32[]{:S(2)}) collective-permute-start(bf16[272,256]{1,0:T(8,128)(2,1)} %get-tuple-element.10), channel_id=1, source_target_pairs={{0,16},{2,18},{4,20},{6,22},{8,24},{10,26},{12,28},{14,30},{16,0},... | collective-permute-start | bytes 417800 | tf_op jit(solution)/shard_map/ppermute | solution.py:21
  9.1 11.1 %collective-permute-start.2 = (bf16[272,256]{1,0:T(8,128)(2,1)}, bf16[272,256]{1,0:T(8,128)(2,1)S(1)}, u32[]{:S(2)}, u32[]{:S(2)}) collective-permute-start(bf16[272,256]{1,0:T(8,128)(2,1)} %get-tuple-element.10), channel_id=1, source_target_pairs={{0,24},{2,26},{4,28},{6,30},{8,16},{10,18},{12,20},{14,22},{16,8},... | collective-permute-start | bytes 417800 | tf_op jit(solution)/shard_map/ppermute | solution.py:21
  20.2 36.6 %copy-start.6 = (bf16[4,272,256]{2,1,0:T(8,128)(2,1)}, bf16[4,272,256]{2,1,0:T(8,128)(2,1)S(1)}, u32[]{:S(2)}) copy-start(bf16[4,272,256]{2,1,0:T(8,128)(2,1)S(1)} %pad_maximum_fusion.refs_4_) | copy-start | bytes 1671172
  20.2 16.4 %collective-permute-start.3 = (bf16[4,272,256]{2,1,0:T(8,128)(2,1)S(1)}, bf16[4,272,256]{2,1,0:T(8,128)(2,1)}, u32[]{:S(2)}, u32[]{:S(2)}) collective-permute-start(bf16[4,272,256]{2,1,0:T(8,128)(2,1)S(1)} %pad_maximum_fusion.refs_4_), channel_id=1, source_target_pairs={{0,2},{2,0},{4,6},{6,4},{8,10},{10,8},{12,14},{14,12},{16,18},{18,... | collective-permute-start | bytes 1671176 | tf_op jit(solution)/shard_map/ppermute | solution.py:21
  21.8 17.4 %collective-permute-start.4 = (bf16[4,272,256]{2,1,0:T(8,128)(2,1)S(1)}, bf16[4,272,256]{2,1,0:T(8,128)(2,1)}, u32[]{:S(2)}, u32[]{:S(2)}) collective-permute-start(bf16[4,272,256]{2,1,0:T(8,128)(2,1)S(1)} %pad_maximum_fusion.refs_4_), channel_id=1, source_target_pairs={{0,4},{2,6},{4,0},{6,2},{8,12},{10,14},{12,8},{14,10},{16,20},{18,... | collective-permute-start | bytes 1671176 | tf_op jit(solution)/shard_map/ppermute | solution.py:21
  23.3 11.8 %collective-permute-start.8 = (bf16[256,256]{1,0:T(8,128)(2,1)S(1)}, bf16[256,256]{1,0:T(8,128)(2,1)S(1)}, u32[]{:S(2)}, u32[]{:S(2)}) collective-permute-start(bf16[256,256]{1,0:T(8,128)(2,1)S(1)} %copy-done.8), channel_id=1, source_target_pairs={{0,16},{2,18},{4,20},{6,22},{8,24},{10,26},{12,28},{14,30},{16,0},... | collective-permute-start | bytes 393224 | tf_op jit(solution)/shard_map/ppermute | solution.py:21
  26.4 8.7 %collective-permute-start.9 = (bf16[256,256]{1,0:T(8,128)(2,1)S(1)}, bf16[256,256]{1,0:T(8,128)(2,1)S(1)}, u32[]{:S(2)}, u32[]{:S(2)}) collective-permute-start(bf16[256,256]{1,0:T(8,128)(2,1)S(1)} %copy-done.8), channel_id=1, source_target_pairs={{0,24},{2,26},{4,28},{6,30},{8,16},{10,18},{12,20},{14,22},{16,8},... | collective-permute-start | bytes 393224 | tf_op jit(solution)/shard_map/ppermute | solution.py:21
  27.8 7.6 %collective-permute-start.7 = (bf16[256,256]{1,0:T(8,128)(2,1)S(1)}, bf16[256,256]{1,0:T(8,128)(2,1)S(1)}, u32[]{:S(2)}, u32[]{:S(2)}) collective-permute-start(bf16[256,256]{1,0:T(8,128)(2,1)S(1)} %copy-done.8), channel_id=1, source_target_pairs={{0,8},{2,10},{4,12},{6,14},{8,0},{10,2},{12,4},{14,6},{16,24},{18,... | collective-permute-start | bytes 393224 | tf_op jit(solution)/shard_map/ppermute | solution.py:21
  35.5 30.2 %copy-start.2 = (bf16[4,256,256]{2,1,0:T(8,128)(2,1)}, bf16[4,256,256]{2,1,0:T(8,128)(2,1)S(1)}, u32[]{:S(2)}) copy-start(bf16[4,256,256]{2,1,0:T(8,128)(2,1)S(1)} %pad_maximum_fusion.1.refs_4_) | copy-start | bytes 1572868
  35.5 14.9 %collective-permute-start.10 = (bf16[4,256,256]{2,1,0:T(8,128)(2,1)S(1)}, bf16[4,256,256]{2,1,0:T(8,128)(2,1)S(1)}, u32[]{:S(2)}, u32[]{:S(2)}) collective-permute-start(bf16[4,256,256]{2,1,0:T(8,128)(2,1)S(1)} %pad_maximum_fusion.1.refs_4_), channel_id=1, source_target_pairs={{0,2},{2,0},{4,6},{6,4},{8,10},{10,8},{12,14},{14,12},{16,18},{18,... | collective-permute-start | bytes 1572872 | tf_op jit(solution)/shard_map/ppermute | solution.py:21
  36.1 15.6 %collective-permute-start.11 = (bf16[4,256,256]{2,1,0:T(8,128)(2,1)S(1)}, bf16[4,256,256]{2,1,0:T(8,128)(2,1)S(1)}, u32[]{:S(2)}, u32[]{:S(2)}) collective-permute-start(bf16[4,256,256]{2,1,0:T(8,128)(2,1)S(1)} %pad_maximum_fusion.1.refs_4_), channel_id=1, source_target_pairs={{0,4},{2,6},{4,0},{6,2},{8,12},{10,14},{12,8},{14,10},{16,20},{18,... | collective-permute-start | bytes 1572872 | tf_op jit(solution)/shard_map/ppermute | solution.py:21
  37.6 17.6 %collective-permute-start.5 = (bf16[2,272,256]{2,1,0:T(8,128)(2,1)S(1)}, bf16[2,272,256]{2,1,0:T(8,128)(2,1)S(1)}, u32[]{:S(2)}, u32[]{:S(2)}) collective-permute-start(bf16[2,272,256]{2,1,0:T(8,128)(2,1)S(1)} %slice.88), channel_id=1, source_target_pairs={{0,4},{2,6},{4,0},{6,2},{8,12},{10,14},{12,8},{14,10},{16,20},{18,... | collective-permute-start | bytes 835592 | tf_op jit(solution)/shard_map/ppermute | solution.py:21
  40.2 15.0 %collective-permute-start.6 = (bf16[2,272,256]{2,1,0:T(8,128)(2,1)S(1)}, bf16[2,272,256]{2,1,0:T(8,128)(2,1)S(1)}, u32[]{:S(2)}, u32[]{:S(2)}) collective-permute-start(bf16[2,272,256]{2,1,0:T(8,128)(2,1)S(1)} %slice.90), channel_id=1, source_target_pairs={{0,2},{2,0},{4,6},{6,4},{8,10},{10,8},{12,14},{14,12},{16,18},{18,... | collective-permute-start | bytes 835592 | tf_op jit(solution)/shard_map/ppermute | solution.py:21
  50.4 15.2 %copy-start.3 = (bf16[4,256,256]{2,1,0:T(8,128)(2,1)}, bf16[4,256,256]{2,1,0:T(8,128)(2,1)S(1)}, u32[]{:S(2)}) copy-start(bf16[4,256,256]{2,1,0:T(8,128)(2,1)S(1)} %collective-permute-done.10.refs_5_) | copy-start | bytes 1572868
  51.2 14.5 %collective-permute-start.12 = (bf16[2,256,256]{2,1,0:T(8,128)(2,1)}, bf16[2,256,256]{2,1,0:T(8,128)(2,1)}, u32[]{:S(2)}, u32[]{:S(2)}) collective-permute-start(bf16[2,256,256]{2,1,0:T(8,128)(2,1)} %slice.92), channel_id=1, source_target_pairs={{0,4},{2,6},{4,0},{6,2},{8,12},{10,14},{12,8},{14,10},{16,20},{18,... | collective-permute-start | bytes 786440 | tf_op jit(solution)/shard_map/ppermute | solution.py:21
  51.7 14.0 %copy-start.4 = (bf16[4,256,256]{2,1,0:T(8,128)(2,1)}, bf16[4,256,256]{2,1,0:T(8,128)(2,1)S(1)}, u32[]{:S(2)}) copy-start(bf16[4,256,256]{2,1,0:T(8,128)(2,1)S(1)} %collective-permute-done.11.refs_6_) | copy-start | bytes 1572868
  52.4 13.2 %collective-permute-start.13 = (bf16[2,256,256]{2,1,0:T(8,128)(2,1)}, bf16[2,256,256]{2,1,0:T(8,128)(2,1)}, u32[]{:S(2)}, u32[]{:S(2)}) collective-permute-start(bf16[2,256,256]{2,1,0:T(8,128)(2,1)} %slice.93), channel_id=1, source_target_pairs={{0,2},{2,0},{4,6},{6,4},{8,10},{10,8},{12,14},{14,12},{16,18},{18,... | collective-permute-start | bytes 786440 | tf_op jit(solution)/shard_map/ppermute | solution.py:21
  55.2 0.7 copy-start.9
  55.9 0.7 copy-start.10
  65.7 8.0 %copy-start.5 = (bf16[1,256,512]{2,1,0:T(8,128)(2,1)S(1)}, bf16[1,256,512]{2,1,0:T(8,128)(2,1)}, u32[]{:S(2)}) copy-start(bf16[1,256,512]{2,1,0:T(8,128)(2,1)} %param.8) | copy-start | bytes 786436
  75.7 2.0 %collective-permute-start.14 = (bf16[4,4,16,1024]{3,2,1,0:T(8,128)(2,1)S(1)}, bf16[4,4,16,1024]{3,2,1,0:T(8,128)(2,1)S(1)}, u32[]{:S(2)}, u32[]{:S(2)}) collective-permute-start(bf16[4,4,16,1024]{3,2,1,0:T(8,128)(2,1)S(1)} %bitcast.63), channel_id=1, source_target_pairs={{0,1},{1,0},{2,3},{3,2},{4,5},{5,4},{6,7},{7,6},{8,9},{9,8},{10,11... | collective-permute-start | bytes 1572872 | tf_op jit(solution)/shard_map/ppermute | solution.py:21
  77.6 16.2 %copy-start.1 = (bf16[1,256,1024]{2,1,0:T(8,128)(2,1)S(1)}, bf16[1,256,1024]{2,1,0:T(8,128)(2,1)}, u32[]{:S(2)}) copy-start(bf16[1,256,1024]{2,1,0:T(8,128)(2,1)} %get-tuple-element.16) | copy-start | bytes 1572868
  77.9 5.9 %collective-permute-start.15 = (bf16[4,16,1024]{2,1,0:T(8,128)(2,1)S(1)}, bf16[4,16,1024]{2,1,0:T(8,128)(2,1)S(1)}, u32[]{:S(2)}, u32[]{:S(2)}) collective-permute-start(bf16[4,16,1024]{2,1,0:T(8,128)(2,1)S(1)} %get-tuple-element.21), channel_id=1, source_target_pairs={{0,2},{2,0},{4,6},{6,4},{8,10},{10,8},{12,14},{14,12},{16,18},{18,... | collective-permute-start | bytes 393224 | tf_op jit(solution)/shard_map/ppermute | solution.py:21
  79.5 8.1 %collective-permute-start.16 = (bf16[4,16,1024]{2,1,0:T(8,128)(2,1)S(1)}, bf16[4,16,1024]{2,1,0:T(8,128)(2,1)S(1)}, u32[]{:S(2)}, u32[]{:S(2)}) collective-permute-start(bf16[4,16,1024]{2,1,0:T(8,128)(2,1)S(1)} %get-tuple-element.23), channel_id=1, source_target_pairs={{0,4},{2,6},{4,0},{6,2},{8,12},{10,14},{12,8},{14,10},{16,20},{18,... | collective-permute-start | bytes 393224 | tf_op jit(solution)/shard_map/ppermute | solution.py:21
  80.0 7.6 %collective-permute-start.17 = (bf16[4,16,1024]{2,1,0:T(8,128)(2,1)S(1)}, bf16[4,16,1024]{2,1,0:T(8,128)(2,1)S(1)}, u32[]{:S(2)}, u32[]{:S(2)}) collective-permute-start(bf16[4,16,1024]{2,1,0:T(8,128)(2,1)S(1)} %get-tuple-element.22), channel_id=1, source_target_pairs={{0,6},{2,4},{4,2},{6,0},{8,14},{10,12},{12,10},{14,8},{16,22},{18,... | collective-permute-start | bytes 393224 | tf_op jit(solution)/shard_map/ppermute | solution.py:21
  87.6 7.4 %collective-permute-start.18 = (bf16[16,1024]{1,0:T(8,128)(2,1)S(1)}, bf16[16,1024]{1,0:T(8,128)(2,1)S(1)}, u32[]{:S(2)}, u32[]{:S(2)}) collective-permute-start(bf16[16,1024]{1,0:T(8,128)(2,1)S(1)} %get-tuple-element.24), channel_id=1, source_target_pairs={{0,8},{2,10},{4,12},{6,14},{8,0},{10,2},{12,4},{14,6},{16,24},{18,... | collective-permute-start | bytes 98312 | tf_op jit(solution)/shard_map/ppermute | solution.py:21
  91.4 4.8 %collective-permute-start.19 = (bf16[16,1024]{1,0:T(8,128)(2,1)S(1)}, bf16[16,1024]{1,0:T(8,128)(2,1)S(1)}, u32[]{:S(2)}, u32[]{:S(2)}) collective-permute-start(bf16[16,1024]{1,0:T(8,128)(2,1)S(1)} %get-tuple-element.26), channel_id=1, source_target_pairs={{0,16},{2,18},{4,20},{6,22},{8,24},{10,26},{12,28},{14,30},{16,0},... | collective-permute-start | bytes 98312 | tf_op jit(solution)/shard_map/ppermute | solution.py:21
  91.5 5.7 %collective-permute-start.20 = (bf16[16,1024]{1,0:T(8,128)(2,1)S(1)}, bf16[16,1024]{1,0:T(8,128)(2,1)S(1)}, u32[]{:S(2)}, u32[]{:S(2)}) collective-permute-start(bf16[16,1024]{1,0:T(8,128)(2,1)S(1)} %get-tuple-element.25), channel_id=1, source_target_pairs={{0,24},{2,26},{4,28},{6,30},{8,16},{10,18},{12,20},{14,22},{16,8},... | collective-permute-start | bytes 98312 | tf_op jit(solution)/shard_map/ppermute | solution.py:21

commit v2 on v1

v2 whole, which is shorter than its diff:
```python
import functools

import jax
import jax.numpy as jnp
from jax import lax
from jax.experimental import pallas as pl
from jax.experimental.pallas import tpu as pltpu
from jax.sharding import PartitionSpec as P

BLK = 64
LANES = 128
TILE = 16
QUAD = 4
PAIR = 2
DEAD = -1e30
VMEM_LIMIT = 60 * 1024 * 1024
CUT = 2
STEP = 256
F32 = jnp.float32
BF16 = jnp.bfloat16


def swap(array, axis, mask):
    size = lax.axis_size(axis)
    return lax.ppermute(array, axis, [(i, i ^ mask) for i in range(size)])


def after(array, other):
    return lax.optimization_barrier((array, other))[0]


def select_kernel(cut, blocks_ref, lengths_ref, keys_ref, values_ref, *outs):
    heads, topk = blocks_ref.shape[1:]
    rows, width = keys_ref.shape[1:]
    half = heads // PAIR
    head_dim = width // heads
    blk_dev = rows // BLK
    rank = lax.axis_index("hist")
    side = (rank // QUAD) % PAIR
    length = lengths_ref[0]
    count = half * blk_dev
    room = -(-count // TILE) * TILE
    for out, first in zip(outs, (side * half, (1 - side) * half)):
        for index in range(half):
            head = first + index
            local = jnp.int32(0)
            for entry in range(topk):
                block = blocks_ref[0, head, entry] - rank * blk_dev
                local = jnp.where((block >= 0) & (block < blk_dev), block, local)
            low = pl.multiple_of(local * BLK, BLK)
            at = index * BLK + (room if index >= cut else 0)
            columns = pl.ds(pl.multiple_of(head * head_dim, head_dim), head_dim)
            out[at : at + BLK, :head_dim] = keys_ref[0, pl.ds(low, BLK), columns]
            out[at : at + BLK, head_dim:] = values_ref[0, pl.ds(low, BLK), columns]
        span = pl.ds(pl.multiple_of(first * head_dim, head_dim), half * head_dim)
        for source, low in ((keys_ref, 0), (values_ref, head_dim)):
            totals = []
            for block in range(blk_dev):
                part = source[0, block * BLK : (block + 1) * BLK, span].astype(F32)
                spot = lax.broadcasted_iota(jnp.int32, part.shape, 0) + (rank * rows + block * BLK)
                part = jnp.where(spot < length, part, 0.0)
                totals.append(jnp.sum(part, axis=0, keepdims=True) * BLK ** (-0.5))
            lines = [
                totals[block][:, index * head_dim : (index + 1) * head_dim]
                for index in range(half)
                for block in range(blk_dev)
            ]
            lines.append(jnp.zeros((room - count, head_dim), F32))
            summary = jnp.concatenate(lines, axis=0).astype(BF16)
            out[cut * BLK : cut * BLK + room, low : low + head_dim] = summary


def attend_kernel(pieces, fine_width, scale, *refs):
    query_ref, grad_ref, bias_ref, ordered_ref = refs[:4]
    piece_refs = refs[4 : 4 + 2 * pieces]
    out_ref, dq_ref, away_ref, keep_ref, send_ref = refs[-5:]
    head_dim = query_ref.shape[1]
    keys = jnp.concatenate(
        [r[:, :, :head_dim].reshape(-1, head_dim) for r in piece_refs], axis=0
    )
    values = jnp.concatenate(
        [r[:, :, head_dim:].reshape(-1, head_dim) for r in piece_refs], axis=0
    )
    bias = bias_ref[0]
    cols = (slice(0, fine_width), slice(fine_width, keys.shape[0]))
    rows = out_ref.shape[0]
    step = min(STEP, rows)
    contract = (((1,), (1,)), ((), ()))
    d_queries = []
    places = ((out_ref, dq_ref, 0), (away_ref.at[0], away_ref.at[1], rows))
    for out_part, dq_part, base in places:
        for low in range(0, rows, step):
            query = query_ref[base + low : base + low + step, :]
            grad = grad_ref[base + low : base + low + step, :]
            scores = lax.dot_general(query, keys, contract, preferred_element_type=F32) * scale + bias
            d_probs = lax.dot_general(grad, values, contract, preferred_element_type=F32)
            probs_parts = []
            d_parts = []
            for part in cols:
                score = scores[:, part]
                expo = jnp.exp(score - jnp.max(score, axis=1, keepdims=True))
                probs = expo * (1.0 / jnp.sum(expo, axis=1, keepdims=True))
                d_prob = d_probs[:, part]
                delta = jnp.sum(probs * d_prob, axis=1, keepdims=True)
                probs_parts.append(probs.astype(BF16))
                d_parts.append((probs * (d_prob - delta)).astype(BF16))
            out = jnp.dot(jnp.concatenate(probs_parts, axis=1), values, preferred_element_type=F32)
            d_query = jnp.dot(jnp.concatenate(d_parts, axis=1), keys, preferred_element_type=F32)
            d_query = (d_query * scale).astype(BF16)
            out_part[low : low + step, :] = out.astype(BF16)
            dq_part[low : low + step, :] = d_query
            d_queries.append(d_query)
    weight = jnp.dot(
        ordered_ref[...], jnp.concatenate(d_queries, axis=0), preferred_element_type=F32
    )
    kept = keep_ref.shape[0]
    keep_ref[...] = weight[:kept]
    send_ref[...] = weight[kept:].astype(BF16)


def attend(first, count, query, grad, bias, ordered, summaries, pieces, share, earlier):
    rows, width = query.shape
    half = bias.shape[0]
    head_dim = width // half
    fine_width = sum(p.shape[0] for p in pieces) * BLK
    room = (bias.shape[-1] - fine_width) // sum(p.shape[0] for p in pieces)
    depth = ordered.shape[0]
    kept = depth // share
    in_specs = [
        pl.BlockSpec((rows, head_dim), lambda i: (0, first + i)),
        pl.BlockSpec((rows, head_dim), lambda i: (0, first + i)),
        pl.BlockSpec((1,) + bias.shape[1:], lambda i: (first + i, 0, 0)),
        pl.BlockSpec(ordered.shape, lambda i: (0, 0)),
    ]
    in_specs += [
        pl.BlockSpec((p.shape[0], BLK, 2 * head_dim), lambda i: (0, i, 0)) for p in pieces
    ]
    in_specs += [
        pl.BlockSpec((p.shape[0], room, 2 * head_dim), lambda i: (0, CUT * BLK // room, 0))
        for p in summaries
    ]
    args = [query, grad, bias, ordered, *pieces, *summaries]
    aliases = {}
    if earlier is not None:
        aliases = {len(args) + i: 3 + i for i in range(len(earlier))}
        args += list(earlier)
        in_specs += [pl.BlockSpec(memory_space=pl.ANY)] * len(earlier)
    own = jax.ShapeDtypeStruct((rows // PAIR, count * head_dim), BF16)
    own_spec = pl.BlockSpec((rows // PAIR, head_dim), lambda i: (0, i))
    columns = bias.shape[-1]
    return pl.pallas_call(
        functools.partial(attend_kernel, len(pieces), fine_width, head_dim ** (-0.5)),
        grid=(count,),
        in_specs=in_specs,
        out_specs=(
            own_spec,
            own_spec,
            pl.BlockSpec((2, rows // PAIR, head_dim), lambda i: (0, 0, i)),
            pl.BlockSpec((kept, head_dim), lambda i: (0, first + i)),
            pl.BlockSpec((depth - kept, head_dim), lambda i: (0, first + i)),
        ),
        out_shape=(
            own,
            own,
            jax.ShapeDtypeStruct((2,) + own.shape, BF16),
            jax.ShapeDtypeStruct((kept, width), F32),
            jax.ShapeDtypeStruct((depth - kept, width), BF16),
        ),
        input_output_aliases=aliases,
        compiler_params=pltpu.CompilerParams(vmem_limit_bytes=VMEM_LIMIT),
        cost_estimate=pl.CostEstimate(
            flops=8 * count * rows * columns * head_dim,
            bytes_accessed=count * (columns * 512 + rows * head_dim * 8),
            transcendentals=count * rows * columns,
        ),
        name="attend",
    )(*args)


def gather_quad(column):
    return [column] + [swap(column, "hist", mask) for mask in range(1, QUAD)]


def gather_rest(pair):
    count = lax.axis_size("hist") // (QUAD * PAIR)
    return jnp.concatenate(
        [pair] + [swap(pair, "hist", QUAD * PAIR * k) for k in range(1, count)], axis=0
    )


def shards(targets, w_query, keys, values, blocks, lengths, d_attended):
    heads = blocks.shape[1]
    local_rows, width = keys.shape[1:]
    head_dim = width // heads
    blk_dev = local_rows // BLK
    n_hist = lax.axis_size("hist")
    n_batch = lax.axis_size("batch")
    rank = lax.axis_index("hist")
    lane = lax.axis_index("batch")
    rows = targets.shape[1]
    depth = targets.shape[2]
    half = heads // PAIR
    side = (rank // QUAD) % PAIR
    wide = half * head_dim
    count = half * blk_dev
    room = -(-count // TILE) * TILE
    first_rows = CUT * BLK + room

    shape = jax.ShapeDtypeStruct((half * BLK + room, 2 * head_dim), BF16)
    keep, send = pl.pallas_call(
        functools.partial(select_kernel, CUT),
        in_specs=[
            pl.BlockSpec(memory_space=pltpu.SMEM),
            pl.BlockSpec(memory_space=pltpu.SMEM),
            pl.BlockSpec(memory_space=pltpu.VMEM),
            pl.BlockSpec(memory_space=pltpu.VMEM),
        ],
        out_specs=[pl.BlockSpec(memory_space=pltpu.VMEM)] * 2,
        out_shape=[shape] * 2,
        name="select",
    )(blocks, lengths, keys, values)
    came = swap(send, "hist", QUAD)
    pair_near = jnp.stack([keep[:first_rows], came[:first_rows]])
    pair_late = jnp.stack([keep[first_rows:], came[first_rows:]])
    column_near = gather_rest(pair_near)
    column_late = gather_rest(after(pair_late, column_near))
    near = gather_quad(column_near)

    grad = d_attended[0]
    grad_keep = lax.dynamic_slice_in_dim(grad, side * wide, wide, 1)
    grad_send = lax.dynamic_slice_in_dim(grad, (1 - side) * wide, wide, 1)
    mine = jnp.concatenate([targets[0], grad_send], axis=0)
    theirs = swap(after(mine, came), "hist", QUAD)
    both_targets = jnp.concatenate([targets[0], theirs[:rows]], axis=0)
    both_grads = jnp.concatenate([grad_keep, theirs[rows:]], axis=0)
    weights = lax.dynamic_slice_in_dim(w_query, side * wide, wide, 1)
    query = jnp.dot(both_targets, weights, preferred_element_type=F32).astype(BF16)

    masks = jnp.asarray([q + QUAD * k for q in range(QUAD) for k in range(n_hist // QUAD)], jnp.int32)
    source = rank ^ masks
    lists = lax.dynamic_slice_in_dim(after(blocks, column_near)[0], side * half, half, 0)
    listed = jnp.max(
        jnp.where((lists // blk_dev)[:, :, None] == source[None, None, :], lists[:, :, None], -1),
        axis=1,
    )
    spots = jnp.arange(BLK, dtype=jnp.int32)
    live = (listed[:, :, None] >= 0) & (listed[:, :, None] * BLK + spots < lengths[0])
    fine_bias = jnp.where(live, 0.0, DEAD).astype(F32).reshape(half, -1)
    line = jnp.arange(room, dtype=jnp.int32)
    names = source[:, None] * blk_dev + line[None, :] % blk_dev
    own_line = (line // blk_dev)[None, :] == jnp.arange(half, dtype=jnp.int32)[:, None]
    coarse_live = own_line[:, None, :] & (names * BLK < lengths[0])[None]
    coarse_bias = jnp.where(coarse_live, 0.0, DEAD).astype(F32).reshape(half, -1)
    bias = jnp.concatenate([fine_bias, coarse_bias], axis=1)[:, None, :]

    places = (
        (rank ^ masks)[None, :] * n_batch + (lane ^ jnp.arange(n_batch, dtype=jnp.int32))[:, None]
    ).reshape(-1)
    share = depth // (n_hist * n_batch)
    chosen = (places[:, None] * share + jnp.arange(share, dtype=jnp.int32)).reshape(-1)
    shuffle = (chosen[:, None] == jnp.arange(depth, dtype=jnp.int32)[None, :]).astype(BF16)
    ordered = lax.dot_general(
        shuffle, both_targets, (((1,), (1,)), ((), ())), preferred_element_type=F32
    ).astype(BF16)

    late = gather_quad(after(column_late, (near[1:], query, ordered, both_grads, bias)))
    fixed = (query, both_grads, bias, ordered, near)
    out_near, dq_near, away_near, *weight = attend(0, CUT, *fixed, near, n_batch, None)
    out_late, dq_late, away_late, kept, sent = attend(
        CUT, half - CUT, *fixed, late, n_batch, weight
    )

    back_near = swap(away_near, "hist", QUAD)
    back_late = swap(away_late, "hist", QUAD)
    sent = after(sent, back_near)
    kept = kept.reshape(QUAD, n_hist // QUAD, share, wide)
    sent = sent.reshape(n_batch - 1, QUAD, n_hist // QUAD, share, wide)
    total = kept
    for index in range(1, n_batch):
        total = total + swap(sent[index - 1], "batch", index).astype(F32)
    parts = [swap(total[index].astype(BF16), "hist", index) for index in range(1, QUAD)]
    back_late = after(back_late, parts[0])
    level = total[0]
    for part in parts:
        level = level + part.astype(F32)

    def join(index):
        own = [(out_near, dq_near)[index], (out_late, dq_late)[index]]
        back = [back_near[index], back_late[index]]
        return jnp.where(
            side == 0, jnp.concatenate(own + back, axis=1), jnp.concatenate(back + own, axis=1)
        )

    attended = join(0)
    d_targets = lax.dot_general(
        join(1), w_query, (((1,), (1,)), ((), ())), preferred_element_type=F32
    ).astype(BF16)
    level = after(level, (attended, d_targets))

    mask = n_hist // QUAD
    while mask > PAIR:
        mask //= 2
        level = level[:mask] + swap(level[mask:].astype(BF16), "hist", QUAD * mask).astype(F32)
    other = swap(level[1].astype(BF16), "hist", QUAD).astype(F32)
    d_query_weight = jnp.where(
        side == 0,
        jnp.concatenate([level[0], other], axis=1),
        jnp.concatenate([other, level[0]], axis=1),
    )
    return (attended[None], d_targets[None], d_query_weight)


def solution(mesh):
    in_specs = (
        P("batch", "hist", None),
        P(),
        P("batch", "hist", None),
        P("batch", "hist", None),
        P("batch", None, None),
        P("batch"),
        P("batch", "hist", None),
    )
    out_specs = (P("batch", "hist", None), P("batch", "hist", None), P(("hist", "batch"), None))
    return jax.shard_map(shards, mesh=mesh, in_specs=in_specs, out_specs=out_specs, check_vma=False)
```

time: 98.4 us -> 78.1 us (0.79)
  waiting for transfers between devices: 31.9 us -> 19.8 us
  local copies, waits for them, and re-layouts: 9.03 us -> 4.77 us
  Pallas kernels: 18 us -> 16.4 us
  matrix products: 5.26 us -> 3.74 us
  starting transfers between devices: 28.6 us -> 27.2 us
    ppermute x21 -> x18, waiting for transfers between devices: 31.9 us -> 19.8 us  [swap(): return lax.ppermute(array, axis, [(i, i ^ mask) for i in range(size)])]
    slice x6 -> x2, local copies, waits for them, and re-layouts: 3.62 us -> 0.04 us  [the longest x1 0.04 us: shards(): both_grads = jnp.concatenate([grad_keep, theirs[rows:]], axis=0)]
    dot_general x3, matrix products: 5.26 us -> 3.74 us  [the longest x1 1.3 us: shards(): lax.dot_general(shuffle, both_targets, (((1,), (1,)), ((), ())), preferre...]
    pallas_call x2, Pallas kernels: 15.9 us -> 14.4 us  [attend(): pl.pallas_call(functools.partial(attend_kernel, len(pieces), fine_width,...]
    ppermute x21 -> x18, starting transfers between devices: 28.6 us -> 27.2 us  [swap(): return lax.ppermute(array, axis, [(i, i ^ mask) for i in range(size)])]
    unnamed x26 -> x30, local copies, waits for them, and re-layouts: 3.01 us -> 2.21 us
  transfers between devices with their start and end apart: 21 -> 18, of which waited for: 10 -> 8; matrix products, arithmetic and copies ran while one was open for 14% -> 12% of each run, Pallas kernels for 8% -> 19%
where the time goes in v2:
time: 78.1 us; the launch traced here: 77.7 us
  starting transfers between devices  27.2 us (35%)
  waiting for transfers between devices  19.8 us (25%)
  Pallas kernels  16.4 us (21%)
  local copies, waits for them, and re-layouts  4.77 us (6%)
  other arithmetic  4.02 us (5%)
  matrix products  3.74 us (5%)
  between operations  1.71 us (2%)
    ppermute x18, starting transfers between devices, swap(): return lax.ppermute(array, axis, [(i, i ^ mask) for i in range(size)])  27.2 us
    ppermute x18, waiting for transfers between devices, swap(): return lax.ppermute(array, axis, [(i, i ^ mask) for i in range(size)])  19.8 us
    pallas_call x2, Pallas kernels, attend(): pl.pallas_call(functools.partial(attend_kernel, len(pieces), fine_width,...  14.4 us
    unnamed x30, local copies, waits for them, and re-layouts  2.21 us
    pallas_call x1, Pallas kernels, shards(): pl.pallas_call(functools.partial(select_kernel, CUT), in_specs=[pl.BlockS...  2.04 us
  transfers between devices with their start and end apart: 18, of which 8 were waited for; matrix products, arithmetic and copies ran while one was open for 12% of the time, Pallas kernels for 19%

profile of v2, /device:TPU:0, one launch (start us, length us, event | category | flops | bytes accessed | tf_op | source)
XLA Modules:
  0.0 77.7 jit_solution(12141770092502224061)
XLA Ops:
  1.4 2.0 %select.34 = (bf16[272,256]{1,0:T(8,128)(2,1)}, bf16[272,256]{1,0:T(8,128)(2,1)}) custom-call(s32[1,8,16]{2,1,0:T(8,128)} %blocks_ref.1, s32[1]{0:T(128)} %copy.15.lengths_ref, bf16[1,128,1024]{2,1,0:T(8,128)(2,1)} %keys_ref.1, bf16[1,128,1024]{2,1,0:T(8,128)(2,1)} %values_ref.1), custom_call_target="tpu_custom_call" | custom-call | tf_op jit(solution)/shard_map/select/pallas_call | solution.py:210
  3.5 3.0 %collective-permute-start = (bf16[272,256]{1,0:T(8,128)(2,1)}, bf16[272,256]{1,0:T(8,128)(2,1)S(1)}, u32[]{:S(2)}, u32[]{:S(2)}) collective-permute-start(bf16[272,256]{1,0:T(8,128)(2,1)} %get-tuple-element.22), channel_id=1, source_target_pairs={{0,8},{2,10},{4,12},{6,14},{8,0},{10,2},{12,4},{14,6},{16,24},{18,... | collective-permute-start | bytes 417800 | tf_op jit(solution)/shard_map/ppermute | solution.py:25
  6.5 0.8 %slice_bitcast_fusion.9 = bf16[1,128,256]{2,1,0:T(8,128)(2,1)S(1)} fusion(bf16[272,256]{1,0:T(8,128)(2,1)} %get-tuple-element.24), kind=kLoop, calls=%fused_computation.47 | loop fusion | bytes 131072 | tf_op jit(solution)/shard_map/stack | solution.py:224
  7.4 0.6 copy-done.9
  8.0 0.1 broadcast_reduce_fusion
  8.2 0.1 mul.61
  8.3 0.1 and.86
  8.9 0.7 copy-done.4
  9.6 0.7 collective-permute-done
  10.4 2.8 %collective-permute-start.2 = (bf16[2,144,256]{2,1,0:T(8,128)(2,1)S(1)}, bf16[2,144,256]{2,1,0:T(8,128)(2,1)S(1)}, u32[]{:S(2)}, u32[]{:S(2)}) collective-permute-start(bf16[2,144,256]{2,1,0:T(8,128)(2,1)S(1)} %pad_maximum_fusion.7), channel_id=1, source_target_pairs={{0,16},{2,18},{4,20},{6,22},{8,24},{10,26},{12,28},{14,30},{16,0},... | collective-permute-start | bytes 442376 | tf_op jit(solution)/shard_map/ppermute | solution.py:25
  13.2 1.6 %collective-permute-start.1 = (bf16[512,512]{1,0:T(8,128)(2,1)S(1)}, bf16[512,512]{1,0:T(8,128)(2,1)S(1)}, u32[]{:S(2)}, u32[]{:S(2)}) collective-permute-start(bf16[512,512]{1,0:T(8,128)(2,1)S(1)} %pad_maximum_fusion), channel_id=1, source_target_pairs={{0,8},{2,10},{4,12},{6,14},{8,0},{10,2},{12,4},{14,6},{16,24},{18,... | collective-permute-start | bytes 1572872 | tf_op jit(solution)/shard_map/ppermute | solution.py:25
  14.8 4.8 %collective-permute-done.2 = bf16[2,144,256]{2,1,0:T(8,128)(2,1)S(1)} collective-permute-done((bf16[2,144,256]{2,1,0:T(8,128)(2,1)S(1)}, bf16[2,144,256]{2,1,0:T(8,128)(2,1)S(1)}, u32[]{:S(2)}, u32[]{:S(2)}) %collective-permute-start.2) | collective-permute-done | bytes 147488 | tf_op jit(solution)/shard_map/ppermute | solution.py:25
  19.6 0.1 select_reduce_fusion
  19.8 2.3 %collective-permute-start.5 = (bf16[4,144,256]{2,1,0:T(8,128)(2,1)S(1)}, bf16[4,144,256]{2,1,0:T(8,128)(2,1)}, u32[]{:S(2)}, u32[]{:S(2)}) collective-permute-start(bf16[4,144,256]{2,1,0:T(8,128)(2,1)S(1)} %pad_maximum_fusion.5.refs_4_.refs_8_), channel_id=1, source_target_pairs={{0,6},{2,4},{4,2},{6,0},{8,14},{10,12},{12,10},{14,8},{16,22},{18,... | collective-permute-start | bytes 884744 | tf_op jit(solution)/shard_map/ppermute | solution.py:25
  22.1 0.5 collective-permute-start.4
  22.6 0.7 collective-permute-start.3
  23.4 0.1 and.82
  23.6 0.1 add.136
  23.7 1.4 %collective-permute-start.6 = (bf16[2,128,256]{2,1,0:T(8,128)(2,1)S(1)}, bf16[2,128,256]{2,1,0:T(8,128)(2,1)S(1)}, u32[]{:S(2)}, u32[]{:S(2)}) collective-permute-start(bf16[2,128,256]{2,1,0:T(8,128)(2,1)S(1)} %pad_maximum_fusion.8), channel_id=1, source_target_pairs={{0,16},{2,18},{4,20},{6,22},{8,24},{10,26},{12,28},{14,30},{16,0},... | collective-permute-start | bytes 393224 | tf_op jit(solution)/shard_map/ppermute | solution.py:25
  25.0 0.6 broadcast_in_dim.57.refs_2_
  25.7 5.9 %collective-permute-done.6 = bf16[2,128,256]{2,1,0:T(8,128)(2,1)S(1)} collective-permute-done((bf16[2,128,256]{2,1,0:T(8,128)(2,1)S(1)}, bf16[2,128,256]{2,1,0:T(8,128)(2,1)S(1)}, u32[]{:S(2)}, u32[]{:S(2)}) %collective-permute-start.6) | collective-permute-done | bytes 131104 | tf_op jit(solution)/shard_map/ppermute | solution.py:25
  31.7 0.8 %pad_maximum_fusion.2.refs_1_ = bf16[512,512]{1,0:T(8,128)(2,1)} fusion(bf16[256,512]{1,0:T(8,128)(2,1)S(1)} %get-tuple-element.47, bf16[256,512]{1,0:T(8,128)(2,1)S(1)} %get-tuple-element.45), kind=kLoop, calls=%fused_computation.6 | loop fusion | flops 1048576 | bytes 1048576 | tf_op jit(solution)/shard_map/concatenate | solution.py:235
  32.5 1.2 %convolution_convert_fusion.1.refs_0_ = bf16[512,512]{1,0:T(8,128)(2,1)} fusion(bf16[512,1024]{1,0:T(8,128)(2,1)S(1)} %copy-done, s32[]{:T(128)S(6)} %select_n.97, bf16[256,512]{1,0:T(8,128)(2,1)S(1)} %bitcast.49, bf16[256,512]{1,0:T(8,128)(2,1)S(1)} %get-tuple-element.48), kind=kOutput, calls=%fused_computation.1 | convolution fusion | flops 269746176 | bytes 1572868 | tf_op jit(solution)/shard_map/dot_general | solution.py:237
  33.8 1.3 %convolution_convert_fusion.refs_3_ = bf16[512,512]{1,0:T(8,128)(2,1)} fusion(s32[512]{0:T(512)S(1)} %add.153, bf16[256,512]{1,0:T(8,128)(2,1)S(1)} %bitcast.50, bf16[256,512]{1,0:T(8,128)(2,1)S(1)} %get-tuple-element.48), kind=kOutput, calls=%fused_computation | convolution fusion | flops 270008320 | bytes 1050624 | tf_op jit(solution)/shard_map/dot_general | solution.py:262
  35.1 2.4 %collective-permute-start.9 = (bf16[4,128,256]{2,1,0:T(8,128)(2,1)S(1)}, bf16[4,128,256]{2,1,0:T(8,128)(2,1)S(1)}, u32[]{:S(2)}, u32[]{:S(2)}) collective-permute-start(bf16[4,128,256]{2,1,0:T(8,128)(2,1)S(1)} %pad_maximum_fusion.6.refs_4_), channel_id=1, source_target_pairs={{0,6},{2,4},{4,2},{6,0},{8,14},{10,12},{12,10},{14,8},{16,22},{18,... | collective-permute-start | bytes 786440 | tf_op jit(solution)/shard_map/ppermute | solution.py:25
  37.5 0.5 collective-permute-start.8
  38.0 0.6 collective-permute-start.7
  38.7 7.2 %attend.2 = (bf16[256,256]{1,0:T(8,128)(2,1)}, bf16[256,256]{1,0:T(8,128)(2,1)}, bf16[2,256,256]{2,1,0:T(8,128)(2,1)}, f32[256,512]{1,0:T(8,128)}, bf16[256,512]{1,0:T(8,128)(2,1)}) custom-call(bf16[512,512]{1,0:T(8,128)(2,1)} %convolution_convert_fusion.1.refs_0_, bf16[512,512]{1,0:T(8,128)(2,1)} %pad_maximum_fusion.2.refs_1_, ...), custom_call_target="tpu_custom_call" | custom-call | flops 1342177280 | bytes 2359296 | tf_op jit(solution)/shard_map/attend/pallas_call | solution.py:151
  45.8 1.0 %collective-permute-start.10 = (bf16[2,256,256]{2,1,0:T(8,128)(2,1)}, bf16[2,256,256]{2,1,0:T(8,128)(2,1)S(1)}, u32[]{:S(2)}, u32[]{:S(2)}) collective-permute-start(bf16[2,256,256]{2,1,0:T(8,128)(2,1)} %get-tuple-element.32), channel_id=1, source_target_pairs={{0,8},{2,10},{4,12},{6,14},{8,0},{10,2},{12,4},{14,6},{16,24},{18,... | collective-permute-start | bytes 786440 | tf_op jit(solution)/shard_map/ppermute | solution.py:25
  46.8 2.1 %collective-permute-done.8.refs_6_ = bf16[4,128,256]{2,1,0:T(8,128)(2,1)S(1)} collective-permute-done((bf16[4,128,256]{2,1,0:T(8,128)(2,1)S(1)}, bf16[4,128,256]{2,1,0:T(8,128)(2,1)S(1)}, u32[]{:S(2)}, u32[]{:S(2)}) %collective-permute-start.8) | collective-permute-done | bytes 262176 | tf_op jit(solution)/shard_map/ppermute | solution.py:25
  48.9 0.7 copy-done.11
  49.6 0.1 copy-done.12
  49.7 7.2 %attend.3 = (bf16[256,256]{1,0:T(8,128)(2,1)}, bf16[256,256]{1,0:T(8,128)(2,1)}, bf16[2,256,256]{2,1,0:T(8,128)(2,1)}, f32[256,512]{1,0:T(8,128)}, bf16[256,512]{1,0:T(8,128)(2,1)}) custom-call(bf16[512,512]{1,0:T(8,128)(2,1)} %convolution_convert_fusion.1.refs_0_, ...), custom_call_target="tpu_custom_call", output_to_operand_aliasing={{3}: (12, {}), {4}: (13, {})} | custom-call | flops 1342177280 | bytes 2359296 | tf_op jit(solution)/shard_map/attend/pallas_call | solution.py:151
  56.9 0.1 collective-permute-start.12
  57.0 1.9 %collective-permute-start.11 = (bf16[2,256,256]{2,1,0:T(8,128)(2,1)}, bf16[2,256,256]{2,1,0:T(8,128)(2,1)S(1)}, u32[]{:S(2)}, u32[]{:S(2)}) collective-permute-start(bf16[2,256,256]{2,1,0:T(8,128)(2,1)} %get-tuple-element.33), channel_id=1, source_target_pairs={{0,8},{2,10},{4,12},{6,14},{8,0},{10,2},{12,4},{14,6},{16,24},{18,... | collective-permute-start | bytes 786440 | tf_op jit(solution)/shard_map/ppermute | solution.py:25
  58.9 1.1 %fusion.28 = (bf16[4,4,16,512]{3,2,1,0:T(8,128)(2,1)S(1)}, f32[4,4,16,512]{3,2,1,0:T(8,128)S(1)}) fusion(f32[4,4,16,512]{3,2,1,0:T(8,128)} %bitcast.47, bf16[4,4,16,512]{3,2,1,0:T(8,128)(2,1)S(1)} %collective-permute-done.12), kind=kLoop, calls=%fused_computation.84 | loop fusion | flops 393216 | bytes 1572864 | tf_op jit(solution)/shard_map/convert.4
  60.0 1.6 %collective-permute-start.13 = (bf16[4,16,512]{2,1,0:T(8,128)(2,1)S(1)}, bf16[4,16,512]{2,1,0:T(8,128)(2,1)S(1)}, u32[]{:S(2)}, u32[]{:S(2)}) collective-permute-start(bf16[4,16,512]{2,1,0:T(8,128)(2,1)S(1)} %get-tuple-element.51), channel_id=1, source_target_pairs={{0,2},{2,0},{4,6},{6,4},{8,10},{10,8},{12,14},{14,12},{16,18},{18,... | collective-permute-start | bytes 196616 | tf_op jit(solution)/shard_map/ppermute | solution.py:25
  61.6 0.7 collective-permute-start.14
  62.4 1.3 %collective-permute-start.15 = (bf16[4,16,512]{2,1,0:T(8,128)(2,1)S(1)}, bf16[4,16,512]{2,1,0:T(8,128)(2,1)S(1)}, u32[]{:S(2)}, u32[]{:S(2)}) collective-permute-start(bf16[4,16,512]{2,1,0:T(8,128)(2,1)S(1)} %get-tuple-element.50), channel_id=1, source_target_pairs={{0,6},{2,4},{4,2},{6,0},{8,14},{10,12},{12,10},{14,8},{16,22},{18,... | collective-permute-start | bytes 196616 | tf_op jit(solution)/shard_map/ppermute | solution.py:25
  63.7 2.3 %collective-permute-done.11 = bf16[2,256,256]{2,1,0:T(8,128)(2,1)S(1)} collective-permute-done((bf16[2,256,256]{2,1,0:T(8,128)(2,1)}, bf16[2,256,256]{2,1,0:T(8,128)(2,1)S(1)}, u32[]{:S(2)}, u32[]{:S(2)}) %collective-permute-start.11) | collective-permute-done | bytes 262176 | tf_op jit(solution)/shard_map/ppermute | solution.py:25
  66.0 1.2 %convolution_convert_fusion.2 = bf16[256,512]{1,0:T(8,128)(2,1)} fusion(bf16[512,1024]{1,0:T(8,128)(2,1)S(1)} %copy-done, bf16[256,256]{1,0:T(8,128)(2,1)S(1)} %get-tuple-element.54, bf16[256,256]{1,0:T(8,128)(2,1)S(1)} %get-tuple-element.52, bf16[256,256]{1,0:T(8,128)(2,1)S(1)} %copy-done.13, bf16[256,256]{1,0:T(8,128)(2,1)S(1)} %copy-done.14, pred[]{:T(512)S(6)} %eq.52), kind=kOutput, calls=%fused_computation.2 | convolution fusion | flops 273022976 | bytes 1835009 | tf_op jit(solution)/shard_map/dot_general | solution.py:295
  67.2 0.3 collective-permute-done.15
  67.6 3.4 %collective-permute-start.16 = (bf16[2,16,512]{2,1,0:T(8,128)(2,1)S(1)}, bf16[2,16,512]{2,1,0:T(8,128)(2,1)S(1)}, u32[]{:S(2)}, u32[]{:S(2)}) collective-permute-start(bf16[2,16,512]{2,1,0:T(8,128)(2,1)S(1)} %slice.113), channel_id=1, source_target_pairs={{0,16},{2,18},{4,20},{6,22},{8,24},{10,26},{12,28},{14,30},{16,0},... | collective-permute-start | bytes 98312 | tf_op jit(solution)/shard_map/ppermute | solution.py:25
  71.0 0.9 %maximum_select_fusion = bf16[1,256,1024]{2,1,0:T(8,128)(2,1)} fusion(bf16[1,256,256]{2,1,0:T(8,128)(2,1)S(1)} %get-tuple-element.55, bf16[1,256,256]{2,1,0:T(8,128)(2,1)S(1)} %get-tuple-element.53, bf16[1,256,256]{2,1,0:T(8,128)(2,1)S(1)} %bitcast.52, bf16[1,256,256]{2,1,0:T(8,128)(2,1)S(1)} %bitcast.51, pred[]{:T(512)S(6)} %eq.52), kind=kLoop, calls=%fused_computation.7 | loop fusion | flops 4456448 | bytes 1048577 | tf_op jit(solution)/shard_map/jit(_where)/select_n | solution.py:290
  71.9 1.3 %collective-permute-done.16 = bf16[2,16,512]{2,1,0:T(8,128)(2,1)S(1)} collective-permute-done((bf16[2,16,512]{2,1,0:T(8,128)(2,1)S(1)}, bf16[2,16,512]{2,1,0:T(8,128)(2,1)S(1)}, u32[]{:S(2)}, u32[]{:S(2)}) %collective-permute-start.16) | collective-permute-done | bytes 32800 | tf_op jit(solution)/shard_map/ppermute | solution.py:25
  73.3 1.4 %collective-permute-start.17 = (bf16[16,512]{1,0:T(8,128)(2,1)S(1)}, bf16[16,512]{1,0:T(8,128)(2,1)S(1)}, u32[]{:S(2)}, u32[]{:S(2)}) collective-permute-start(bf16[16,512]{1,0:T(8,128)(2,1)S(1)} %fusion.19), channel_id=1, source_target_pairs={{0,8},{2,10},{4,12},{6,14},{8,0},{10,2},{12,4},{14,6},{16,24},{18,... | collective-permute-start | bytes 49160 | tf_op jit(solution)/shard_map/ppermute | solution.py:25
  74.6 2.4 %collective-permute-done.17 = bf16[16,512]{1,0:T(8,128)(2,1)S(1)} collective-permute-done((bf16[16,512]{1,0:T(8,128)(2,1)S(1)}, bf16[16,512]{1,0:T(8,128)(2,1)S(1)}, u32[]{:S(2)}, u32[]{:S(2)}) %collective-permute-start.17) | collective-permute-done | bytes 16416 | tf_op jit(solution)/shard_map/ppermute | solution.py:25
  77.1 0.6 maximum_select_fusion.3
  (77 shorter events, 1.1 us)
Async XLA Ops:
  0.6 31.9 %copy-start = (bf16[512,1024]{1,0:T(8,128)(2,1)S(1)}, bf16[512,1024]{1,0:T(8,128)(2,1)}, u32[]{:S(2)}) copy-start(bf16[512,1024]{1,0:T(8,128)(2,1)} %param.9) | copy-start | bytes 3145732
  0.6 8.0 %copy-start.1 = (bf16[1,256,1024]{2,1,0:T(8,128)(2,1)S(1)}, bf16[1,256,1024]{2,1,0:T(8,128)(2,1)}, u32[]{:S(2)}) copy-start(bf16[1,256,1024]{2,1,0:T(8,128)(2,1)} %param.14) | copy-start | bytes 1572868
  3.5 3.9 %copy-start.5 = (bf16[272,256]{1,0:T(8,128)(2,1)S(1)}, bf16[272,256]{1,0:T(8,128)(2,1)}, u32[]{:S(2)}) copy-start(bf16[272,256]{1,0:T(8,128)(2,1)} %get-tuple-element.24) | copy-start | bytes 417796
  3.5 6.9 %collective-permute-start = (bf16[272,256]{1,0:T(8,128)(2,1)}, bf16[272,256]{1,0:T(8,128)(2,1)S(1)}, u32[]{:S(2)}, u32[]{:S(2)}) collective-permute-start(bf16[272,256]{1,0:T(8,128)(2,1)} %get-tuple-element.22), channel_id=1, source_target_pairs={{0,8},{2,10},{4,12},{6,14},{8,0},{10,2},{12,4},{14,6},{16,24},{18,... | collective-permute-start | bytes 417800 | tf_op jit(solution)/shard_map/ppermute | solution.py:25
  7.3 0.7 copy-start.9
  8.7 1.0 %copy-start.4 = (bf16[1,256,512]{2,1,0:T(8,128)(2,1)S(1)}, bf16[1,256,512]{2,1,0:T(8,128)(2,1)}, u32[]{:S(2)}) copy-start(bf16[1,256,512]{2,1,0:T(8,128)(2,1)} %param.8) | copy-start | bytes 786436
  10.4 9.2 %collective-permute-start.2 = (bf16[2,144,256]{2,1,0:T(8,128)(2,1)S(1)}, bf16[2,144,256]{2,1,0:T(8,128)(2,1)S(1)}, u32[]{:S(2)}, u32[]{:S(2)}) collective-permute-start(bf16[2,144,256]{2,1,0:T(8,128)(2,1)S(1)} %pad_maximum_fusion.7), channel_id=1, source_target_pairs={{0,16},{2,18},{4,20},{6,22},{8,24},{10,26},{12,28},{14,30},{16,0},... | collective-permute-start | bytes 442376 | tf_op jit(solution)/shard_map/ppermute | solution.py:25
  13.2 18.4 %collective-permute-start.1 = (bf16[512,512]{1,0:T(8,128)(2,1)S(1)}, bf16[512,512]{1,0:T(8,128)(2,1)S(1)}, u32[]{:S(2)}, u32[]{:S(2)}) collective-permute-start(bf16[512,512]{1,0:T(8,128)(2,1)S(1)} %pad_maximum_fusion), channel_id=1, source_target_pairs={{0,8},{2,10},{4,12},{6,14},{8,0},{10,2},{12,4},{14,6},{16,24},{18,... | collective-permute-start | bytes 1572872 | tf_op jit(solution)/shard_map/ppermute | solution.py:25
  14.8 4.8 %copy-start.8 = (s32[1,8,16]{2,1,0:T(8,128)S(1)}, s32[1,8,16]{2,1,0:T(8,128)}, u32[]{:S(2)}) copy-start(s32[1,8,16]{2,1,0:T(8,128)} %blocks_ref.1) | copy-start | bytes 1540
  19.6 12.0 %copy-start.2 = (bf16[4,144,256]{2,1,0:T(8,128)(2,1)}, bf16[4,144,256]{2,1,0:T(8,128)(2,1)S(1)}, u32[]{:S(2)}) copy-start(bf16[4,144,256]{2,1,0:T(8,128)(2,1)S(1)} %pad_maximum_fusion.5.refs_4_.refs_8_) | copy-start | bytes 884740
  19.8 15.3 %collective-permute-start.5 = (bf16[4,144,256]{2,1,0:T(8,128)(2,1)S(1)}, bf16[4,144,256]{2,1,0:T(8,128)(2,1)}, u32[]{:S(2)}, u32[]{:S(2)}) collective-permute-start(bf16[4,144,256]{2,1,0:T(8,128)(2,1)S(1)} %pad_maximum_fusion.5.refs_4_.refs_8_), channel_id=1, source_target_pairs={{0,6},{2,4},{4,2},{6,0},{8,14},{10,12},{12,10},{14,8},{16,22},{18,... | collective-permute-start | bytes 884744 | tf_op jit(solution)/shard_map/ppermute | solution.py:25
  22.1 13.0 %collective-permute-start.4 = (bf16[4,144,256]{2,1,0:T(8,128)(2,1)S(1)}, bf16[4,144,256]{2,1,0:T(8,128)(2,1)}, u32[]{:S(2)}, u32[]{:S(2)}) collective-permute-start(bf16[4,144,256]{2,1,0:T(8,128)(2,1)S(1)} %pad_maximum_fusion.5.refs_4_.refs_8_), channel_id=1, source_target_pairs={{0,4},{2,6},{4,0},{6,2},{8,12},{10,14},{12,8},{14,10},{16,20},{18,... | collective-permute-start | bytes 884744 | tf_op jit(solution)/shard_map/ppermute | solution.py:25
  22.6 12.5 %collective-permute-start.3 = (bf16[4,144,256]{2,1,0:T(8,128)(2,1)S(1)}, bf16[4,144,256]{2,1,0:T(8,128)(2,1)}, u32[]{:S(2)}, u32[]{:S(2)}) collective-permute-start(bf16[4,144,256]{2,1,0:T(8,128)(2,1)S(1)} %pad_maximum_fusion.5.refs_4_.refs_8_), channel_id=1, source_target_pairs={{0,2},{2,0},{4,6},{6,4},{8,10},{10,8},{12,14},{14,12},{16,18},{18,... | collective-permute-start | bytes 884744 | tf_op jit(solution)/shard_map/ppermute | solution.py:25
  23.7 7.9 %collective-permute-start.6 = (bf16[2,128,256]{2,1,0:T(8,128)(2,1)S(1)}, bf16[2,128,256]{2,1,0:T(8,128)(2,1)S(1)}, u32[]{:S(2)}, u32[]{:S(2)}) collective-permute-start(bf16[2,128,256]{2,1,0:T(8,128)(2,1)S(1)} %pad_maximum_fusion.8), channel_id=1, source_target_pairs={{0,16},{2,18},{4,20},{6,22},{8,24},{10,26},{12,28},{14,30},{16,0},... | collective-permute-start | bytes 393224 | tf_op jit(solution)/shard_map/ppermute | solution.py:25
  31.6 6.4 %copy-start.3 = (bf16[4,128,256]{2,1,0:T(8,128)(2,1)}, bf16[4,128,256]{2,1,0:T(8,128)(2,1)S(1)}, u32[]{:S(2)}) copy-start(bf16[4,128,256]{2,1,0:T(8,128)(2,1)S(1)} %pad_maximum_fusion.6.refs_4_) | copy-start | bytes 786436
  35.1 11.7 %collective-permute-start.9 = (bf16[4,128,256]{2,1,0:T(8,128)(2,1)S(1)}, bf16[4,128,256]{2,1,0:T(8,128)(2,1)S(1)}, u32[]{:S(2)}, u32[]{:S(2)}) collective-permute-start(bf16[4,128,256]{2,1,0:T(8,128)(2,1)S(1)} %pad_maximum_fusion.6.refs_4_), channel_id=1, source_target_pairs={{0,6},{2,4},{4,2},{6,0},{8,14},{10,12},{12,10},{14,8},{16,22},{18,... | collective-permute-start | bytes 786440 | tf_op jit(solution)/shard_map/ppermute | solution.py:25
  37.5 11.4 %collective-permute-start.8 = (bf16[4,128,256]{2,1,0:T(8,128)(2,1)S(1)}, bf16[4,128,256]{2,1,0:T(8,128)(2,1)S(1)}, u32[]{:S(2)}, u32[]{:S(2)}) collective-permute-start(bf16[4,128,256]{2,1,0:T(8,128)(2,1)S(1)} %pad_maximum_fusion.6.refs_4_), channel_id=1, source_target_pairs={{0,4},{2,6},{4,0},{6,2},{8,12},{10,14},{12,8},{14,10},{16,20},{18,... | collective-permute-start | bytes 786440 | tf_op jit(solution)/shard_map/ppermute | solution.py:25
  38.0 10.9 %collective-permute-start.7 = (bf16[4,128,256]{2,1,0:T(8,128)(2,1)S(1)}, bf16[4,128,256]{2,1,0:T(8,128)(2,1)S(1)}, u32[]{:S(2)}, u32[]{:S(2)}) collective-permute-start(bf16[4,128,256]{2,1,0:T(8,128)(2,1)S(1)} %pad_maximum_fusion.6.refs_4_), channel_id=1, source_target_pairs={{0,2},{2,0},{4,6},{6,4},{8,10},{10,8},{12,14},{14,12},{16,18},{18,... | collective-permute-start | bytes 786440 | tf_op jit(solution)/shard_map/ppermute | solution.py:25
  45.8 11.1 %collective-permute-start.10 = (bf16[2,256,256]{2,1,0:T(8,128)(2,1)}, bf16[2,256,256]{2,1,0:T(8,128)(2,1)S(1)}, u32[]{:S(2)}, u32[]{:S(2)}) collective-permute-start(bf16[2,256,256]{2,1,0:T(8,128)(2,1)} %get-tuple-element.32), channel_id=1, source_target_pairs={{0,8},{2,10},{4,12},{6,14},{8,0},{10,2},{12,4},{14,6},{16,24},{18,... | collective-permute-start | bytes 786440 | tf_op jit(solution)/shard_map/ppermute | solution.py:25
  46.8 2.1 %copy-start.10 = (bf16[4,128,256]{2,1,0:T(8,128)(2,1)}, bf16[4,128,256]{2,1,0:T(8,128)(2,1)S(1)}, u32[]{:S(2)}) copy-start(bf16[4,128,256]{2,1,0:T(8,128)(2,1)S(1)} %collective-permute-done.9.refs_7_) | copy-start | bytes 786436
  48.9 0.7 copy-start.11
  48.9 0.8 %copy-start.12 = (bf16[4,128,256]{2,1,0:T(8,128)(2,1)}, bf16[4,128,256]{2,1,0:T(8,128)(2,1)S(1)}, u32[]{:S(2)}) copy-start(bf16[4,128,256]{2,1,0:T(8,128)(2,1)S(1)} %collective-permute-done.7.refs_5_) | copy-start | bytes 786436
  56.9 2.0 %collective-permute-start.12 = (bf16[4,4,16,512]{3,2,1,0:T(8,128)(2,1)}, bf16[4,4,16,512]{3,2,1,0:T(8,128)(2,1)S(1)}, u32[]{:S(2)}, u32[]{:S(2)}) collective-permute-start(bf16[4,4,16,512]{3,2,1,0:T(8,128)(2,1)} %bitcast.53), channel_id=1, source_target_pairs={{0,1},{1,0},{2,3},{3,2},{4,5},{5,4},{6,7},{7,6},{8,9},{9,8},{10,11... | collective-permute-start | bytes 786440 | tf_op jit(solution)/shard_map/ppermute | solution.py:25
  57.0 9.0 %collective-permute-start.11 = (bf16[2,256,256]{2,1,0:T(8,128)(2,1)}, bf16[2,256,256]{2,1,0:T(8,128)(2,1)S(1)}, u32[]{:S(2)}, u32[]{:S(2)}) collective-permute-start(bf16[2,256,256]{2,1,0:T(8,128)(2,1)} %get-tuple-element.33), channel_id=1, source_target_pairs={{0,8},{2,10},{4,12},{6,14},{8,0},{10,2},{12,4},{14,6},{16,24},{18,... | collective-permute-start | bytes 786440 | tf_op jit(solution)/shard_map/ppermute | solution.py:25
  60.0 5.9 %collective-permute-start.13 = (bf16[4,16,512]{2,1,0:T(8,128)(2,1)S(1)}, bf16[4,16,512]{2,1,0:T(8,128)(2,1)S(1)}, u32[]{:S(2)}, u32[]{:S(2)}) collective-permute-start(bf16[4,16,512]{2,1,0:T(8,128)(2,1)S(1)} %get-tuple-element.51), channel_id=1, source_target_pairs={{0,2},{2,0},{4,6},{6,4},{8,10},{10,8},{12,14},{14,12},{16,18},{18,... | collective-permute-start | bytes 196616 | tf_op jit(solution)/shard_map/ppermute | solution.py:25
  61.6 5.6 %collective-permute-start.14 = (bf16[4,16,512]{2,1,0:T(8,128)(2,1)S(1)}, bf16[4,16,512]{2,1,0:T(8,128)(2,1)S(1)}, u32[]{:S(2)}, u32[]{:S(2)}) collective-permute-start(bf16[4,16,512]{2,1,0:T(8,128)(2,1)S(1)} %get-tuple-element.49), channel_id=1, source_target_pairs={{0,4},{2,6},{4,0},{6,2},{8,12},{10,14},{12,8},{14,10},{16,20},{18,... | collective-permute-start | bytes 196616 | tf_op jit(solution)/shard_map/ppermute | solution.py:25
  62.4 3.7 %copy-start.13 = (bf16[256,256]{1,0:T(8,128)(2,1)S(1)}, bf16[256,256]{1,0:T(8,128)(2,1)}, u32[]{:S(2)}) copy-start(bf16[256,256]{1,0:T(8,128)(2,1)} %get-tuple-element.39) | copy-start | bytes 393220
  62.4 3.7 %copy-start.14 = (bf16[256,256]{1,0:T(8,128)(2,1)S(1)}, bf16[256,256]{1,0:T(8,128)(2,1)}, u32[]{:S(2)}) copy-start(bf16[256,256]{1,0:T(8,128)(2,1)} %get-tuple-element.38) | copy-start | bytes 393220
  62.4 5.2 %collective-permute-start.15 = (bf16[4,16,512]{2,1,0:T(8,128)(2,1)S(1)}, bf16[4,16,512]{2,1,0:T(8,128)(2,1)S(1)}, u32[]{:S(2)}, u32[]{:S(2)}) collective-permute-start(bf16[4,16,512]{2,1,0:T(8,128)(2,1)S(1)} %get-tuple-element.50), channel_id=1, source_target_pairs={{0,6},{2,4},{4,2},{6,0},{8,14},{10,12},{12,10},{14,8},{16,22},{18,... | collective-permute-start | bytes 196616 | tf_op jit(solution)/shard_map/ppermute | solution.py:25
  67.5 3.5 %copy-start.6 = (bf16[256,256]{1,0:T(8,128)(2,1)S(1)}, bf16[256,256]{1,0:T(8,128)(2,1)}, u32[]{:S(2)}) copy-start(bf16[256,256]{1,0:T(8,128)(2,1)} %get-tuple-element.26) | copy-start | bytes 393220
  67.5 3.5 %copy-start.7 = (bf16[256,256]{1,0:T(8,128)(2,1)S(1)}, bf16[256,256]{1,0:T(8,128)(2,1)}, u32[]{:S(2)}) copy-start(bf16[256,256]{1,0:T(8,128)(2,1)} %get-tuple-element.31) | copy-start | bytes 393220
  67.6 5.7 %collective-permute-start.16 = (bf16[2,16,512]{2,1,0:T(8,128)(2,1)S(1)}, bf16[2,16,512]{2,1,0:T(8,128)(2,1)S(1)}, u32[]{:S(2)}, u32[]{:S(2)}) collective-permute-start(bf16[2,16,512]{2,1,0:T(8,128)(2,1)S(1)} %slice.113), channel_id=1, source_target_pairs={{0,16},{2,18},{4,20},{6,22},{8,24},{10,26},{12,28},{14,30},{16,0},... | collective-permute-start | bytes 98312 | tf_op jit(solution)/shard_map/ppermute | solution.py:25
  73.3 3.8 %collective-permute-start.17 = (bf16[16,512]{1,0:T(8,128)(2,1)S(1)}, bf16[16,512]{1,0:T(8,128)(2,1)S(1)}, u32[]{:S(2)}, u32[]{:S(2)}) collective-permute-start(bf16[16,512]{1,0:T(8,128)(2,1)S(1)} %fusion.19), channel_id=1, source_target_pairs={{0,8},{2,10},{4,12},{6,14},{8,0},{10,2},{12,4},{14,6},{16,24},{18,... | collective-permute-start | bytes 49160 | tf_op jit(solution)/shard_map/ppermute | solution.py:25

commit v3 on v2

--- a/solution.py
+++ b/solution.py
@@ -40,7 +40,13 @@
     length = lengths_ref[0]
     count = half * blk_dev
     room = -(-count // TILE) * TILE
-    for out, first in zip(outs, (side * half, (1 - side) * half)):
+    keep_near, keep_late, send_near, send_all = outs
+    near_rows = keep_near.shape[0]
+    sides = (
+        (side * half, ((keep_near, 0),), ((keep_late, 0),)),
+        ((1 - side) * half, ((send_near, 0), (send_all, 0)), ((send_all, near_rows),)),
+    )
+    for first, near, late in sides:
         for index in range(half):
             head = first + index
             local = jnp.int32(0)
@@ -48,10 +54,13 @@
                 block = blocks_ref[0, head, entry] - rank * blk_dev
                 local = jnp.where((block >= 0) & (block < blk_dev), block, local)
             low = pl.multiple_of(local * BLK, BLK)
-            at = index * BLK + (room if index >= cut else 0)
+            at = (index - (cut if index >= cut else 0)) * BLK
             columns = pl.ds(pl.multiple_of(head * head_dim, head_dim), head_dim)
-            out[at : at + BLK, :head_dim] = keys_ref[0, pl.ds(low, BLK), columns]
-            out[at : at + BLK, head_dim:] = values_ref[0, pl.ds(low, BLK), columns]
+            key = keys_ref[0, pl.ds(low, BLK), columns]
+            value = values_ref[0, pl.ds(low, BLK), columns]
+            for out, base in late if index >= cut else near:
+                out[base + at : base + at + BLK, :head_dim] = key
+                out[base + at : base + at + BLK, head_dim:] = value
         span = pl.ds(pl.multiple_of(first * head_dim, head_dim), half * head_dim)
         for source, low in ((keys_ref, 0), (values_ref, head_dim)):
             totals = []
@@ -67,7 +76,8 @@
             ]
             lines.append(jnp.zeros((room - count, head_dim), F32))
             summary = jnp.concatenate(lines, axis=0).astype(BF16)
-            out[cut * BLK : cut * BLK + room, low : low + head_dim] = summary
+            for out, _ in near:
+                out[cut * BLK : cut * BLK + room, low : low + head_dim] = summary
 
 
 def attend_kernel(pieces, fine_width, scale, *refs):
@@ -181,13 +191,6 @@
     return [column] + [swap(column, "hist", mask) for mask in range(1, QUAD)]
 
 
-def gather_rest(pair):
-    count = lax.axis_size("hist") // (QUAD * PAIR)
-    return jnp.concatenate(
-        [pair] + [swap(pair, "hist", QUAD * PAIR * k) for k in range(1, count)], axis=0
-    )
-
-
 def shards(targets, w_query, keys, values, blocks, lengths, d_attended):
     heads = blocks.shape[1]
     local_rows, width = keys.shape[1:]
@@ -204,10 +207,9 @@
     wide = half * head_dim
     count = half * blk_dev
     room = -(-count // TILE) * TILE
-    first_rows = CUT * BLK + room
-
-    shape = jax.ShapeDtypeStruct((half * BLK + room, 2 * head_dim), BF16)
-    keep, send = pl.pallas_call(
+    near_rows = CUT * BLK + room
+    late_rows = (half - CUT) * BLK
+    keep_near, keep_late, send_near, send = pl.pallas_call(
         functools.partial(select_kernel, CUT),
         in_specs=[
             pl.BlockSpec(memory_space=pltpu.SMEM),
@@ -215,24 +217,35 @@
             pl.BlockSpec(memory_space=pltpu.VMEM),
             pl.BlockSpec(memory_space=pltpu.VMEM),
         ],
-        out_specs=[pl.BlockSpec(memory_space=pltpu.VMEM)] * 2,
-        out_shape=[shape] * 2,
+        out_specs=[pl.BlockSpec(memory_space=pltpu.VMEM)] * 4,
+        out_shape=[
+            jax.ShapeDtypeStruct((size, 2 * head_dim), BF16)
+            for size in (near_rows, late_rows, near_rows, near_rows + late_rows)
+        ],
         name="select",
     )(blocks, lengths, keys, values)
     came = swap(send, "hist", QUAD)
-    pair_near = jnp.stack([keep[:first_rows], came[:first_rows]])
-    pair_late = jnp.stack([keep[first_rows:], came[first_rows:]])
-    column_near = gather_rest(pair_near)
-    column_late = gather_rest(after(pair_late, column_near))
+    column_near = jnp.stack(
+        [keep_near, came[:near_rows]]
+        + [
+            swap((keep_near, send_near)[k % PAIR], "hist", QUAD * k)
+            for k in range(PAIR, n_hist // QUAD)
+        ]
+    )
     near = gather_quad(column_near)
+    pair_late = after(jnp.stack([keep_late, came[near_rows:]]), column_near)
+    column_late = jnp.concatenate(
+        [pair_late]
+        + [swap(pair_late, "hist", QUAD * k) for k in range(PAIR, n_hist // QUAD, PAIR)]
+    )
 
     grad = d_attended[0]
     grad_keep = lax.dynamic_slice_in_dim(grad, side * wide, wide, 1)
     grad_send = lax.dynamic_slice_in_dim(grad, (1 - side) * wide, wide, 1)
-    mine = jnp.concatenate([targets[0], grad_send], axis=0)
-    theirs = swap(after(mine, came), "hist", QUAD)
-    both_targets = jnp.concatenate([targets[0], theirs[:rows]], axis=0)
-    both_grads = jnp.concatenate([grad_keep, theirs[rows:]], axis=0)
+    theirs = swap(jnp.concatenate([targets[0], grad_send]), "hist", QUAD)
+    their_targets, their_grads = theirs[:rows], theirs[rows:]
+    both_targets = jnp.concatenate([targets[0], their_targets], axis=0)
+    both_grads = jnp.concatenate([grad_keep, their_grads], axis=0)
     weights = lax.dynamic_slice_in_dim(w_query, side * wide, wide, 1)
     query = jnp.dot(both_targets, weights, preferred_element_type=F32).astype(BF16)
 
@@ -297,15 +310,12 @@
     ).astype(BF16)
     level = after(level, (attended, d_targets))
 
-    mask = n_hist // QUAD
-    while mask > PAIR:
-        mask //= 2
-        level = level[:mask] + swap(level[mask:].astype(BF16), "hist", QUAD * mask).astype(F32)
-    other = swap(level[1].astype(BF16), "hist", QUAD).astype(F32)
+    sums = [level[0], None]
+    for index in range(1, n_hist // QUAD):
+        got = swap(level[index].astype(BF16), "hist", QUAD * index).astype(F32)
+        sums[index % PAIR] = got if sums[index % PAIR] is None else sums[index % PAIR] + got
     d_query_weight = jnp.where(
-        side == 0,
-        jnp.concatenate([level[0], other], axis=1),
-        jnp.concatenate([other, level[0]], axis=1),
+        side == 0, jnp.concatenate(sums, axis=1), jnp.concatenate(sums[::-1], axis=1)
     )
     return (attended[None], d_targets[None], d_query_weight)
 

time: 78.1 us -> 74.9 us (0.959)
  starting transfers between devices: 27.2 us -> 25 us
  waiting for transfers between devices: 19.8 us -> 19 us
    ppermute x18 -> x20, starting transfers between devices: 27.2 us -> 25 us  [swap(): return lax.ppermute(array, axis, [(i, i ^ mask) for i in range(size)])]
    another operation x4 -> x2, local copies, waits for them, and re-layouts: 0.86 us -> 0.01 us  [the longest x1 0.01 us: shards(): jnp.stack([keep_near, came[:near_rows]] + [swap((keep_near, send_near)[k...]
    ppermute x18 -> x20, waiting for transfers between devices: 19.8 us -> 19 us  [swap(): return lax.ppermute(array, axis, [(i, i ^ mask) for i in range(size)])]
    unnamed x30 -> x32, local copies, waits for them, and re-layouts: 2.21 us -> 2.95 us
  transfers between devices with their start and end apart: 18 -> 20, of which waited for: 8 -> 9; matrix products, arithmetic and copies ran while one was open for 12% -> 12% of each run, Pallas kernels for 19% -> 19%
where the time goes in v3:
time: 74.9 us; the launch traced here: 74.5 us
  starting transfers between devices  25 us (33%)
  waiting for transfers between devices  19 us (25%)
  Pallas kernels  16.4 us (22%)
  local copies, waits for them, and re-layouts  4.64 us (6%)
  other arithmetic  4 us (5%)
  matrix products  3.75 us (5%)
  between operations  1.71 us (2%)
    ppermute x20, starting transfers between devices, swap(): return lax.ppermute(array, axis, [(i, i ^ mask) for i in range(size)])  25 us
    ppermute x20, waiting for transfers between devices, swap(): return lax.ppermute(array, axis, [(i, i ^ mask) for i in range(size)])  19 us
    pallas_call x2, Pallas kernels, attend(): pl.pallas_call(functools.partial(attend_kernel, len(pieces), fine_width,...  14.4 us
    unnamed x32, local copies, waits for them, and re-layouts  2.95 us
    pallas_call x1, Pallas kernels, shards(): pl.pallas_call(functools.partial(select_kernel, CUT), in_specs=[pl.BlockS...  2.07 us
  transfers between devices with their start and end apart: 20, of which 9 were waited for; matrix products, arithmetic and copies ran while one was open for 12% of the time, Pallas kernels for 19%

profile of v3, /device:TPU:0, one launch (start us, length us, event | category | flops | bytes accessed | tf_op | source)
XLA Modules:
  0.0 74.5 jit_solution(1489285330801972275)
XLA Ops:
  1.4 2.1 %select.34 = (bf16[144,256]{1,0:T(8,128)(2,1)}, bf16[128,256]{1,0:T(8,128)(2,1)}, bf16[144,256]{1,0:T(8,128)(2,1)}, bf16[272,256]{1,0:T(8,128)(2,1)}) custom-call(s32[1,8,16]{2,1,0:T(8,128)} %blocks_ref.1, s32[1]{0:T(128)} %copy.15.lengths_ref, bf16[1,128,1024]{2,1,0:T(8,128)(2,1)} %keys_ref.1, bf16[1,128,1024]{2,1,0:T(8,128)(2,1)} %values_ref.1), custom_call_target="tpu_custom_call" | custom-call | tf_op jit(solution)/shard_map/select/pallas_call | solution.py:212
  3.5 5.0 %collective-permute-start.3 = (bf16[144,256]{1,0:T(8,128)(2,1)}, bf16[144,256]{1,0:T(8,128)(2,1)S(1)}, u32[]{:S(2)}, u32[]{:S(2)}) collective-permute-start(bf16[144,256]{1,0:T(8,128)(2,1)} %get-tuple-element.25), channel_id=1, source_target_pairs={{0,24},{2,26},{4,28},{6,30},{8,16},{10,18},{12,20},{14,22},{16,8},... | collective-permute-start | bytes 221192 | tf_op jit(solution)/shard_map/ppermute | solution.py:25
  8.5 0.6 collective-permute-start.1
  9.2 0.9 %copy-done.4 = bf16[1,256,512]{2,1,0:T(8,128)(2,1)S(1)} copy-done((bf16[1,256,512]{2,1,0:T(8,128)(2,1)S(1)}, bf16[1,256,512]{2,1,0:T(8,128)(2,1)}, u32[]{:S(2)}) %copy-start.4) | copy-done | bytes 262168
  10.1 1.5 %collective-permute-start = (bf16[512,512]{1,0:T(8,128)(2,1)S(1)}, bf16[512,512]{1,0:T(8,128)(2,1)S(1)}, u32[]{:S(2)}, u32[]{:S(2)}) collective-permute-start(bf16[512,512]{1,0:T(8,128)(2,1)S(1)} %pad_maximum_fusion), channel_id=1, source_target_pairs={{0,8},{2,10},{4,12},{6,14},{8,0},{10,2},{12,4},{14,6},{16,24},{18,... | collective-permute-start | bytes 1572872 | tf_op jit(solution)/shard_map/ppermute | solution.py:25
  11.6 0.6 copy-done.10
  12.3 0.1 broadcast_reduce_fusion
  12.6 0.1 and.86
  13.1 3.7 %collective-permute-done.1 = bf16[272,256]{1,0:T(8,128)(2,1)S(1)} collective-permute-done((bf16[272,256]{1,0:T(8,128)(2,1)}, bf16[272,256]{1,0:T(8,128)(2,1)S(1)}, u32[]{:S(2)}, u32[]{:S(2)}) %collective-permute-start.1) | collective-permute-done | bytes 139296 | tf_op jit(solution)/shard_map/ppermute | solution.py:25
  16.9 0.6 copy-done.9
  17.5 0.1 select_reduce_fusion
  17.7 2.6 %collective-permute-start.6 = (bf16[4,144,256]{2,1,0:T(8,128)(2,1)S(1)}, bf16[4,144,256]{2,1,0:T(8,128)(2,1)}, u32[]{:S(2)}, u32[]{:S(2)}) collective-permute-start(bf16[4,144,256]{2,1,0:T(8,128)(2,1)S(1)} %pad_maximum_fusion.5.refs_4_.refs_8_), channel_id=1, source_target_pairs={{0,6},{2,4},{4,2},{6,0},{8,14},{10,12},{12,10},{14,8},{16,22},{18,... | collective-permute-start | bytes 884744 | tf_op jit(solution)/shard_map/ppermute | solution.py:25
  20.3 0.5 collective-permute-start.5
  20.8 0.4 collective-permute-start.4
  21.3 0.1 and.82
  21.5 0.1 add.139
  21.6 1.5 %collective-permute-start.7 = (bf16[2,128,256]{2,1,0:T(8,128)(2,1)S(1)}, bf16[2,128,256]{2,1,0:T(8,128)(2,1)S(1)}, u32[]{:S(2)}, u32[]{:S(2)}) collective-permute-start(bf16[2,128,256]{2,1,0:T(8,128)(2,1)S(1)} %pad_maximum_fusion.7), channel_id=1, source_target_pairs={{0,16},{2,18},{4,20},{6,22},{8,24},{10,26},{12,28},{14,30},{16,0},... | collective-permute-start | bytes 393224 | tf_op jit(solution)/shard_map/ppermute | solution.py:25
  23.2 0.6 broadcast_in_dim.57.refs_2_
  23.8 5.2 %collective-permute-done.7 = bf16[2,128,256]{2,1,0:T(8,128)(2,1)S(1)} collective-permute-done((bf16[2,128,256]{2,1,0:T(8,128)(2,1)S(1)}, bf16[2,128,256]{2,1,0:T(8,128)(2,1)S(1)}, u32[]{:S(2)}, u32[]{:S(2)}) %collective-permute-start.7) | collective-permute-done | bytes 131104 | tf_op jit(solution)/shard_map/ppermute | solution.py:25
  29.0 0.8 %collective-permute-done = bf16[512,512]{1,0:T(8,128)(2,1)S(1)} collective-permute-done((bf16[512,512]{1,0:T(8,128)(2,1)S(1)}, bf16[512,512]{1,0:T(8,128)(2,1)S(1)}, u32[]{:S(2)}, u32[]{:S(2)}) %collective-permute-start) | collective-permute-done | bytes 524320 | tf_op jit(solution)/shard_map/ppermute | solution.py:25
  29.8 0.8 %pad_maximum_fusion.2.refs_1_ = bf16[512,512]{1,0:T(8,128)(2,1)} fusion(bf16[256,512]{1,0:T(8,128)(2,1)S(1)} %get-tuple-element.49, bf16[256,512]{1,0:T(8,128)(2,1)S(1)} %get-tuple-element.47), kind=kLoop, calls=%fused_computation.6 | loop fusion | flops 1048576 | bytes 1048576 | tf_op jit(solution)/shard_map/concatenate | solution.py:248
  30.7 1.2 %convolution_convert_fusion.1.refs_0_ = bf16[512,512]{1,0:T(8,128)(2,1)} fusion(bf16[512,1024]{1,0:T(8,128)(2,1)S(1)} %copy-done, s32[]{:T(128)S(6)} %select_n.97, bf16[256,512]{1,0:T(8,128)(2,1)S(1)} %bitcast.53, bf16[256,512]{1,0:T(8,128)(2,1)S(1)} %get-tuple-element.50), kind=kOutput, calls=%fused_computation.1 | convolution fusion | flops 269746176 | bytes 1572868 | tf_op jit(solution)/shard_map/dot_general | solution.py:250
  31.9 1.3 %convolution_convert_fusion.refs_3_ = bf16[512,512]{1,0:T(8,128)(2,1)} fusion(s32[512]{0:T(512)S(1)} %add.156, bf16[256,512]{1,0:T(8,128)(2,1)S(1)} %bitcast.54, bf16[256,512]{1,0:T(8,128)(2,1)S(1)} %get-tuple-element.50), kind=kOutput, calls=%fused_computation | convolution fusion | flops 270008320 | bytes 1050624 | tf_op jit(solution)/shard_map/dot_general | solution.py:275
  33.2 2.7 %collective-permute-start.10 = (bf16[4,128,256]{2,1,0:T(8,128)(2,1)S(1)}, bf16[4,128,256]{2,1,0:T(8,128)(2,1)S(1)}, u32[]{:S(2)}, u32[]{:S(2)}) collective-permute-start(bf16[4,128,256]{2,1,0:T(8,128)(2,1)S(1)} %pad_maximum_fusion.6.refs_4_), channel_id=1, source_target_pairs={{0,6},{2,4},{4,2},{6,0},{8,14},{10,12},{12,10},{14,8},{16,22},{18,... | collective-permute-start | bytes 786440 | tf_op jit(solution)/shard_map/ppermute | solution.py:25
  35.9 0.5 collective-permute-start.9
  36.4 0.3 collective-permute-start.8
  36.8 7.2 %attend.2 = (bf16[256,256]{1,0:T(8,128)(2,1)}, bf16[256,256]{1,0:T(8,128)(2,1)}, bf16[2,256,256]{2,1,0:T(8,128)(2,1)}, f32[256,512]{1,0:T(8,128)}, bf16[256,512]{1,0:T(8,128)(2,1)}) custom-call(bf16[512,512]{1,0:T(8,128)(2,1)} %convolution_convert_fusion.1.refs_0_, bf16[512,512]{1,0:T(8,128)(2,1)} %pad_maximum_fusion.2.refs_1_, ...), custom_call_target="tpu_custom_call" | custom-call | flops 1342177280 | bytes 2359296 | tf_op jit(solution)/shard_map/attend/pallas_call | solution.py:161
  43.9 0.9 %collective-permute-start.11 = (bf16[2,256,256]{2,1,0:T(8,128)(2,1)}, bf16[2,256,256]{2,1,0:T(8,128)(2,1)S(1)}, u32[]{:S(2)}, u32[]{:S(2)}) collective-permute-start(bf16[2,256,256]{2,1,0:T(8,128)(2,1)} %get-tuple-element.34), channel_id=1, source_target_pairs={{0,8},{2,10},{4,12},{6,14},{8,0},{10,2},{12,4},{14,6},{16,24},{18,... | collective-permute-start | bytes 786440 | tf_op jit(solution)/shard_map/ppermute | solution.py:25
  44.8 2.4 %collective-permute-done.9.refs_6_ = bf16[4,128,256]{2,1,0:T(8,128)(2,1)S(1)} collective-permute-done((bf16[4,128,256]{2,1,0:T(8,128)(2,1)S(1)}, bf16[4,128,256]{2,1,0:T(8,128)(2,1)S(1)}, u32[]{:S(2)}, u32[]{:S(2)}) %collective-permute-start.9) | collective-permute-done | bytes 262176 | tf_op jit(solution)/shard_map/ppermute | solution.py:25
  47.3 0.3 collective-permute-done.8.refs_5_
  47.6 0.4 copy-done.12
  48.0 0.3 copy-done.13
  48.3 7.2 %attend.3 = (bf16[256,256]{1,0:T(8,128)(2,1)}, bf16[256,256]{1,0:T(8,128)(2,1)}, bf16[2,256,256]{2,1,0:T(8,128)(2,1)}, f32[256,512]{1,0:T(8,128)}, bf16[256,512]{1,0:T(8,128)(2,1)}) custom-call(bf16[512,512]{1,0:T(8,128)(2,1)} %convolution_convert_fusion.1.refs_0_, ...), custom_call_target="tpu_custom_call", output_to_operand_aliasing={{3}: (12, {}), {4}: (13, {})} | custom-call | flops 1342177280 | bytes 2359296 | tf_op jit(solution)/shard_map/attend/pallas_call | solution.py:161
  55.6 0.8 %collective-permute-start.12 = (bf16[2,256,256]{2,1,0:T(8,128)(2,1)}, bf16[2,256,256]{2,1,0:T(8,128)(2,1)S(1)}, u32[]{:S(2)}, u32[]{:S(2)}) collective-permute-start(bf16[2,256,256]{2,1,0:T(8,128)(2,1)} %get-tuple-element.35), channel_id=1, source_target_pairs={{0,8},{2,10},{4,12},{6,14},{8,0},{10,2},{12,4},{14,6},{16,24},{18,... | collective-permute-start | bytes 786440 | tf_op jit(solution)/shard_map/ppermute | solution.py:25
  56.4 0.9 %collective-permute-done.13 = bf16[4,4,16,512]{3,2,1,0:T(8,128)(2,1)S(1)} collective-permute-done((bf16[4,4,16,512]{3,2,1,0:T(8,128)(2,1)}, bf16[4,4,16,512]{3,2,1,0:T(8,128)(2,1)S(1)}, u32[]{:S(2)}, u32[]{:S(2)}) %collective-permute-start.13) | collective-permute-done | bytes 262176 | tf_op jit(solution)/shard_map/ppermute | solution.py:25
  57.3 1.1 %fusion.27 = (bf16[4,4,16,512]{3,2,1,0:T(8,128)(2,1)S(1)}, f32[4,4,16,512]{3,2,1,0:T(8,128)S(1)}) fusion(f32[4,4,16,512]{3,2,1,0:T(8,128)} %bitcast.51, bf16[4,4,16,512]{3,2,1,0:T(8,128)(2,1)S(1)} %collective-permute-done.13), kind=kLoop, calls=%fused_computation.81 | loop fusion | flops 393216 | bytes 1572864 | tf_op jit(solution)/shard_map/convert.5
  58.4 1.6 %collective-permute-start.14 = (bf16[4,16,512]{2,1,0:T(8,128)(2,1)S(1)}, bf16[4,16,512]{2,1,0:T(8,128)(2,1)S(1)}, u32[]{:S(2)}, u32[]{:S(2)}) collective-permute-start(bf16[4,16,512]{2,1,0:T(8,128)(2,1)S(1)} %get-tuple-element.53), channel_id=1, source_target_pairs={{0,2},{2,0},{4,6},{6,4},{8,10},{10,8},{12,14},{14,12},{16,18},{18,... | collective-permute-start | bytes 196616 | tf_op jit(solution)/shard_map/ppermute | solution.py:25
  60.0 0.8 %collective-permute-start.15 = (bf16[4,16,512]{2,1,0:T(8,128)(2,1)S(1)}, bf16[4,16,512]{2,1,0:T(8,128)(2,1)S(1)}, u32[]{:S(2)}, u32[]{:S(2)}) collective-permute-start(bf16[4,16,512]{2,1,0:T(8,128)(2,1)S(1)} %get-tuple-element.51), channel_id=1, source_target_pairs={{0,4},{2,6},{4,0},{6,2},{8,12},{10,14},{12,8},{14,10},{16,20},{18,... | collective-permute-start | bytes 196616 | tf_op jit(solution)/shard_map/ppermute | solution.py:25
  60.8 1.3 %collective-permute-start.16 = (bf16[4,16,512]{2,1,0:T(8,128)(2,1)S(1)}, bf16[4,16,512]{2,1,0:T(8,128)(2,1)S(1)}, u32[]{:S(2)}, u32[]{:S(2)}) collective-permute-start(bf16[4,16,512]{2,1,0:T(8,128)(2,1)S(1)} %get-tuple-element.52), channel_id=1, source_target_pairs={{0,6},{2,4},{4,2},{6,0},{8,14},{10,12},{12,10},{14,8},{16,22},{18,... | collective-permute-start | bytes 196616 | tf_op jit(solution)/shard_map/ppermute | solution.py:25
  62.1 2.4 %collective-permute-done.12 = bf16[2,256,256]{2,1,0:T(8,128)(2,1)S(1)} collective-permute-done((bf16[2,256,256]{2,1,0:T(8,128)(2,1)}, bf16[2,256,256]{2,1,0:T(8,128)(2,1)S(1)}, u32[]{:S(2)}, u32[]{:S(2)}) %collective-permute-start.12) | collective-permute-done | bytes 262176 | tf_op jit(solution)/shard_map/ppermute | solution.py:25
  64.5 1.2 %convolution_convert_fusion.2 = bf16[256,512]{1,0:T(8,128)(2,1)} fusion(bf16[512,1024]{1,0:T(8,128)(2,1)S(1)} %copy-done, bf16[256,256]{1,0:T(8,128)(2,1)S(1)} %get-tuple-element.56, bf16[256,256]{1,0:T(8,128)(2,1)S(1)} %get-tuple-element.54, bf16[256,256]{1,0:T(8,128)(2,1)S(1)} %copy-done.14, bf16[256,256]{1,0:T(8,128)(2,1)S(1)} %copy-done.15, pred[]{:T(512)S(6)} %eq.52), kind=kOutput, calls=%fused_computation.2 | convolution fusion | flops 273022976 | bytes 1835009 | tf_op jit(solution)/shard_map/dot_general | solution.py:308
  65.7 0.2 collective-permute-done.16
  66.0 2.3 %collective-permute-start.17 = (bf16[16,512]{1,0:T(8,128)(2,1)S(1)}, bf16[16,512]{1,0:T(8,128)(2,1)S(1)}, u32[]{:S(2)}, u32[]{:S(2)}) collective-permute-start(bf16[16,512]{1,0:T(8,128)(2,1)S(1)} %get-tuple-element.58), channel_id=1, source_target_pairs={{0,16},{2,18},{4,20},{6,22},{8,24},{10,26},{12,28},{14,30},{16,0},... | collective-permute-start | bytes 49160 | tf_op jit(solution)/shard_map/ppermute | solution.py:25
  68.4 1.0 %collective-permute-start.19 = (bf16[16,512]{1,0:T(8,128)(2,1)S(1)}, bf16[16,512]{1,0:T(8,128)(2,1)S(1)}, u32[]{:S(2)}, u32[]{:S(2)}) collective-permute-start(bf16[16,512]{1,0:T(8,128)(2,1)S(1)} %get-tuple-element.59), channel_id=1, source_target_pairs={{0,24},{2,26},{4,28},{6,30},{8,16},{10,18},{12,20},{14,22},{16,8},... | collective-permute-start | bytes 49160 | tf_op jit(solution)/shard_map/ppermute | solution.py:25
  69.4 0.5 collective-permute-start.18
  69.9 0.9 %maximum_select_fusion = bf16[1,256,1024]{2,1,0:T(8,128)(2,1)} fusion(bf16[1,256,256]{2,1,0:T(8,128)(2,1)S(1)} %get-tuple-element.57, bf16[1,256,256]{2,1,0:T(8,128)(2,1)S(1)} %get-tuple-element.55, bf16[1,256,256]{2,1,0:T(8,128)(2,1)S(1)} %bitcast.56, bf16[1,256,256]{2,1,0:T(8,128)(2,1)S(1)} %bitcast.55, pred[]{:T(512)S(6)} %eq.52), kind=kLoop, calls=%fused_computation.7 | loop fusion | flops 4456448 | bytes 1048577 | tf_op jit(solution)/shard_map/jit(_where)/select_n | solution.py:303
  70.8 3.1 %collective-permute-done.19 = bf16[16,512]{1,0:T(8,128)(2,1)S(1)} collective-permute-done((bf16[16,512]{1,0:T(8,128)(2,1)S(1)}, bf16[16,512]{1,0:T(8,128)(2,1)S(1)}, u32[]{:S(2)}, u32[]{:S(2)}) %collective-permute-start.19) | collective-permute-done | bytes 16416 | tf_op jit(solution)/shard_map/ppermute | solution.py:25
  73.9 0.6 maximum_select_fusion.3
  (79 shorter events, 1.3 us)
Async XLA Ops:
  0.6 30.0 %copy-start = (bf16[512,1024]{1,0:T(8,128)(2,1)S(1)}, bf16[512,1024]{1,0:T(8,128)(2,1)}, u32[]{:S(2)}) copy-start(bf16[512,1024]{1,0:T(8,128)(2,1)} %param.9) | copy-start | bytes 3145732
  0.6 8.5 %copy-start.1 = (bf16[1,256,1024]{2,1,0:T(8,128)(2,1)S(1)}, bf16[1,256,1024]{2,1,0:T(8,128)(2,1)}, u32[]{:S(2)}) copy-start(bf16[1,256,1024]{2,1,0:T(8,128)(2,1)} %param.14) | copy-start | bytes 1572868
  3.5 13.3 %collective-permute-start.3 = (bf16[144,256]{1,0:T(8,128)(2,1)}, bf16[144,256]{1,0:T(8,128)(2,1)S(1)}, u32[]{:S(2)}, u32[]{:S(2)}) collective-permute-start(bf16[144,256]{1,0:T(8,128)(2,1)} %get-tuple-element.25), channel_id=1, source_target_pairs={{0,24},{2,26},{4,28},{6,30},{8,16},{10,18},{12,20},{14,22},{16,8},... | collective-permute-start | bytes 221192 | tf_op jit(solution)/shard_map/ppermute | solution.py:25
  8.5 8.3 %collective-permute-start.2 = (bf16[144,256]{1,0:T(8,128)(2,1)}, bf16[144,256]{1,0:T(8,128)(2,1)S(1)}, u32[]{:S(2)}, u32[]{:S(2)}) collective-permute-start(bf16[144,256]{1,0:T(8,128)(2,1)} %get-tuple-element.23), channel_id=1, source_target_pairs={{0,16},{2,18},{4,20},{6,22},{8,24},{10,26},{12,28},{14,30},{16,0},... | collective-permute-start | bytes 221192 | tf_op jit(solution)/shard_map/ppermute | solution.py:25
  8.5 8.2 %collective-permute-start.1 = (bf16[272,256]{1,0:T(8,128)(2,1)}, bf16[272,256]{1,0:T(8,128)(2,1)S(1)}, u32[]{:S(2)}, u32[]{:S(2)}) collective-permute-start(bf16[272,256]{1,0:T(8,128)(2,1)} %get-tuple-element.24), channel_id=1, source_target_pairs={{0,8},{2,10},{4,12},{6,14},{8,0},{10,2},{12,4},{14,6},{16,24},{18,... | collective-permute-start | bytes 417800 | tf_op jit(solution)/shard_map/ppermute | solution.py:25
  9.1 1.0 %copy-start.4 = (bf16[1,256,512]{2,1,0:T(8,128)(2,1)S(1)}, bf16[1,256,512]{2,1,0:T(8,128)(2,1)}, u32[]{:S(2)}) copy-start(bf16[1,256,512]{2,1,0:T(8,128)(2,1)} %param.8) | copy-start | bytes 786436
  10.1 19.7 %collective-permute-start = (bf16[512,512]{1,0:T(8,128)(2,1)S(1)}, bf16[512,512]{1,0:T(8,128)(2,1)S(1)}, u32[]{:S(2)}, u32[]{:S(2)}) collective-permute-start(bf16[512,512]{1,0:T(8,128)(2,1)S(1)} %pad_maximum_fusion), channel_id=1, source_target_pairs={{0,8},{2,10},{4,12},{6,14},{8,0},{10,2},{12,4},{14,6},{16,24},{18,... | collective-permute-start | bytes 1572872 | tf_op jit(solution)/shard_map/ppermute | solution.py:25
  11.6 0.7 copy-start.10
  13.1 3.7 %copy-start.7 = (bf16[144,256]{1,0:T(8,128)(2,1)S(1)}, bf16[144,256]{1,0:T(8,128)(2,1)}, u32[]{:S(2)}) copy-start(bf16[144,256]{1,0:T(8,128)(2,1)} %get-tuple-element.23) | copy-start | bytes 221188
  16.8 0.7 copy-start.9
  17.5 5.6 %copy-start.2 = (bf16[4,144,256]{2,1,0:T(8,128)(2,1)}, bf16[4,144,256]{2,1,0:T(8,128)(2,1)S(1)}, u32[]{:S(2)}) copy-start(bf16[4,144,256]{2,1,0:T(8,128)(2,1)S(1)} %pad_maximum_fusion.5.refs_4_.refs_8_) | copy-start | bytes 884740
  17.7 3.6 %copy-start.8 = (bf16[128,256]{1,0:T(8,128)(2,1)S(1)}, bf16[128,256]{1,0:T(8,128)(2,1)}, u32[]{:S(2)}) copy-start(bf16[128,256]{1,0:T(8,128)(2,1)} %get-tuple-element.28) | copy-start | bytes 196612
  17.7 15.5 %collective-permute-start.6 = (bf16[4,144,256]{2,1,0:T(8,128)(2,1)S(1)}, bf16[4,144,256]{2,1,0:T(8,128)(2,1)}, u32[]{:S(2)}, u32[]{:S(2)}) collective-permute-start(bf16[4,144,256]{2,1,0:T(8,128)(2,1)S(1)} %pad_maximum_fusion.5.refs_4_.refs_8_), channel_id=1, source_target_pairs={{0,6},{2,4},{4,2},{6,0},{8,14},{10,12},{12,10},{14,8},{16,22},{18,... | collective-permute-start | bytes 884744 | tf_op jit(solution)/shard_map/ppermute | solution.py:25
  20.3 12.9 %collective-permute-start.5 = (bf16[4,144,256]{2,1,0:T(8,128)(2,1)S(1)}, bf16[4,144,256]{2,1,0:T(8,128)(2,1)}, u32[]{:S(2)}, u32[]{:S(2)}) collective-permute-start(bf16[4,144,256]{2,1,0:T(8,128)(2,1)S(1)} %pad_maximum_fusion.5.refs_4_.refs_8_), channel_id=1, source_target_pairs={{0,4},{2,6},{4,0},{6,2},{8,12},{10,14},{12,8},{14,10},{16,20},{18,... | collective-permute-start | bytes 884744 | tf_op jit(solution)/shard_map/ppermute | solution.py:25
  20.8 12.4 %collective-permute-start.4 = (bf16[4,144,256]{2,1,0:T(8,128)(2,1)S(1)}, bf16[4,144,256]{2,1,0:T(8,128)(2,1)}, u32[]{:S(2)}, u32[]{:S(2)}) collective-permute-start(bf16[4,144,256]{2,1,0:T(8,128)(2,1)S(1)} %pad_maximum_fusion.5.refs_4_.refs_8_), channel_id=1, source_target_pairs={{0,2},{2,0},{4,6},{6,4},{8,10},{10,8},{12,14},{14,12},{16,18},{18,... | collective-permute-start | bytes 884744 | tf_op jit(solution)/shard_map/ppermute | solution.py:25
  21.6 7.4 %collective-permute-start.7 = (bf16[2,128,256]{2,1,0:T(8,128)(2,1)S(1)}, bf16[2,128,256]{2,1,0:T(8,128)(2,1)S(1)}, u32[]{:S(2)}, u32[]{:S(2)}) collective-permute-start(bf16[2,128,256]{2,1,0:T(8,128)(2,1)S(1)} %pad_maximum_fusion.7), channel_id=1, source_target_pairs={{0,16},{2,18},{4,20},{6,22},{8,24},{10,26},{12,28},{14,30},{16,0},... | collective-permute-start | bytes 393224 | tf_op jit(solution)/shard_map/ppermute | solution.py:25
  29.0 7.5 %copy-start.3 = (bf16[4,128,256]{2,1,0:T(8,128)(2,1)}, bf16[4,128,256]{2,1,0:T(8,128)(2,1)S(1)}, u32[]{:S(2)}) copy-start(bf16[4,128,256]{2,1,0:T(8,128)(2,1)S(1)} %pad_maximum_fusion.6.refs_4_) | copy-start | bytes 786436
  33.2 11.6 %collective-permute-start.10 = (bf16[4,128,256]{2,1,0:T(8,128)(2,1)S(1)}, bf16[4,128,256]{2,1,0:T(8,128)(2,1)S(1)}, u32[]{:S(2)}, u32[]{:S(2)}) collective-permute-start(bf16[4,128,256]{2,1,0:T(8,128)(2,1)S(1)} %pad_maximum_fusion.6.refs_4_), channel_id=1, source_target_pairs={{0,6},{2,4},{4,2},{6,0},{8,14},{10,12},{12,10},{14,8},{16,22},{18,... | collective-permute-start | bytes 786440 | tf_op jit(solution)/shard_map/ppermute | solution.py:25
  35.9 11.3 %collective-permute-start.9 = (bf16[4,128,256]{2,1,0:T(8,128)(2,1)S(1)}, bf16[4,128,256]{2,1,0:T(8,128)(2,1)S(1)}, u32[]{:S(2)}, u32[]{:S(2)}) collective-permute-start(bf16[4,128,256]{2,1,0:T(8,128)(2,1)S(1)} %pad_maximum_fusion.6.refs_4_), channel_id=1, source_target_pairs={{0,4},{2,6},{4,0},{6,2},{8,12},{10,14},{12,8},{14,10},{16,20},{18,... | collective-permute-start | bytes 786440 | tf_op jit(solution)/shard_map/ppermute | solution.py:25
  36.4 11.1 %collective-permute-start.8 = (bf16[4,128,256]{2,1,0:T(8,128)(2,1)S(1)}, bf16[4,128,256]{2,1,0:T(8,128)(2,1)S(1)}, u32[]{:S(2)}, u32[]{:S(2)}) collective-permute-start(bf16[4,128,256]{2,1,0:T(8,128)(2,1)S(1)} %pad_maximum_fusion.6.refs_4_), channel_id=1, source_target_pairs={{0,2},{2,0},{4,6},{6,4},{8,10},{10,8},{12,14},{14,12},{16,18},{18,... | collective-permute-start | bytes 786440 | tf_op jit(solution)/shard_map/ppermute | solution.py:25
  43.9 11.5 %collective-permute-start.11 = (bf16[2,256,256]{2,1,0:T(8,128)(2,1)}, bf16[2,256,256]{2,1,0:T(8,128)(2,1)S(1)}, u32[]{:S(2)}, u32[]{:S(2)}) collective-permute-start(bf16[2,256,256]{2,1,0:T(8,128)(2,1)} %get-tuple-element.34), channel_id=1, source_target_pairs={{0,8},{2,10},{4,12},{6,14},{8,0},{10,2},{12,4},{14,6},{16,24},{18,... | collective-permute-start | bytes 786440 | tf_op jit(solution)/shard_map/ppermute | solution.py:25
  44.8 2.7 %copy-start.11 = (bf16[4,128,256]{2,1,0:T(8,128)(2,1)}, bf16[4,128,256]{2,1,0:T(8,128)(2,1)S(1)}, u32[]{:S(2)}) copy-start(bf16[4,128,256]{2,1,0:T(8,128)(2,1)S(1)} %collective-permute-done.10.refs_7_) | copy-start | bytes 786436
  47.3 0.7 copy-start.12
  47.6 0.7 copy-start.13
  55.5 1.8 %collective-permute-start.13 = (bf16[4,4,16,512]{3,2,1,0:T(8,128)(2,1)}, bf16[4,4,16,512]{3,2,1,0:T(8,128)(2,1)S(1)}, u32[]{:S(2)}, u32[]{:S(2)}) collective-permute-start(bf16[4,4,16,512]{3,2,1,0:T(8,128)(2,1)} %bitcast.61), channel_id=1, source_target_pairs={{0,1},{1,0},{2,3},{3,2},{4,5},{5,4},{6,7},{7,6},{8,9},{9,8},{10,11... | collective-permute-start | bytes 786440 | tf_op jit(solution)/shard_map/ppermute | solution.py:25
  55.6 8.9 %collective-permute-start.12 = (bf16[2,256,256]{2,1,0:T(8,128)(2,1)}, bf16[2,256,256]{2,1,0:T(8,128)(2,1)S(1)}, u32[]{:S(2)}, u32[]{:S(2)}) collective-permute-start(bf16[2,256,256]{2,1,0:T(8,128)(2,1)} %get-tuple-element.35), channel_id=1, source_target_pairs={{0,8},{2,10},{4,12},{6,14},{8,0},{10,2},{12,4},{14,6},{16,24},{18,... | collective-permute-start | bytes 786440 | tf_op jit(solution)/shard_map/ppermute | solution.py:25
  58.4 6.0 %collective-permute-start.14 = (bf16[4,16,512]{2,1,0:T(8,128)(2,1)S(1)}, bf16[4,16,512]{2,1,0:T(8,128)(2,1)S(1)}, u32[]{:S(2)}, u32[]{:S(2)}) collective-permute-start(bf16[4,16,512]{2,1,0:T(8,128)(2,1)S(1)} %get-tuple-element.53), channel_id=1, source_target_pairs={{0,2},{2,0},{4,6},{6,4},{8,10},{10,8},{12,14},{14,12},{16,18},{18,... | collective-permute-start | bytes 196616 | tf_op jit(solution)/shard_map/ppermute | solution.py:25
  60.0 5.7 %collective-permute-start.15 = (bf16[4,16,512]{2,1,0:T(8,128)(2,1)S(1)}, bf16[4,16,512]{2,1,0:T(8,128)(2,1)S(1)}, u32[]{:S(2)}, u32[]{:S(2)}) collective-permute-start(bf16[4,16,512]{2,1,0:T(8,128)(2,1)S(1)} %get-tuple-element.51), channel_id=1, source_target_pairs={{0,4},{2,6},{4,0},{6,2},{8,12},{10,14},{12,8},{14,10},{16,20},{18,... | collective-permute-start | bytes 196616 | tf_op jit(solution)/shard_map/ppermute | solution.py:25
  60.8 3.7 %copy-start.14 = (bf16[256,256]{1,0:T(8,128)(2,1)S(1)}, bf16[256,256]{1,0:T(8,128)(2,1)}, u32[]{:S(2)}) copy-start(bf16[256,256]{1,0:T(8,128)(2,1)} %get-tuple-element.41) | copy-start | bytes 393220
  60.8 3.7 %copy-start.15 = (bf16[256,256]{1,0:T(8,128)(2,1)S(1)}, bf16[256,256]{1,0:T(8,128)(2,1)}, u32[]{:S(2)}) copy-start(bf16[256,256]{1,0:T(8,128)(2,1)} %get-tuple-element.40) | copy-start | bytes 393220
  60.8 5.2 %collective-permute-start.16 = (bf16[4,16,512]{2,1,0:T(8,128)(2,1)S(1)}, bf16[4,16,512]{2,1,0:T(8,128)(2,1)S(1)}, u32[]{:S(2)}, u32[]{:S(2)}) collective-permute-start(bf16[4,16,512]{2,1,0:T(8,128)(2,1)S(1)} %get-tuple-element.52), channel_id=1, source_target_pairs={{0,6},{2,4},{4,2},{6,0},{8,14},{10,12},{12,10},{14,8},{16,22},{18,... | collective-permute-start | bytes 196616 | tf_op jit(solution)/shard_map/ppermute | solution.py:25
  66.0 3.9 %copy-start.5 = (bf16[256,256]{1,0:T(8,128)(2,1)S(1)}, bf16[256,256]{1,0:T(8,128)(2,1)}, u32[]{:S(2)}) copy-start(bf16[256,256]{1,0:T(8,128)(2,1)} %get-tuple-element.27) | copy-start | bytes 393220
  66.0 3.9 %copy-start.6 = (bf16[256,256]{1,0:T(8,128)(2,1)S(1)}, bf16[256,256]{1,0:T(8,128)(2,1)}, u32[]{:S(2)}) copy-start(bf16[256,256]{1,0:T(8,128)(2,1)} %get-tuple-element.33) | copy-start | bytes 393220
  66.0 4.8 %collective-permute-start.17 = (bf16[16,512]{1,0:T(8,128)(2,1)S(1)}, bf16[16,512]{1,0:T(8,128)(2,1)S(1)}, u32[]{:S(2)}, u32[]{:S(2)}) collective-permute-start(bf16[16,512]{1,0:T(8,128)(2,1)S(1)} %get-tuple-element.58), channel_id=1, source_target_pairs={{0,16},{2,18},{4,20},{6,22},{8,24},{10,26},{12,28},{14,30},{16,0},... | collective-permute-start | bytes 49160 | tf_op jit(solution)/shard_map/ppermute | solution.py:25
  68.4 5.5 %collective-permute-start.19 = (bf16[16,512]{1,0:T(8,128)(2,1)S(1)}, bf16[16,512]{1,0:T(8,128)(2,1)S(1)}, u32[]{:S(2)}, u32[]{:S(2)}) collective-permute-start(bf16[16,512]{1,0:T(8,128)(2,1)S(1)} %get-tuple-element.59), channel_id=1, source_target_pairs={{0,24},{2,26},{4,28},{6,30},{8,16},{10,18},{12,20},{14,22},{16,8},... | collective-permute-start | bytes 49160 | tf_op jit(solution)/shard_map/ppermute | solution.py:25
  69.4 4.5 %collective-permute-start.18 = (bf16[16,512]{1,0:T(8,128)(2,1)S(1)}, bf16[16,512]{1,0:T(8,128)(2,1)S(1)}, u32[]{:S(2)}, u32[]{:S(2)}) collective-permute-start(bf16[16,512]{1,0:T(8,128)(2,1)S(1)} %get-tuple-element.60), channel_id=1, source_target_pairs={{0,8},{2,10},{4,12},{6,14},{8,0},{10,2},{12,4},{14,6},{16,24},{18,... | collective-permute-start | bytes 49160 | tf_op jit(solution)/shard_map/ppermute | solution.py:25

commit v4 on v3

--- a/solution.py
+++ b/solution.py
@@ -15,7 +15,6 @@
 DEAD = -1e30
 VMEM_LIMIT = 60 * 1024 * 1024
 CUT = 2
-STEP = 256
 F32 = jnp.float32
 BF16 = jnp.bfloat16
 
@@ -81,10 +80,11 @@
 
 
 def attend_kernel(pieces, fine_width, scale, *refs):
-    query_ref, grad_ref, bias_ref, ordered_ref = refs[:4]
-    piece_refs = refs[4 : 4 + 2 * pieces]
+    bias_ref = refs[0]
+    inputs = (refs[1:4], refs[4:7])
+    piece_refs = refs[7 : 7 + pieces]
     out_ref, dq_ref, away_ref, keep_ref, send_ref = refs[-5:]
-    head_dim = query_ref.shape[1]
+    head_dim = out_ref.shape[1]
     keys = jnp.concatenate(
         [r[:, :, :head_dim].reshape(-1, head_dim) for r in piece_refs], axis=0
     )
@@ -93,55 +93,50 @@
     )
     bias = bias_ref[0]
     cols = (slice(0, fine_width), slice(fine_width, keys.shape[0]))
-    rows = out_ref.shape[0]
-    step = min(STEP, rows)
     contract = (((1,), (1,)), ((), ()))
-    d_queries = []
-    places = ((out_ref, dq_ref, 0), (away_ref.at[0], away_ref.at[1], rows))
-    for out_part, dq_part, base in places:
-        for low in range(0, rows, step):
-            query = query_ref[base + low : base + low + step, :]
-            grad = grad_ref[base + low : base + low + step, :]
-            scores = lax.dot_general(query, keys, contract, preferred_element_type=F32) * scale + bias
-            d_probs = lax.dot_general(grad, values, contract, preferred_element_type=F32)
-            probs_parts = []
-            d_parts = []
-            for part in cols:
-                score = scores[:, part]
-                expo = jnp.exp(score - jnp.max(score, axis=1, keepdims=True))
-                probs = expo * (1.0 / jnp.sum(expo, axis=1, keepdims=True))
-                d_prob = d_probs[:, part]
-                delta = jnp.sum(probs * d_prob, axis=1, keepdims=True)
-                probs_parts.append(probs.astype(BF16))
-                d_parts.append((probs * (d_prob - delta)).astype(BF16))
-            out = jnp.dot(jnp.concatenate(probs_parts, axis=1), values, preferred_element_type=F32)
-            d_query = jnp.dot(jnp.concatenate(d_parts, axis=1), keys, preferred_element_type=F32)
-            d_query = (d_query * scale).astype(BF16)
-            out_part[low : low + step, :] = out.astype(BF16)
-            dq_part[low : low + step, :] = d_query
-            d_queries.append(d_query)
-    weight = jnp.dot(
-        ordered_ref[...], jnp.concatenate(d_queries, axis=0), preferred_element_type=F32
-    )
+    weight = 0.0
+    places = ((out_ref, dq_ref), (away_ref.at[0], away_ref.at[1]))
+    for (query_ref, grad_ref, ordered_ref), (out_part, dq_part) in zip(inputs, places):
+        scores = lax.dot_general(query_ref[...], keys, contract, preferred_element_type=F32)
+        scores = scores * scale + bias
+        d_probs = lax.dot_general(grad_ref[...], values, contract, preferred_element_type=F32)
+        probs_parts = []
+        d_parts = []
+        for part in cols:
+            score = scores[:, part]
+            expo = jnp.exp(score - jnp.max(score, axis=1, keepdims=True))
+            probs = expo * (1.0 / jnp.sum(expo, axis=1, keepdims=True))
+            d_prob = d_probs[:, part]
+            delta = jnp.sum(probs * d_prob, axis=1, keepdims=True)
+            probs_parts.append(probs.astype(BF16))
+            d_parts.append((probs * (d_prob - delta)).astype(BF16))
+        out = jnp.dot(jnp.concatenate(probs_parts, axis=1), values, preferred_element_type=F32)
+        d_query = jnp.dot(jnp.concatenate(d_parts, axis=1), keys, preferred_element_type=F32)
+        d_query = (d_query * scale).astype(BF16)
+        out_part[...] = out.astype(BF16)
+        dq_part[...] = d_query
+        weight = weight + jnp.dot(ordered_ref[...], d_query, preferred_element_type=F32)
     kept = keep_ref.shape[0]
     keep_ref[...] = weight[:kept]
     send_ref[...] = weight[kept:].astype(BF16)
 
 
-def attend(first, count, query, grad, bias, ordered, summaries, pieces, share, earlier):
-    rows, width = query.shape
+def attend(first, count, bias, own_side, their_side, summaries, pieces, share, earlier):
+    rows = own_side[0].shape[0]
+    depth = own_side[2].shape[0]
     half = bias.shape[0]
+    width = own_side[0].shape[1]
     head_dim = width // half
     fine_width = sum(p.shape[0] for p in pieces) * BLK
     room = (bias.shape[-1] - fine_width) // sum(p.shape[0] for p in pieces)
-    depth = ordered.shape[0]
     kept = depth // share
-    in_specs = [
-        pl.BlockSpec((rows, head_dim), lambda i: (0, first + i)),
-        pl.BlockSpec((rows, head_dim), lambda i: (0, first + i)),
-        pl.BlockSpec((1,) + bias.shape[1:], lambda i: (first + i, 0, 0)),
-        pl.BlockSpec(ordered.shape, lambda i: (0, 0)),
-    ]
+    in_specs = [pl.BlockSpec((1,) + bias.shape[1:], lambda i: (first + i, 0, 0))]
+    for at in (0, own_side[1].shape[0] // rows - 1), (0, their_side[1].shape[0] // rows - 1):
+        in_specs += [
+            pl.BlockSpec((rows, head_dim), lambda i, at=at[0]: (at, first + i)),
+            pl.BlockSpec((rows, head_dim), lambda i, at=at[1]: (at, first + i)),
+            pl.BlockSpec((depth, rows), lambda i: (0, 0)),
+        ]
     in_specs += [
         pl.BlockSpec((p.shape[0], BLK, 2 * head_dim), lambda i: (0, i, 0)) for p in pieces
     ]
@@ -149,23 +144,23 @@
         pl.BlockSpec((p.shape[0], room, 2 * head_dim), lambda i: (0, CUT * BLK // room, 0))
         for p in summaries
     ]
-    args = [query, grad, bias, ordered, *pieces, *summaries]
+    args = [bias, *own_side, *their_side, *pieces, *summaries]
     aliases = {}
     if earlier is not None:
         aliases = {len(args) + i: 3 + i for i in range(len(earlier))}
         args += list(earlier)
         in_specs += [pl.BlockSpec(memory_space=pl.ANY)] * len(earlier)
-    own = jax.ShapeDtypeStruct((rows // PAIR, count * head_dim), BF16)
-    own_spec = pl.BlockSpec((rows // PAIR, head_dim), lambda i: (0, i))
+    own = jax.ShapeDtypeStruct((rows, count * head_dim), BF16)
+    own_spec = pl.BlockSpec((rows, head_dim), lambda i: (0, i))
     columns = bias.shape[-1]
     return pl.pallas_call(
-        functools.partial(attend_kernel, len(pieces), fine_width, head_dim ** (-0.5)),
+        functools.partial(attend_kernel, len(pieces) + len(summaries), fine_width, head_dim ** (-0.5)),
         grid=(count,),
         in_specs=in_specs,
         out_specs=(
             own_spec,
             own_spec,
-            pl.BlockSpec((2, rows // PAIR, head_dim), lambda i: (0, 0, i)),
+            pl.BlockSpec((2, rows, head_dim), lambda i: (0, 0, i)),
             pl.BlockSpec((kept, head_dim), lambda i: (0, first + i)),
             pl.BlockSpec((depth - kept, head_dim), lambda i: (0, first + i)),
         ),
@@ -179,9 +174,9 @@
         input_output_aliases=aliases,
         compiler_params=pltpu.CompilerParams(vmem_limit_bytes=VMEM_LIMIT),
         cost_estimate=pl.CostEstimate(
-            flops=8 * count * rows * columns * head_dim,
+            flops=16 * count * rows * columns * head_dim,
             bytes_accessed=count * (columns * 512 + rows * head_dim * 8),
-            transcendentals=count * rows * columns,
+            transcendentals=2 * count * rows * columns,
         ),
         name="attend",
     )(*args)
@@ -243,15 +238,14 @@
     grad_keep = lax.dynamic_slice_in_dim(grad, side * wide, wide, 1)
     grad_send = lax.dynamic_slice_in_dim(grad, (1 - side) * wide, wide, 1)
     theirs = swap(jnp.concatenate([targets[0], grad_send]), "hist", QUAD)
-    their_targets, their_grads = theirs[:rows], theirs[rows:]
-    both_targets = jnp.concatenate([targets[0], their_targets], axis=0)
-    both_grads = jnp.concatenate([grad_keep, their_grads], axis=0)
     weights = lax.dynamic_slice_in_dim(w_query, side * wide, wide, 1)
-    query = jnp.dot(both_targets, weights, preferred_element_type=F32).astype(BF16)
+
+    def project(part):
+        return jnp.dot(part, weights, preferred_element_type=F32).astype(BF16)
 
     masks = jnp.asarray([q + QUAD * k for q in range(QUAD) for k in range(n_hist // QUAD)], jnp.int32)
     source = rank ^ masks
-    lists = lax.dynamic_slice_in_dim(after(blocks, column_near)[0], side * half, half, 0)
+    lists = lax.dynamic_slice_in_dim(blocks[0], side * half, half, 0)
     listed = jnp.max(
         jnp.where((lists // blk_dev)[:, :, None] == source[None, None, :], lists[:, :, None], -1),
         axis=1,
@@ -264,6 +258,7 @@
     own_line = (line // blk_dev)[None, :] == jnp.arange(half, dtype=jnp.int32)[:, None]
     coarse_live = own_line[:, None, :] & (names * BLK < lengths[0])[None]
     coarse_bias = jnp.where(coarse_live, 0.0, DEAD).astype(F32).reshape(half, -1)
+    fine_bias = after(fine_bias, column_near)
     bias = jnp.concatenate([fine_bias, coarse_bias], axis=1)[:, None, :]
 
     places = (
@@ -272,12 +267,17 @@
     share = depth // (n_hist * n_batch)
     chosen = (places[:, None] * share + jnp.arange(share, dtype=jnp.int32)).reshape(-1)
     shuffle = (chosen[:, None] == jnp.arange(depth, dtype=jnp.int32)[None, :]).astype(BF16)
-    ordered = lax.dot_general(
-        shuffle, both_targets, (((1,), (1,)), ((), ())), preferred_element_type=F32
-    ).astype(BF16)
-
-    late = gather_quad(after(column_late, (near[1:], query, ordered, both_grads, bias)))
-    fixed = (query, both_grads, bias, ordered, near)
+
+    def reorder(part):
+        product = lax.dot_general(
+            shuffle, part, (((1,), (1,)), ((), ())), preferred_element_type=F32
+        )
+        return product.astype(BF16)
+
+    own_side = (project(targets[0]), grad_keep, reorder(targets[0]))
+    their_side = (project(theirs[:rows]), theirs, reorder(theirs[:rows]))
+    late = gather_quad(after(column_late, theirs))
+    fixed = (bias, own_side, their_side, near)
     out_near, dq_near, away_near, *weight = attend(0, CUT, *fixed, near, n_batch, None)
     out_late, dq_late, away_late, kept, sent = attend(
         CUT, half - CUT, *fixed, late, n_batch, weight

time: 74.9 us -> 73 us (0.975)
  waiting for transfers between devices: 19 us -> 14.2 us
  starting transfers between devices: 25 us -> 26.7 us
  matrix products: 3.75 us -> 5.33 us
  other arithmetic: 4 us -> 3.18 us
    ppermute x20, waiting for transfers between devices: 19 us -> 14.2 us  [swap(): return lax.ppermute(array, axis, [(i, i ^ mask) for i in range(size)])]
    ppermute x20, starting transfers between devices: 25 us -> 26.7 us  [swap(): return lax.ppermute(array, axis, [(i, i ^ mask) for i in range(size)])]
    dot_general x2 -> x4, matrix products: 2.54 us -> 4.13 us  [the longest x2 2.12 us: reorder(): lax.dot_general(shuffle, part, (((1,), (1,)), ((), ())), preferred_elemen...]
    concatenate x1 -> x0, other arithmetic: 0.82 us -> none  [shards(): both_grads = jnp.concatenate([grad_keep, their_grads], axis=0)]
    unnamed x32 -> x40, local copies, waits for them, and re-layouts: 2.95 us -> 2.65 us
  transfers between devices with their start and end apart: 20 -> 20, of which waited for: 9 -> 7; matrix products, arithmetic and copies ran while one was open for 12% -> 14% of each run, Pallas kernels for 19% -> 20%
where the time goes in v4:
time: 73 us; the launch traced here: 72.7 us
  starting transfers between devices  26.7 us (37%)
  Pallas kernels  16.4 us (22%)
  waiting for transfers between devices  14.2 us (19%)
  matrix products  5.33 us (7%)
  local copies, waits for them, and re-layouts  5.02 us (7%)
  other arithmetic  3.18 us (4%)
  between operations  1.74 us (2%)
    ppermute x20, starting transfers between devices, swap(): return lax.ppermute(array, axis, [(i, i ^ mask) for i in range(size)])  26.7 us
    pallas_call x2, Pallas kernels, attend(): pl.pallas_call(functools.partial(attend_kernel, len(pieces) + len(summari...  14.4 us
    ppermute x20, waiting for transfers between devices, swap(): return lax.ppermute(array, axis, [(i, i ^ mask) for i in range(size)])  14.2 us
    unnamed x40, local copies, waits for them, and re-layouts  2.65 us
    dot_general x2, matrix products, reorder(): lax.dot_general(shuffle, part, (((1,), (1,)), ((), ())), preferred_elemen...  2.12 us
    pallas_call x1, Pallas kernels, shards(): pl.pallas_call(functools.partial(select_kernel, CUT), in_specs=[pl.BlockS...  2.07 us
    dot_general x2, matrix products, project(): return jnp.dot(part, weights, preferred_element_type=F32).astype(BF16)  2.01 us
  transfers between devices with their start and end apart: 20, of which 7 were waited for; matrix products, arithmetic and copies ran while one was open for 14% of the time, Pallas kernels for 20%

profile of v4, /device:TPU:0, one launch (start us, length us, event | category | flops | bytes accessed | tf_op | source)
XLA Modules:
  0.0 72.7 jit_solution(6032189673719887802)
XLA Ops:
  1.4 2.1 %select.34 = (bf16[144,256]{1,0:T(8,128)(2,1)}, bf16[128,256]{1,0:T(8,128)(2,1)}, bf16[144,256]{1,0:T(8,128)(2,1)}, bf16[272,256]{1,0:T(8,128)(2,1)}) custom-call(s32[1,8,16]{2,1,0:T(8,128)} %blocks_ref.1, s32[1]{0:T(128)} %copy.19.lengths_ref, bf16[1,128,1024]{2,1,0:T(8,128)(2,1)} %keys_ref.1, bf16[1,128,1024]{2,1,0:T(8,128)(2,1)} %values_ref.1), custom_call_target="tpu_custom_call" | custom-call | tf_op jit(solution)/shard_map/select/pallas_call | solution.py:207
  3.5 5.0 %collective-permute-start.2 = (bf16[144,256]{1,0:T(8,128)(2,1)}, bf16[144,256]{1,0:T(8,128)(2,1)S(1)}, u32[]{:S(2)}, u32[]{:S(2)}) collective-permute-start(bf16[144,256]{1,0:T(8,128)(2,1)} %get-tuple-element.25), channel_id=1, source_target_pairs={{0,24},{2,26},{4,28},{6,30},{8,16},{10,18},{12,20},{14,22},{16,8},... | collective-permute-start | bytes 221192 | tf_op jit(solution)/shard_map/ppermute | solution.py:24
  8.5 0.6 collective-permute-start
  9.1 0.7 %dynamic-slice_bitcast_fusion = (bf16[256,512]{1,0:T(8,128)(2,1)S(1)}, bf16[256,512]{1,0:T(8,128)(2,1)}) fusion(bf16[1,256,1024]{2,1,0:T(8,128)(2,1)S(1)} %copy-done.2, s32[]{:T(128)S(6)} %select_n.104, s32[]{:T(128)S(6)} %select_n.103), kind=kLoop, calls=%fused_computation.31 | loop fusion | bytes 1048584 | tf_op jit(solution)/shard_map/dynamic_slice | solution.py:239
  9.9 0.3 copy-done.1
  10.2 1.5 %collective-permute-start.3 = (bf16[512,512]{1,0:T(8,128)(2,1)S(1)}, bf16[512,512]{1,0:T(8,128)(2,1)S(1)}, u32[]{:S(2)}, u32[]{:S(2)}) collective-permute-start(bf16[512,512]{1,0:T(8,128)(2,1)S(1)} %pad_maximum_fusion), channel_id=1, source_target_pairs={{0,8},{2,10},{4,12},{6,14},{8,0},{10,2},{12,4},{14,6},{16,24},{18,... | collective-permute-start | bytes 1572872 | tf_op jit(solution)/shard_map/ppermute | solution.py:24
  11.7 0.7 copy-done.10
  12.4 0.1 select_reduce_fusion
  12.5 0.1 broadcast_reduce_fusion
  12.9 0.1 and.82
  13.0 0.1 and.86
  13.6 0.1 add.137
  13.6 1.1 %convolution_convert_fusion.4.refs_3_ = bf16[512,256]{1,0:T(8,128)(2,1)} fusion(s32[512]{0:T(512)S(1)} %add.155, bf16[1,256,512]{2,1,0:T(8,128)(2,1)S(1)} %copy-done.1), kind=kOutput, calls=%fused_computation.4 | convolution fusion | flops 134610944 | bytes 526336 | tf_op jit(solution)/shard_map/dot_general | solution.py:272
  14.7 1.0 %fusion.refs_1_ = bf16[256,512]{1,0:T(8,128)(2,1)} fusion(bf16[512,1024]{1,0:T(8,128)(2,1)S(1)} %copy-done, s32[]{:T(128)S(6)} %select_n.103, bf16[1,256,512]{2,1,0:T(8,128)(2,1)S(1)} %copy-done.1), kind=kOutput, calls=%fused_computation.5 | convolution fusion | flops 134348800 | bytes 1048580 | tf_op jit(solution)/shard_map/dot_general | solution.py:244
  15.8 1.0 %collective-permute-done = bf16[272,256]{1,0:T(8,128)(2,1)S(1)} collective-permute-done((bf16[272,256]{1,0:T(8,128)(2,1)}, bf16[272,256]{1,0:T(8,128)(2,1)S(1)}, u32[]{:S(2)}, u32[]{:S(2)}) %collective-permute-start) | collective-permute-done | bytes 139296 | tf_op jit(solution)/shard_map/ppermute | solution.py:24
  16.9 2.6 %collective-permute-start.6 = (bf16[4,144,256]{2,1,0:T(8,128)(2,1)S(1)}, bf16[4,144,256]{2,1,0:T(8,128)(2,1)S(1)}, u32[]{:S(2)}, u32[]{:S(2)}) collective-permute-start(bf16[4,144,256]{2,1,0:T(8,128)(2,1)S(1)} %pad_maximum_fusion.1.refs_7_.refs_11_), channel_id=1, source_target_pairs={{0,6},{2,4},{4,2},{6,0},{8,14},{10,12},{12,10},{14,8},{16,22},{18,... | collective-permute-start | bytes 884744 | tf_op jit(solution)/shard_map/ppermute | solution.py:24
  19.5 0.5 collective-permute-start.5
  20.0 0.4 collective-permute-start.4
  20.5 2.8 %collective-permute-start.7 = (bf16[2,128,256]{2,1,0:T(8,128)(2,1)S(1)}, bf16[2,128,256]{2,1,0:T(8,128)(2,1)S(1)}, u32[]{:S(2)}, u32[]{:S(2)}) collective-permute-start(bf16[2,128,256]{2,1,0:T(8,128)(2,1)S(1)} %pad_maximum_fusion.3), channel_id=1, source_target_pairs={{0,16},{2,18},{4,20},{6,22},{8,24},{10,26},{12,28},{14,30},{16,0},... | collective-permute-start | bytes 393224 | tf_op jit(solution)/shard_map/ppermute | solution.py:24
  23.3 0.6 broadcast_in_dim.57.refs_0_
  23.9 5.0 %collective-permute-done.7 = bf16[2,128,256]{2,1,0:T(8,128)(2,1)S(1)} collective-permute-done((bf16[2,128,256]{2,1,0:T(8,128)(2,1)S(1)}, bf16[2,128,256]{2,1,0:T(8,128)(2,1)S(1)}, u32[]{:S(2)}, u32[]{:S(2)}) %collective-permute-start.7) | collective-permute-done | bytes 131104 | tf_op jit(solution)/shard_map/ppermute | solution.py:24
  29.0 0.8 %collective-permute-done.3.refs_5_ = bf16[512,512]{1,0:T(8,128)(2,1)S(1)} collective-permute-done((bf16[512,512]{1,0:T(8,128)(2,1)S(1)}, bf16[512,512]{1,0:T(8,128)(2,1)S(1)}, u32[]{:S(2)}, u32[]{:S(2)}) %collective-permute-start.3) | collective-permute-done | bytes 524320 | tf_op jit(solution)/shard_map/ppermute | solution.py:24
  29.8 2.6 %collective-permute-start.10 = (bf16[4,128,256]{2,1,0:T(8,128)(2,1)S(1)}, bf16[4,128,256]{2,1,0:T(8,128)(2,1)S(1)}, u32[]{:S(2)}, u32[]{:S(2)}) collective-permute-start(bf16[4,128,256]{2,1,0:T(8,128)(2,1)S(1)} %pad_maximum_fusion.2.refs_7_), channel_id=1, source_target_pairs={{0,6},{2,4},{4,2},{6,0},{8,14},{10,12},{12,10},{14,8},{16,22},{18,... | collective-permute-start | bytes 786440 | tf_op jit(solution)/shard_map/ppermute | solution.py:24
  32.4 0.5 collective-permute-start.9
  32.9 1.0 %convolution_convert_fusion.3.refs_4_ = bf16[256,512]{1,0:T(8,128)(2,1)} fusion(bf16[512,1024]{1,0:T(8,128)(2,1)S(1)} %copy-done, s32[]{:T(128)S(6)} %select_n.103, bf16[512,512]{1,0:T(8,128)(2,1)S(1)} %collective-permute-done.3.refs_5_), kind=kOutput, calls=%fused_computation.3 | convolution fusion | flops 134348800 | bytes 1048580 | tf_op jit(solution)/shard_map/dot_general | solution.py:244
  34.0 1.0 %convolution_convert_fusion.2.refs_6_ = bf16[512,256]{1,0:T(8,128)(2,1)} fusion(s32[512]{0:T(512)S(1)} %add.155, bf16[512,512]{1,0:T(8,128)(2,1)S(1)} %collective-permute-done.3.refs_5_), kind=kOutput, calls=%fused_computation.2 | convolution fusion | flops 134610944 | bytes 526336 | tf_op jit(solution)/shard_map/dot_general | solution.py:272
  35.0 0.4 collective-permute-start.8
  35.4 0.7 copy-done.14
  36.2 7.2 %attend.2 = (bf16[256,256]{1,0:T(8,128)(2,1)}, bf16[256,256]{1,0:T(8,128)(2,1)}, bf16[2,256,256]{2,1,0:T(8,128)(2,1)}, f32[256,512]{1,0:T(8,128)}, bf16[256,512]{1,0:T(8,128)(2,1)}) custom-call(f32[4,1,1280]{2,1,0:T(1,128)} %broadcast_in_dim.57.refs_0_, bf16[256,512]{1,0:T(8,128)(2,1)} %fusion.refs_1_, bf16[256,512]{1,0:T(8,128)(2,1)} %get-tuple-element.48.refs_2_, ...), custom_call_target="tpu_custom_call" | custom-call | flops 1342177280 | bytes 1835008 | tf_op jit(solution)/shard_map/attend/pallas_call | solution.py:156
  43.4 1.0 %collective-permute-start.11 = (bf16[2,256,256]{2,1,0:T(8,128)(2,1)}, bf16[2,256,256]{2,1,0:T(8,128)(2,1)S(1)}, u32[]{:S(2)}, u32[]{:S(2)}) collective-permute-start(bf16[2,256,256]{2,1,0:T(8,128)(2,1)} %get-tuple-element.34), channel_id=1, source_target_pairs={{0,8},{2,10},{4,12},{6,14},{8,0},{10,2},{12,4},{14,6},{16,24},{18,... | collective-permute-start | bytes 786440 | tf_op jit(solution)/shard_map/ppermute | solution.py:24
  44.4 0.7 copy-done.15
  45.1 0.1 copy-done.16
  45.3 7.2 %attend.3 = (bf16[256,256]{1,0:T(8,128)(2,1)}, bf16[256,256]{1,0:T(8,128)(2,1)}, bf16[2,256,256]{2,1,0:T(8,128)(2,1)}, f32[256,512]{1,0:T(8,128)}, bf16[256,512]{1,0:T(8,128)(2,1)}) custom-call(f32[4,1,1280]{2,1,0:T(1,128)} %broadcast_in_dim.57.refs_0_, bf16[256,512]{1,0:T(8,128)(2,1)} %fusion.refs_1_, ...), custom_call_target="tpu_custom_call", output_to_operand_aliasing={{3}: (15, {}), {4}: (16, {})} | custom-call | flops 1342177280 | bytes 1835008 | tf_op jit(solution)/shard_map/attend/pallas_call | solution.py:156
  52.6 1.2 %collective-permute-start.12 = (bf16[2,256,256]{2,1,0:T(8,128)(2,1)}, bf16[2,256,256]{2,1,0:T(8,128)(2,1)S(1)}, u32[]{:S(2)}, u32[]{:S(2)}) collective-permute-start(bf16[2,256,256]{2,1,0:T(8,128)(2,1)} %get-tuple-element.35), channel_id=1, source_target_pairs={{0,8},{2,10},{4,12},{6,14},{8,0},{10,2},{12,4},{14,6},{16,24},{18,... | collective-permute-start | bytes 786440 | tf_op jit(solution)/shard_map/ppermute | solution.py:24
  53.8 0.6 collective-permute-done.13
  54.3 1.1 %fusion.33 = (bf16[4,4,16,512]{3,2,1,0:T(8,128)(2,1)S(1)}, f32[4,4,16,512]{3,2,1,0:T(8,128)S(1)}) fusion(f32[4,4,16,512]{3,2,1,0:T(8,128)} %bitcast.58, bf16[4,4,16,512]{3,2,1,0:T(8,128)(2,1)S(1)} %collective-permute-done.13), kind=kLoop, calls=%fused_computation.87 | loop fusion | flops 393216 | bytes 1572864 | tf_op jit(solution)/shard_map/convert.5
  55.5 1.6 %collective-permute-start.14 = (bf16[4,16,512]{2,1,0:T(8,128)(2,1)S(1)}, bf16[4,16,512]{2,1,0:T(8,128)(2,1)S(1)}, u32[]{:S(2)}, u32[]{:S(2)}) collective-permute-start(bf16[4,16,512]{2,1,0:T(8,128)(2,1)S(1)} %get-tuple-element.51), channel_id=1, source_target_pairs={{0,2},{2,0},{4,6},{6,4},{8,10},{10,8},{12,14},{14,12},{16,18},{18,... | collective-permute-start | bytes 196616 | tf_op jit(solution)/shard_map/ppermute | solution.py:24
  57.0 1.6 %collective-permute-start.15 = (bf16[4,16,512]{2,1,0:T(8,128)(2,1)S(1)}, bf16[4,16,512]{2,1,0:T(8,128)(2,1)S(1)}, u32[]{:S(2)}, u32[]{:S(2)}) collective-permute-start(bf16[4,16,512]{2,1,0:T(8,128)(2,1)S(1)} %get-tuple-element.49), channel_id=1, source_target_pairs={{0,4},{2,6},{4,0},{6,2},{8,12},{10,14},{12,8},{14,10},{16,20},{18,... | collective-permute-start | bytes 196616 | tf_op jit(solution)/shard_map/ppermute | solution.py:24
  58.6 0.5 collective-permute-start.16
  59.1 2.4 %collective-permute-done.12 = bf16[2,256,256]{2,1,0:T(8,128)(2,1)S(1)} collective-permute-done((bf16[2,256,256]{2,1,0:T(8,128)(2,1)}, bf16[2,256,256]{2,1,0:T(8,128)(2,1)S(1)}, u32[]{:S(2)}, u32[]{:S(2)}) %collective-permute-start.12) | collective-permute-done | bytes 262176 | tf_op jit(solution)/shard_map/ppermute | solution.py:24
  61.6 1.2 %convolution_convert_fusion.1 = bf16[256,512]{1,0:T(8,128)(2,1)} fusion(bf16[512,1024]{1,0:T(8,128)(2,1)S(1)} %copy-done, bf16[256,256]{1,0:T(8,128)(2,1)S(1)} %get-tuple-element.54, bf16[256,256]{1,0:T(8,128)(2,1)S(1)} %get-tuple-element.52, bf16[256,256]{1,0:T(8,128)(2,1)S(1)} %copy-done.18, bf16[256,256]{1,0:T(8,128)(2,1)S(1)} %copy-done.19, pred[]{:T(512)S(6)} %eq.52), kind=kOutput, calls=%fused_computation.1 | convolution fusion | flops 273022976 | bytes 1835009 | tf_op jit(solution)/shard_map/dot_general | solution.py:308
  62.8 1.0 %collective-permute-done.16 = bf16[4,16,512]{2,1,0:T(8,128)(2,1)S(1)} collective-permute-done((bf16[4,16,512]{2,1,0:T(8,128)(2,1)S(1)}, bf16[4,16,512]{2,1,0:T(8,128)(2,1)S(1)}, u32[]{:S(2)}, u32[]{:S(2)}) %collective-permute-start.16) | collective-permute-done | bytes 65568 | tf_op jit(solution)/shard_map/ppermute | solution.py:24
  63.9 2.6 %collective-permute-start.17 = (bf16[16,512]{1,0:T(8,128)(2,1)S(1)}, bf16[16,512]{1,0:T(8,128)(2,1)S(1)}, u32[]{:S(2)}, u32[]{:S(2)}) collective-permute-start(bf16[16,512]{1,0:T(8,128)(2,1)S(1)} %get-tuple-element.56), channel_id=1, source_target_pairs={{0,16},{2,18},{4,20},{6,22},{8,24},{10,26},{12,28},{14,30},{16,0},... | collective-permute-start | bytes 49160 | tf_op jit(solution)/shard_map/ppermute | solution.py:24
  66.5 1.1 %collective-permute-start.19 = (bf16[16,512]{1,0:T(8,128)(2,1)S(1)}, bf16[16,512]{1,0:T(8,128)(2,1)S(1)}, u32[]{:S(2)}, u32[]{:S(2)}) collective-permute-start(bf16[16,512]{1,0:T(8,128)(2,1)S(1)} %get-tuple-element.57), channel_id=1, source_target_pairs={{0,24},{2,26},{4,28},{6,30},{8,16},{10,18},{12,20},{14,22},{16,8},... | collective-permute-start | bytes 49160 | tf_op jit(solution)/shard_map/ppermute | solution.py:24
  67.6 0.1 collective-permute-start.18
  67.7 0.9 %maximum_select_fusion = bf16[1,256,1024]{2,1,0:T(8,128)(2,1)} fusion(bf16[1,256,256]{2,1,0:T(8,128)(2,1)S(1)} %get-tuple-element.55, bf16[1,256,256]{2,1,0:T(8,128)(2,1)S(1)} %get-tuple-element.53, bf16[1,256,256]{2,1,0:T(8,128)(2,1)S(1)} %bitcast.60, bf16[1,256,256]{2,1,0:T(8,128)(2,1)S(1)} %bitcast.59, pred[]{:T(512)S(6)} %eq.52), kind=kLoop, calls=%fused_computation.8 | loop fusion | flops 4456448 | bytes 1048577 | tf_op jit(solution)/shard_map/jit(_where)/select_n | solution.py:303
  68.7 3.4 %collective-permute-done.19 = bf16[16,512]{1,0:T(8,128)(2,1)S(1)} collective-permute-done((bf16[16,512]{1,0:T(8,128)(2,1)S(1)}, bf16[16,512]{1,0:T(8,128)(2,1)S(1)}, u32[]{:S(2)}, u32[]{:S(2)}) %collective-permute-start.19) | collective-permute-done | bytes 16416 | tf_op jit(solution)/shard_map/ppermute | solution.py:24
  72.1 0.6 maximum_select_fusion.3
  (87 shorter events, 1.3 us)
Async XLA Ops:
  0.6 14.1 %copy-start = (bf16[512,1024]{1,0:T(8,128)(2,1)S(1)}, bf16[512,1024]{1,0:T(8,128)(2,1)}, u32[]{:S(2)}) copy-start(bf16[512,1024]{1,0:T(8,128)(2,1)} %param.9) | copy-start | bytes 3145732
  0.6 8.5 %copy-start.2 = (bf16[1,256,1024]{2,1,0:T(8,128)(2,1)S(1)}, bf16[1,256,1024]{2,1,0:T(8,128)(2,1)}, u32[]{:S(2)}) copy-start(bf16[1,256,1024]{2,1,0:T(8,128)(2,1)} %param.14) | copy-start | bytes 1572868
  3.5 13.3 %collective-permute-start.2 = (bf16[144,256]{1,0:T(8,128)(2,1)}, bf16[144,256]{1,0:T(8,128)(2,1)S(1)}, u32[]{:S(2)}, u32[]{:S(2)}) collective-permute-start(bf16[144,256]{1,0:T(8,128)(2,1)} %get-tuple-element.25), channel_id=1, source_target_pairs={{0,24},{2,26},{4,28},{6,30},{8,16},{10,18},{12,20},{14,22},{16,8},... | collective-permute-start | bytes 221192 | tf_op jit(solution)/shard_map/ppermute | solution.py:24
  8.5 8.3 %collective-permute-start.1 = (bf16[144,256]{1,0:T(8,128)(2,1)}, bf16[144,256]{1,0:T(8,128)(2,1)S(1)}, u32[]{:S(2)}, u32[]{:S(2)}) collective-permute-start(bf16[144,256]{1,0:T(8,128)(2,1)} %get-tuple-element.23), channel_id=1, source_target_pairs={{0,16},{2,18},{4,20},{6,22},{8,24},{10,26},{12,28},{14,30},{16,0},... | collective-permute-start | bytes 221192 | tf_op jit(solution)/shard_map/ppermute | solution.py:24
  8.5 8.2 %collective-permute-start = (bf16[272,256]{1,0:T(8,128)(2,1)}, bf16[272,256]{1,0:T(8,128)(2,1)S(1)}, u32[]{:S(2)}, u32[]{:S(2)}) collective-permute-start(bf16[272,256]{1,0:T(8,128)(2,1)} %get-tuple-element.24), channel_id=1, source_target_pairs={{0,8},{2,10},{4,12},{6,14},{8,0},{10,2},{12,4},{14,6},{16,24},{18,... | collective-permute-start | bytes 417800 | tf_op jit(solution)/shard_map/ppermute | solution.py:24
  9.1 1.0 %copy-start.1 = (bf16[1,256,512]{2,1,0:T(8,128)(2,1)S(1)}, bf16[1,256,512]{2,1,0:T(8,128)(2,1)}, u32[]{:S(2)}) copy-start(bf16[1,256,512]{2,1,0:T(8,128)(2,1)} %param.8) | copy-start | bytes 786436
  10.1 1.6 %copy-start.11 = (s32[16]{0:T(128)S(1)}, s32[16]{0:T(128)}, u32[]{:S(2)}) copy-start(s32[16]{0:T(128)} %constant.93.clone) | copy-start | bytes 196
  10.2 19.6 %collective-permute-start.3 = (bf16[512,512]{1,0:T(8,128)(2,1)S(1)}, bf16[512,512]{1,0:T(8,128)(2,1)S(1)}, u32[]{:S(2)}, u32[]{:S(2)}) collective-permute-start(bf16[512,512]{1,0:T(8,128)(2,1)S(1)} %pad_maximum_fusion), channel_id=1, source_target_pairs={{0,8},{2,10},{4,12},{6,14},{8,0},{10,2},{12,4},{14,6},{16,24},{18,... | collective-permute-start | bytes 1572872 | tf_op jit(solution)/shard_map/ppermute | solution.py:24
  11.7 0.7 copy-start.10
  15.8 1.1 %copy-start.8 = (bf16[144,256]{1,0:T(8,128)(2,1)S(1)}, bf16[144,256]{1,0:T(8,128)(2,1)}, u32[]{:S(2)}) copy-start(bf16[144,256]{1,0:T(8,128)(2,1)} %get-tuple-element.23) | copy-start | bytes 221188
  16.9 12.1 %copy-start.3 = (bf16[4,144,256]{2,1,0:T(8,128)(2,1)}, bf16[4,144,256]{2,1,0:T(8,128)(2,1)S(1)}, u32[]{:S(2)}) copy-start(bf16[4,144,256]{2,1,0:T(8,128)(2,1)S(1)} %pad_maximum_fusion.1.refs_7_.refs_11_) | copy-start | bytes 884740
  16.9 3.6 %copy-start.9 = (bf16[128,256]{1,0:T(8,128)(2,1)S(1)}, bf16[128,256]{1,0:T(8,128)(2,1)}, u32[]{:S(2)}) copy-start(bf16[128,256]{1,0:T(8,128)(2,1)} %get-tuple-element.28) | copy-start | bytes 196612
  16.9 18.1 %collective-permute-start.6 = (bf16[4,144,256]{2,1,0:T(8,128)(2,1)S(1)}, bf16[4,144,256]{2,1,0:T(8,128)(2,1)S(1)}, u32[]{:S(2)}, u32[]{:S(2)}) collective-permute-start(bf16[4,144,256]{2,1,0:T(8,128)(2,1)S(1)} %pad_maximum_fusion.1.refs_7_.refs_11_), channel_id=1, source_target_pairs={{0,6},{2,4},{4,2},{6,0},{8,14},{10,12},{12,10},{14,8},{16,22},{18,... | collective-permute-start | bytes 884744 | tf_op jit(solution)/shard_map/ppermute | solution.py:24
  19.5 15.9 %collective-permute-start.5 = (bf16[4,144,256]{2,1,0:T(8,128)(2,1)S(1)}, bf16[4,144,256]{2,1,0:T(8,128)(2,1)S(1)}, u32[]{:S(2)}, u32[]{:S(2)}) collective-permute-start(bf16[4,144,256]{2,1,0:T(8,128)(2,1)S(1)} %pad_maximum_fusion.1.refs_7_.refs_11_), channel_id=1, source_target_pairs={{0,4},{2,6},{4,0},{6,2},{8,12},{10,14},{12,8},{14,10},{16,20},{18,... | collective-permute-start | bytes 884744 | tf_op jit(solution)/shard_map/ppermute | solution.py:24
  20.0 15.4 %collective-permute-start.4 = (bf16[4,144,256]{2,1,0:T(8,128)(2,1)S(1)}, bf16[4,144,256]{2,1,0:T(8,128)(2,1)S(1)}, u32[]{:S(2)}, u32[]{:S(2)}) collective-permute-start(bf16[4,144,256]{2,1,0:T(8,128)(2,1)S(1)} %pad_maximum_fusion.1.refs_7_.refs_11_), channel_id=1, source_target_pairs={{0,2},{2,0},{4,6},{6,4},{8,10},{10,8},{12,14},{14,12},{16,18},{18,... | collective-permute-start | bytes 884744 | tf_op jit(solution)/shard_map/ppermute | solution.py:24
  20.5 8.4 %collective-permute-start.7 = (bf16[2,128,256]{2,1,0:T(8,128)(2,1)S(1)}, bf16[2,128,256]{2,1,0:T(8,128)(2,1)S(1)}, u32[]{:S(2)}, u32[]{:S(2)}) collective-permute-start(bf16[2,128,256]{2,1,0:T(8,128)(2,1)S(1)} %pad_maximum_fusion.3), channel_id=1, source_target_pairs={{0,16},{2,18},{4,20},{6,22},{8,24},{10,26},{12,28},{14,30},{16,0},... | collective-permute-start | bytes 393224 | tf_op jit(solution)/shard_map/ppermute | solution.py:24
  29.0 6.0 %copy-start.4 = (bf16[4,128,256]{2,1,0:T(8,128)(2,1)}, bf16[4,128,256]{2,1,0:T(8,128)(2,1)S(1)}, u32[]{:S(2)}) copy-start(bf16[4,128,256]{2,1,0:T(8,128)(2,1)S(1)} %pad_maximum_fusion.2.refs_7_) | copy-start | bytes 786436
  29.8 4.2 %copy-start.5 = (bf16[512,512]{1,0:T(8,128)(2,1)}, bf16[512,512]{1,0:T(8,128)(2,1)S(1)}, u32[]{:S(2)}) copy-start(bf16[512,512]{1,0:T(8,128)(2,1)S(1)} %collective-permute-done.3.refs_5_) | copy-start | bytes 1572868
  29.8 14.6 %collective-permute-start.10 = (bf16[4,128,256]{2,1,0:T(8,128)(2,1)S(1)}, bf16[4,128,256]{2,1,0:T(8,128)(2,1)S(1)}, u32[]{:S(2)}, u32[]{:S(2)}) collective-permute-start(bf16[4,128,256]{2,1,0:T(8,128)(2,1)S(1)} %pad_maximum_fusion.2.refs_7_), channel_id=1, source_target_pairs={{0,6},{2,4},{4,2},{6,0},{8,14},{10,12},{12,10},{14,8},{16,22},{18,... | collective-permute-start | bytes 786440 | tf_op jit(solution)/shard_map/ppermute | solution.py:24
  32.4 12.0 %collective-permute-start.9 = (bf16[4,128,256]{2,1,0:T(8,128)(2,1)S(1)}, bf16[4,128,256]{2,1,0:T(8,128)(2,1)S(1)}, u32[]{:S(2)}, u32[]{:S(2)}) collective-permute-start(bf16[4,128,256]{2,1,0:T(8,128)(2,1)S(1)} %pad_maximum_fusion.2.refs_7_), channel_id=1, source_target_pairs={{0,4},{2,6},{4,0},{6,2},{8,12},{10,14},{12,8},{14,10},{16,20},{18,... | collective-permute-start | bytes 786440 | tf_op jit(solution)/shard_map/ppermute | solution.py:24
  35.0 1.2 %copy-start.12 = (bf16[4,144,256]{2,1,0:T(8,128)(2,1)}, bf16[4,144,256]{2,1,0:T(8,128)(2,1)S(1)}, u32[]{:S(2)}) copy-start(bf16[4,144,256]{2,1,0:T(8,128)(2,1)S(1)} %collective-permute-done.6.refs_10_.refs_14_) | copy-start | bytes 884740
  35.0 9.4 %collective-permute-start.8 = (bf16[4,128,256]{2,1,0:T(8,128)(2,1)S(1)}, bf16[4,128,256]{2,1,0:T(8,128)(2,1)S(1)}, u32[]{:S(2)}, u32[]{:S(2)}) collective-permute-start(bf16[4,128,256]{2,1,0:T(8,128)(2,1)S(1)} %pad_maximum_fusion.2.refs_7_), channel_id=1, source_target_pairs={{0,2},{2,0},{4,6},{6,4},{8,10},{10,8},{12,14},{14,12},{16,18},{18,... | collective-permute-start | bytes 786440 | tf_op jit(solution)/shard_map/ppermute | solution.py:24
  35.4 0.8 %copy-start.13 = (bf16[4,144,256]{2,1,0:T(8,128)(2,1)}, bf16[4,144,256]{2,1,0:T(8,128)(2,1)S(1)}, u32[]{:S(2)}) copy-start(bf16[4,144,256]{2,1,0:T(8,128)(2,1)S(1)} %collective-permute-done.5.refs_9_.refs_13_) | copy-start | bytes 884740
  35.4 0.7 %copy-start.14 = (bf16[4,144,256]{2,1,0:T(8,128)(2,1)}, bf16[4,144,256]{2,1,0:T(8,128)(2,1)S(1)}, u32[]{:S(2)}) copy-start(bf16[4,144,256]{2,1,0:T(8,128)(2,1)S(1)} %collective-permute-done.4.refs_8_.refs_12_) | copy-start | bytes 884740
  43.4 9.1 %collective-permute-start.11 = (bf16[2,256,256]{2,1,0:T(8,128)(2,1)}, bf16[2,256,256]{2,1,0:T(8,128)(2,1)S(1)}, u32[]{:S(2)}, u32[]{:S(2)}) collective-permute-start(bf16[2,256,256]{2,1,0:T(8,128)(2,1)} %get-tuple-element.34), channel_id=1, source_target_pairs={{0,8},{2,10},{4,12},{6,14},{8,0},{10,2},{12,4},{14,6},{16,24},{18,... | collective-permute-start | bytes 786440 | tf_op jit(solution)/shard_map/ppermute | solution.py:24
  44.4 0.7 copy-start.15
  44.4 0.8 %copy-start.16 = (bf16[4,128,256]{2,1,0:T(8,128)(2,1)}, bf16[4,128,256]{2,1,0:T(8,128)(2,1)S(1)}, u32[]{:S(2)}) copy-start(bf16[4,128,256]{2,1,0:T(8,128)(2,1)S(1)} %collective-permute-done.9.refs_9_) | copy-start | bytes 786436
  44.4 0.9 %copy-start.17 = (bf16[4,128,256]{2,1,0:T(8,128)(2,1)}, bf16[4,128,256]{2,1,0:T(8,128)(2,1)S(1)}, u32[]{:S(2)}) copy-start(bf16[4,128,256]{2,1,0:T(8,128)(2,1)S(1)} %collective-permute-done.8.refs_8_) | copy-start | bytes 786436
  52.5 1.8 %collective-permute-start.13 = (bf16[4,4,16,512]{3,2,1,0:T(8,128)(2,1)}, bf16[4,4,16,512]{3,2,1,0:T(8,128)(2,1)S(1)}, u32[]{:S(2)}, u32[]{:S(2)}) collective-permute-start(bf16[4,4,16,512]{3,2,1,0:T(8,128)(2,1)} %bitcast.65), channel_id=1, source_target_pairs={{0,1},{1,0},{2,3},{3,2},{4,5},{5,4},{6,7},{7,6},{8,9},{9,8},{10,11... | collective-permute-start | bytes 786440 | tf_op jit(solution)/shard_map/ppermute | solution.py:24
  52.6 8.9 %collective-permute-start.12 = (bf16[2,256,256]{2,1,0:T(8,128)(2,1)}, bf16[2,256,256]{2,1,0:T(8,128)(2,1)S(1)}, u32[]{:S(2)}, u32[]{:S(2)}) collective-permute-start(bf16[2,256,256]{2,1,0:T(8,128)(2,1)} %get-tuple-element.35), channel_id=1, source_target_pairs={{0,8},{2,10},{4,12},{6,14},{8,0},{10,2},{12,4},{14,6},{16,24},{18,... | collective-permute-start | bytes 786440 | tf_op jit(solution)/shard_map/ppermute | solution.py:24
  55.5 6.0 %collective-permute-start.14 = (bf16[4,16,512]{2,1,0:T(8,128)(2,1)S(1)}, bf16[4,16,512]{2,1,0:T(8,128)(2,1)S(1)}, u32[]{:S(2)}, u32[]{:S(2)}) collective-permute-start(bf16[4,16,512]{2,1,0:T(8,128)(2,1)S(1)} %get-tuple-element.51), channel_id=1, source_target_pairs={{0,2},{2,0},{4,6},{6,4},{8,10},{10,8},{12,14},{14,12},{16,18},{18,... | collective-permute-start | bytes 196616 | tf_op jit(solution)/shard_map/ppermute | solution.py:24
  57.0 5.7 %collective-permute-start.15 = (bf16[4,16,512]{2,1,0:T(8,128)(2,1)S(1)}, bf16[4,16,512]{2,1,0:T(8,128)(2,1)S(1)}, u32[]{:S(2)}, u32[]{:S(2)}) collective-permute-start(bf16[4,16,512]{2,1,0:T(8,128)(2,1)S(1)} %get-tuple-element.49), channel_id=1, source_target_pairs={{0,4},{2,6},{4,0},{6,2},{8,12},{10,14},{12,8},{14,10},{16,20},{18,... | collective-permute-start | bytes 196616 | tf_op jit(solution)/shard_map/ppermute | solution.py:24
  58.6 2.9 %copy-start.18 = (bf16[256,256]{1,0:T(8,128)(2,1)S(1)}, bf16[256,256]{1,0:T(8,128)(2,1)}, u32[]{:S(2)}) copy-start(bf16[256,256]{1,0:T(8,128)(2,1)} %get-tuple-element.41) | copy-start | bytes 393220
  58.6 2.9 %copy-start.19 = (bf16[256,256]{1,0:T(8,128)(2,1)S(1)}, bf16[256,256]{1,0:T(8,128)(2,1)}, u32[]{:S(2)}) copy-start(bf16[256,256]{1,0:T(8,128)(2,1)} %get-tuple-element.40) | copy-start | bytes 393220
  58.6 5.2 %collective-permute-start.16 = (bf16[4,16,512]{2,1,0:T(8,128)(2,1)S(1)}, bf16[4,16,512]{2,1,0:T(8,128)(2,1)S(1)}, u32[]{:S(2)}, u32[]{:S(2)}) collective-permute-start(bf16[4,16,512]{2,1,0:T(8,128)(2,1)S(1)} %get-tuple-element.50), channel_id=1, source_target_pairs={{0,6},{2,4},{4,2},{6,0},{8,14},{10,12},{12,10},{14,8},{16,22},{18,... | collective-permute-start | bytes 196616 | tf_op jit(solution)/shard_map/ppermute | solution.py:24
  63.8 3.9 %copy-start.6 = (bf16[256,256]{1,0:T(8,128)(2,1)S(1)}, bf16[256,256]{1,0:T(8,128)(2,1)}, u32[]{:S(2)}) copy-start(bf16[256,256]{1,0:T(8,128)(2,1)} %get-tuple-element.27) | copy-start | bytes 393220
  63.8 3.9 %copy-start.7 = (bf16[256,256]{1,0:T(8,128)(2,1)S(1)}, bf16[256,256]{1,0:T(8,128)(2,1)}, u32[]{:S(2)}) copy-start(bf16[256,256]{1,0:T(8,128)(2,1)} %get-tuple-element.33) | copy-start | bytes 393220
  63.9 4.8 %collective-permute-start.17 = (bf16[16,512]{1,0:T(8,128)(2,1)S(1)}, bf16[16,512]{1,0:T(8,128)(2,1)S(1)}, u32[]{:S(2)}, u32[]{:S(2)}) collective-permute-start(bf16[16,512]{1,0:T(8,128)(2,1)S(1)} %get-tuple-element.56), channel_id=1, source_target_pairs={{0,16},{2,18},{4,20},{6,22},{8,24},{10,26},{12,28},{14,30},{16,0},... | collective-permute-start | bytes 49160 | tf_op jit(solution)/shard_map/ppermute | solution.py:24
  66.5 5.5 %collective-permute-start.19 = (bf16[16,512]{1,0:T(8,128)(2,1)S(1)}, bf16[16,512]{1,0:T(8,128)(2,1)S(1)}, u32[]{:S(2)}, u32[]{:S(2)}) collective-permute-start(bf16[16,512]{1,0:T(8,128)(2,1)S(1)} %get-tuple-element.57), channel_id=1, source_target_pairs={{0,24},{2,26},{4,28},{6,30},{8,16},{10,18},{12,20},{14,22},{16,8},... | collective-permute-start | bytes 49160 | tf_op jit(solution)/shard_map/ppermute | solution.py:24
  67.6 4.4 %collective-permute-start.18 = (bf16[16,512]{1,0:T(8,128)(2,1)S(1)}, bf16[16,512]{1,0:T(8,128)(2,1)S(1)}, u32[]{:S(2)}, u32[]{:S(2)}) collective-permute-start(bf16[16,512]{1,0:T(8,128)(2,1)S(1)} %get-tuple-element.58), channel_id=1, source_target_pairs={{0,8},{2,10},{4,12},{6,14},{8,0},{10,2},{12,4},{14,6},{16,24},{18,... | collective-permute-start | bytes 49160 | tf_op jit(solution)/shard_map/ppermute | solution.py:24

commit v5 on v4

--- a/solution.py
+++ b/solution.py
@@ -14,6 +14,7 @@
 PAIR = 2
 DEAD = -1e30
 VMEM_LIMIT = 60 * 1024 * 1024
+VMEM_SOURCE = 1280 * 1024
 CUT = 2
 F32 = jnp.float32
 BF16 = jnp.bfloat16
@@ -81,7 +82,8 @@
 
 def attend_kernel(pieces, fine_width, scale, *refs):
     bias_ref = refs[0]
-    inputs = (refs[1:4], refs[4:7])
+    inputs = (refs[1:3], refs[4:6])
+    own_order, their_order = refs[3], refs[6]
     piece_refs = refs[7 : 7 + pieces]
     out_ref, dq_ref, away_ref, keep_ref, send_ref = refs[-5:]
     head_dim = out_ref.shape[1]
@@ -94,28 +96,30 @@
     bias = bias_ref[0]
     cols = (slice(0, fine_width), slice(fine_width, keys.shape[0]))
     contract = (((1,), (1,)), ((), ()))
-    weight = 0.0
-    places = ((out_ref, dq_ref), (away_ref.at[0], away_ref.at[1]))
-    for (query_ref, grad_ref, ordered_ref), (out_part, dq_part) in zip(inputs, places):
-        scores = lax.dot_general(query_ref[...], keys, contract, preferred_element_type=F32)
-        scores = scores * scale + bias
-        d_probs = lax.dot_general(grad_ref[...], values, contract, preferred_element_type=F32)
-        probs_parts = []
-        d_parts = []
-        for part in cols:
-            score = scores[:, part]
-            expo = jnp.exp(score - jnp.max(score, axis=1, keepdims=True))
-            probs = expo * (1.0 / jnp.sum(expo, axis=1, keepdims=True))
-            d_prob = d_probs[:, part]
-            delta = jnp.sum(probs * d_prob, axis=1, keepdims=True)
-            probs_parts.append(probs.astype(BF16))
-            d_parts.append((probs * (d_prob - delta)).astype(BF16))
-        out = jnp.dot(jnp.concatenate(probs_parts, axis=1), values, preferred_element_type=F32)
-        d_query = jnp.dot(jnp.concatenate(d_parts, axis=1), keys, preferred_element_type=F32)
-        d_query = (d_query * scale).astype(BF16)
-        out_part[...] = out.astype(BF16)
-        dq_part[...] = d_query
-        weight = weight + jnp.dot(ordered_ref[...], d_query, preferred_element_type=F32)
+    query, grad = (jnp.concatenate([own[...], their[...]]) for own, their in zip(*inputs))
+    scores = lax.dot_general(query, keys, contract, preferred_element_type=F32) * scale + bias
+    d_probs = lax.dot_general(grad, values, contract, preferred_element_type=F32)
+    probs_parts = []
+    d_parts = []
+    for part in cols:
+        score = scores[:, part]
+        expo = jnp.exp(score - jnp.max(score, axis=1, keepdims=True))
+        probs = expo * (1.0 / jnp.sum(expo, axis=1, keepdims=True))
+        d_prob = d_probs[:, part]
+        delta = jnp.sum(probs * d_prob, axis=1, keepdims=True)
+        probs_parts.append(probs.astype(BF16))
+        d_parts.append((probs * (d_prob - delta)).astype(BF16))
+    out = jnp.dot(jnp.concatenate(probs_parts, axis=1), values, preferred_element_type=F32)
+    d_query = jnp.dot(jnp.concatenate(d_parts, axis=1), keys, preferred_element_type=F32)
+    out = out.astype(BF16)
+    d_query = (d_query * scale).astype(BF16)
+    rows = out_ref.shape[0]
+    out_ref[...] = out[:rows]
+    dq_ref[...] = d_query[:rows]
+    away_ref[0] = out[rows:]
+    away_ref[1] = d_query[rows:]
+    weight = jnp.dot(own_order[...], d_query[:rows], preferred_element_type=F32)
+    weight += jnp.dot(their_order[...], d_query[rows:], preferred_element_type=F32)
     kept = keep_ref.shape[0]
     keep_ref[...] = weight[:kept]
     send_ref[...] = weight[kept:].astype(BF16)
@@ -172,7 +176,9 @@
             jax.ShapeDtypeStruct((depth - kept, width), BF16),
         ),
         input_output_aliases=aliases,
-        compiler_params=pltpu.CompilerParams(vmem_limit_bytes=VMEM_LIMIT),
+        compiler_params=pltpu.CompilerParams(
+            vmem_limit_bytes=min(VMEM_LIMIT, sum(p.shape[0] for p in pieces) * VMEM_SOURCE)
+        ),
         cost_estimate=pl.CostEstimate(
             flops=16 * count * rows * columns * head_dim,
             bytes_accessed=count * (columns * 512 + rows * head_dim * 8),

time: 73 us -> 68.8 us (0.942)
  waiting for transfers between devices: 14.2 us -> 21.5 us
  Pallas kernels: 16.4 us -> 12.8 us
  matrix products: 5.33 us -> 2.53 us
  starting transfers between devices: 26.7 us -> 24.5 us
  local copies, waits for them, and re-layouts: 5.02 us -> 3.37 us
  other arithmetic: 3.18 us -> 2.16 us
    ppermute x20, waiting for transfers between devices: 14.2 us -> 21.5 us  [swap(): return lax.ppermute(array, axis, [(i, i ^ mask) for i in range(size)])]
    pallas_call x2, Pallas kernels: 14.4 us -> 10.7 us  [attend(): pl.pallas_call(functools.partial(attend_kernel, len(pieces) + len(summari...]
    ppermute x20, starting transfers between devices: 26.7 us -> 24.5 us  [swap(): return lax.ppermute(array, axis, [(i, i ^ mask) for i in range(size)])]
    dot_general x2, matrix products: 2.12 us -> 0.71 us  [reorder(): lax.dot_general(shuffle, part, (((1,), (1,)), ((), ())), preferred_elemen...]
    dot_general x2, matrix products: 2.01 us -> 0.61 us  [project(): return jnp.dot(part, weights, preferred_element_type=F32).astype(BF16)]
    another operation x2, other arithmetic: 1.14 us -> 0.1 us
    unnamed x40 -> x18, local copies, waits for them, and re-layouts: 2.65 us -> 2.32 us
  transfers between devices with their start and end apart: 20 -> 20, of which waited for: 7 -> 9; matrix products, arithmetic and copies ran while one was open for 14% -> 7% of each run, Pallas kernels for 20% -> 16%
where the time goes in v5:
time: 68.8 us; the launch traced here: 68.6 us
  starting transfers between devices  24.5 us (36%)
  waiting for transfers between devices  21.5 us (31%)
  Pallas kernels  12.8 us (19%)
  local copies, waits for them, and re-layouts  3.37 us (5%)
  matrix products  2.53 us (4%)
  other arithmetic  2.16 us (3%)
  between operations  1.71 us (2%)
    ppermute x20, starting transfers between devices, swap(): return lax.ppermute(array, axis, [(i, i ^ mask) for i in range(size)])  24.5 us
    ppermute x20, waiting for transfers between devices, swap(): return lax.ppermute(array, axis, [(i, i ^ mask) for i in range(size)])  21.5 us
    pallas_call x2, Pallas kernels, attend(): pl.pallas_call(functools.partial(attend_kernel, len(pieces) + len(summari...  10.7 us
    unnamed x18, local copies, waits for them, and re-layouts  2.32 us
    pallas_call x1, Pallas kernels, shards(): pl.pallas_call(functools.partial(select_kernel, CUT), in_specs=[pl.BlockS...  2.07 us
  transfers between devices with their start and end apart: 20, of which 9 were waited for; matrix products, arithmetic and copies ran while one was open for 7% of the time, Pallas kernels for 16%

profile of v5, /device:TPU:0, one launch (start us, length us, event | category | flops | bytes accessed | tf_op | source)
XLA Modules:
  0.0 68.6 jit_solution(17725020697016670133)
XLA Ops:
  1.4 2.1 %select.34 = (bf16[144,256]{1,0:T(8,128)(2,1)}, bf16[128,256]{1,0:T(8,128)(2,1)}, bf16[144,256]{1,0:T(8,128)(2,1)}, bf16[272,256]{1,0:T(8,128)(2,1)}) custom-call(s32[1,8,16]{2,1,0:T(8,128)} %blocks_ref.1, s32[1]{0:T(128)} %copy.19.lengths_ref, bf16[1,128,1024]{2,1,0:T(8,128)(2,1)} %keys_ref.1, bf16[1,128,1024]{2,1,0:T(8,128)(2,1)} %values_ref.1), custom_call_target="tpu_custom_call" | custom-call | tf_op jit(solution)/shard_map/select/pallas_call | solution.py:213
  3.5 5.0 %collective-permute-start.2 = (bf16[144,256]{1,0:T(8,128)(2,1)}, bf16[144,256]{1,0:T(8,128)(2,1)S(1)}, u32[]{:S(2)}, u32[]{:S(2)}) collective-permute-start(bf16[144,256]{1,0:T(8,128)(2,1)} %get-tuple-element.25), channel_id=1, source_target_pairs={{0,24},{2,26},{4,28},{6,30},{8,16},{10,18},{12,20},{14,22},{16,8},... | collective-permute-start | bytes 221192 | tf_op jit(solution)/shard_map/ppermute | solution.py:25
  8.5 0.6 collective-permute-start
  9.2 0.9 %copy-done.1 = bf16[1,256,512]{2,1,0:T(8,128)(2,1)S(1)} copy-done((bf16[1,256,512]{2,1,0:T(8,128)(2,1)S(1)}, bf16[1,256,512]{2,1,0:T(8,128)(2,1)}, u32[]{:S(2)}) %copy-start.1) | copy-done | bytes 262168
  10.1 1.5 %collective-permute-start.3 = (bf16[512,512]{1,0:T(8,128)(2,1)S(1)}, bf16[512,512]{1,0:T(8,128)(2,1)S(1)}, u32[]{:S(2)}, u32[]{:S(2)}) collective-permute-start(bf16[512,512]{1,0:T(8,128)(2,1)S(1)} %pad_maximum_fusion), channel_id=1, source_target_pairs={{0,8},{2,10},{4,12},{6,14},{8,0},{10,2},{12,4},{14,6},{16,24},{18,... | collective-permute-start | bytes 1572872 | tf_op jit(solution)/shard_map/ppermute | solution.py:25
  11.6 0.7 copy-done.7
  12.3 0.1 select_reduce_fusion
  12.5 0.1 broadcast_reduce_fusion
  12.6 0.1 mul.60
  12.8 0.1 and.82
  12.9 0.1 and.86
  13.0 0.1 add.146
  13.3 0.1 add.155
  13.5 0.1 add.137
  13.6 0.4 convolution_convert_fusion.4.refs_3_
  14.0 0.3 fusion.refs_1_
  14.3 2.5 %collective-permute-done = bf16[272,256]{1,0:T(8,128)(2,1)S(1)} collective-permute-done((bf16[272,256]{1,0:T(8,128)(2,1)}, bf16[272,256]{1,0:T(8,128)(2,1)S(1)}, u32[]{:S(2)}, u32[]{:S(2)}) %collective-permute-start) | collective-permute-done | bytes 139296 | tf_op jit(solution)/shard_map/ppermute | solution.py:25
  16.9 2.6 %collective-permute-start.6 = (bf16[4,144,256]{2,1,0:T(8,128)(2,1)S(1)}, bf16[4,144,256]{2,1,0:T(8,128)(2,1)S(1)}, u32[]{:S(2)}, u32[]{:S(2)}) collective-permute-start(bf16[4,144,256]{2,1,0:T(8,128)(2,1)S(1)} %pad_maximum_fusion.1.refs_7_.refs_11_), channel_id=1, source_target_pairs={{0,6},{2,4},{4,2},{6,0},{8,14},{10,12},{12,10},{14,8},{16,22},{18,... | collective-permute-start | bytes 884744 | tf_op jit(solution)/shard_map/ppermute | solution.py:25
  19.5 0.5 collective-permute-start.5
  20.0 0.4 collective-permute-start.4
  20.5 1.6 %collective-permute-start.7 = (bf16[2,128,256]{2,1,0:T(8,128)(2,1)S(1)}, bf16[2,128,256]{2,1,0:T(8,128)(2,1)S(1)}, u32[]{:S(2)}, u32[]{:S(2)}) collective-permute-start(bf16[2,128,256]{2,1,0:T(8,128)(2,1)S(1)} %pad_maximum_fusion.3), channel_id=1, source_target_pairs={{0,16},{2,18},{4,20},{6,22},{8,24},{10,26},{12,28},{14,30},{16,0},... | collective-permute-start | bytes 393224 | tf_op jit(solution)/shard_map/ppermute | solution.py:25
  22.1 6.9 %collective-permute-done.7 = bf16[2,128,256]{2,1,0:T(8,128)(2,1)S(1)} collective-permute-done((bf16[2,128,256]{2,1,0:T(8,128)(2,1)S(1)}, bf16[2,128,256]{2,1,0:T(8,128)(2,1)S(1)}, u32[]{:S(2)}, u32[]{:S(2)}) %collective-permute-start.7) | collective-permute-done | bytes 131104 | tf_op jit(solution)/shard_map/ppermute | solution.py:25
  29.0 0.8 %collective-permute-done.3.refs_5_ = bf16[512,512]{1,0:T(8,128)(2,1)S(1)} collective-permute-done((bf16[512,512]{1,0:T(8,128)(2,1)S(1)}, bf16[512,512]{1,0:T(8,128)(2,1)S(1)}, u32[]{:S(2)}, u32[]{:S(2)}) %collective-permute-start.3) | collective-permute-done | bytes 524320 | tf_op jit(solution)/shard_map/ppermute | solution.py:25
  29.8 2.6 %collective-permute-start.10 = (bf16[4,128,256]{2,1,0:T(8,128)(2,1)S(1)}, bf16[4,128,256]{2,1,0:T(8,128)(2,1)S(1)}, u32[]{:S(2)}, u32[]{:S(2)}) collective-permute-start(bf16[4,128,256]{2,1,0:T(8,128)(2,1)S(1)} %pad_maximum_fusion.2.refs_7_), channel_id=1, source_target_pairs={{0,6},{2,4},{4,2},{6,0},{8,14},{10,12},{12,10},{14,8},{16,22},{18,... | collective-permute-start | bytes 786440 | tf_op jit(solution)/shard_map/ppermute | solution.py:25
  32.4 0.5 collective-permute-start.9
  32.9 0.3 convolution_convert_fusion.3.refs_4_
  33.3 0.3 convolution_convert_fusion.2.refs_6_
  33.6 0.4 collective-permute-start.8
  34.0 5.4 %attend.2 = (bf16[256,256]{1,0:T(8,128)(2,1)S(1)}, bf16[256,256]{1,0:T(8,128)(2,1)S(1)}, bf16[2,256,256]{2,1,0:T(8,128)(2,1)S(1)}, f32[256,512]{1,0:T(8,128)S(1)}, bf16[256,512]{1,0:T(8,128)(2,1)S(1)}) custom-call(f32[4,1,1280]{2,1,0:T(1,128)S(1)} %broadcast_in_dim.57.refs_0_, bf16[256,512]{1,0:T(8,128)(2,1)S(1)} %fusion.refs_1_, ...), custom_call_target="tpu_custom_call" | custom-call | flops 1342177280 | bytes 1835008 | tf_op jit(solution)/shard_map/attend/pallas_call | solution.py:160
  39.5 1.0 %collective-permute-start.11 = (bf16[2,256,256]{2,1,0:T(8,128)(2,1)S(1)}, bf16[2,256,256]{2,1,0:T(8,128)(2,1)S(1)}, u32[]{:S(2)}, u32[]{:S(2)}) collective-permute-start(bf16[2,256,256]{2,1,0:T(8,128)(2,1)S(1)} %get-tuple-element.34), channel_id=1, source_target_pairs={{0,8},{2,10},{4,12},{6,14},{8,0},{10,2},{12,4},{14,6},{16,24},{18,... | collective-permute-start | bytes 786440 | tf_op jit(solution)/shard_map/ppermute | solution.py:25
  40.4 3.3 %collective-permute-done.9.refs_9_ = bf16[4,128,256]{2,1,0:T(8,128)(2,1)S(1)} collective-permute-done((bf16[4,128,256]{2,1,0:T(8,128)(2,1)S(1)}, bf16[4,128,256]{2,1,0:T(8,128)(2,1)S(1)}, u32[]{:S(2)}, u32[]{:S(2)}) %collective-permute-start.9) | collective-permute-done | bytes 262176 | tf_op jit(solution)/shard_map/ppermute | solution.py:25
  43.7 0.3 collective-permute-done.8.refs_8_
  44.0 5.3 %attend.3 = (bf16[256,256]{1,0:T(8,128)(2,1)S(1)}, bf16[256,256]{1,0:T(8,128)(2,1)S(1)}, bf16[2,256,256]{2,1,0:T(8,128)(2,1)S(1)}, f32[256,512]{1,0:T(8,128)S(1)}, bf16[256,512]{1,0:T(8,128)(2,1)S(1)}) custom-call(f32[4,1,1280]{2,1,0:T(1,128)S(1)} %broadcast_in_dim.57.refs_0_, ...), custom_call_target="tpu_custom_call", output_to_operand_aliasing={{3}: (15, {}), {4}: (16, {})} | custom-call | flops 1342177280 | bytes 1835008 | tf_op jit(solution)/shard_map/attend/pallas_call | solution.py:160
  49.3 0.7 %copy-done.3 = bf16[2,256,256]{2,1,0:T(8,128)(2,1)} copy-done((bf16[2,256,256]{2,1,0:T(8,128)(2,1)}, bf16[2,256,256]{2,1,0:T(8,128)(2,1)S(1)}, u32[]{:S(2)}) %copy-start.3) | copy-done | bytes 262168
  50.1 1.5 %collective-permute-done.13 = bf16[4,4,16,512]{3,2,1,0:T(8,128)(2,1)S(1)} collective-permute-done((bf16[4,4,16,512]{3,2,1,0:T(8,128)(2,1)S(1)}, bf16[4,4,16,512]{3,2,1,0:T(8,128)(2,1)S(1)}, u32[]{:S(2)}, u32[]{:S(2)}) %collective-permute-start.13) | collective-permute-done | bytes 262176 | tf_op jit(solution)/shard_map/ppermute | solution.py:25
  51.5 0.1 fusion.33
  51.7 1.6 %collective-permute-start.14 = (bf16[4,16,512]{2,1,0:T(8,128)(2,1)S(1)}, bf16[4,16,512]{2,1,0:T(8,128)(2,1)S(1)}, u32[]{:S(2)}, u32[]{:S(2)}) collective-permute-start(bf16[4,16,512]{2,1,0:T(8,128)(2,1)S(1)} %get-tuple-element.51), channel_id=1, source_target_pairs={{0,2},{2,0},{4,6},{6,4},{8,10},{10,8},{12,14},{14,12},{16,18},{18,... | collective-permute-start | bytes 196616 | tf_op jit(solution)/shard_map/ppermute | solution.py:25
  53.3 0.8 %collective-permute-start.15 = (bf16[4,16,512]{2,1,0:T(8,128)(2,1)S(1)}, bf16[4,16,512]{2,1,0:T(8,128)(2,1)S(1)}, u32[]{:S(2)}, u32[]{:S(2)}) collective-permute-start(bf16[4,16,512]{2,1,0:T(8,128)(2,1)S(1)} %get-tuple-element.49), channel_id=1, source_target_pairs={{0,4},{2,6},{4,0},{6,2},{8,12},{10,14},{12,8},{14,10},{16,20},{18,... | collective-permute-start | bytes 196616 | tf_op jit(solution)/shard_map/ppermute | solution.py:25
  54.1 1.5 %collective-permute-start.16 = (bf16[4,16,512]{2,1,0:T(8,128)(2,1)S(1)}, bf16[4,16,512]{2,1,0:T(8,128)(2,1)S(1)}, u32[]{:S(2)}, u32[]{:S(2)}) collective-permute-start(bf16[4,16,512]{2,1,0:T(8,128)(2,1)S(1)} %get-tuple-element.50), channel_id=1, source_target_pairs={{0,6},{2,4},{4,2},{6,0},{8,14},{10,12},{12,10},{14,8},{16,22},{18,... | collective-permute-start | bytes 196616 | tf_op jit(solution)/shard_map/ppermute | solution.py:25
  55.6 3.1 %collective-permute-done.12 = bf16[2,256,256]{2,1,0:T(8,128)(2,1)S(1)} collective-permute-done((bf16[2,256,256]{2,1,0:T(8,128)(2,1)S(1)}, bf16[2,256,256]{2,1,0:T(8,128)(2,1)S(1)}, u32[]{:S(2)}, u32[]{:S(2)}) %collective-permute-start.12) | collective-permute-done | bytes 262176 | tf_op jit(solution)/shard_map/ppermute | solution.py:25
  58.8 1.2 %convolution_convert_fusion.1 = bf16[256,512]{1,0:T(8,128)(2,1)} fusion(bf16[512,1024]{1,0:T(8,128)(2,1)S(1)} %copy-done, bf16[256,256]{1,0:T(8,128)(2,1)S(1)} %get-tuple-element.54, bf16[256,256]{1,0:T(8,128)(2,1)S(1)} %get-tuple-element.52, bf16[256,256]{1,0:T(8,128)(2,1)S(1)} %get-tuple-element.41, bf16[256,256]{1,0:T(8,128)(2,1)S(1)} %get-tuple-element.40, ...), kind=kOutput, calls=%fused_computation.1 | convolution fusion | flops 273022976 | bytes 1835009 | tf_op jit(solution)/shard_map/dot_general | solution.py:314
  60.0 2.3 %collective-permute-start.17 = (bf16[16,512]{1,0:T(8,128)(2,1)S(1)}, bf16[16,512]{1,0:T(8,128)(2,1)S(1)}, u32[]{:S(2)}, u32[]{:S(2)}) collective-permute-start(bf16[16,512]{1,0:T(8,128)(2,1)S(1)} %get-tuple-element.56), channel_id=1, source_target_pairs={{0,16},{2,18},{4,20},{6,22},{8,24},{10,26},{12,28},{14,30},{16,0},... | collective-permute-start | bytes 49160 | tf_op jit(solution)/shard_map/ppermute | solution.py:25
  62.4 0.9 %collective-permute-start.19 = (bf16[16,512]{1,0:T(8,128)(2,1)S(1)}, bf16[16,512]{1,0:T(8,128)(2,1)S(1)}, u32[]{:S(2)}, u32[]{:S(2)}) collective-permute-start(bf16[16,512]{1,0:T(8,128)(2,1)S(1)} %get-tuple-element.57), channel_id=1, source_target_pairs={{0,24},{2,26},{4,28},{6,30},{8,16},{10,18},{12,20},{14,22},{16,8},... | collective-permute-start | bytes 49160 | tf_op jit(solution)/shard_map/ppermute | solution.py:25
  63.2 0.5 collective-permute-start.18
  63.7 0.9 %maximum_select_fusion = bf16[1,256,1024]{2,1,0:T(8,128)(2,1)} fusion(bf16[1,256,256]{2,1,0:T(8,128)(2,1)S(1)} %get-tuple-element.55, bf16[1,256,256]{2,1,0:T(8,128)(2,1)S(1)} %get-tuple-element.53, bf16[1,256,256]{2,1,0:T(8,128)(2,1)S(1)} %bitcast.59, bf16[1,256,256]{2,1,0:T(8,128)(2,1)S(1)} %bitcast.58, pred[]{:T(512)S(6)} %eq.52), kind=kLoop, calls=%fused_computation.8 | loop fusion | flops 4456448 | bytes 1048577 | tf_op jit(solution)/shard_map/jit(_where)/select_n | solution.py:309
  64.7 0.1 collective-permute-done.17
  64.8 3.2 %collective-permute-done.19 = bf16[16,512]{1,0:T(8,128)(2,1)S(1)} collective-permute-done((bf16[16,512]{1,0:T(8,128)(2,1)S(1)}, bf16[16,512]{1,0:T(8,128)(2,1)S(1)}, u32[]{:S(2)}, u32[]{:S(2)}) %collective-permute-start.19) | collective-permute-done | bytes 16416 | tf_op jit(solution)/shard_map/ppermute | solution.py:25
  67.9 0.6 maximum_select_fusion.3
  (65 shorter events, 1.0 us)
Async XLA Ops:
  0.6 13.3 %copy-start = (bf16[512,1024]{1,0:T(8,128)(2,1)S(1)}, bf16[512,1024]{1,0:T(8,128)(2,1)}, u32[]{:S(2)}) copy-start(bf16[512,1024]{1,0:T(8,128)(2,1)} %param.9) | copy-start | bytes 3145732
  0.6 8.5 %copy-start.2 = (bf16[1,256,1024]{2,1,0:T(8,128)(2,1)S(1)}, bf16[1,256,1024]{2,1,0:T(8,128)(2,1)}, u32[]{:S(2)}) copy-start(bf16[1,256,1024]{2,1,0:T(8,128)(2,1)} %param.14) | copy-start | bytes 1572868
  3.5 13.3 %collective-permute-start.2 = (bf16[144,256]{1,0:T(8,128)(2,1)}, bf16[144,256]{1,0:T(8,128)(2,1)S(1)}, u32[]{:S(2)}, u32[]{:S(2)}) collective-permute-start(bf16[144,256]{1,0:T(8,128)(2,1)} %get-tuple-element.25), channel_id=1, source_target_pairs={{0,24},{2,26},{4,28},{6,30},{8,16},{10,18},{12,20},{14,22},{16,8},... | collective-permute-start | bytes 221192 | tf_op jit(solution)/shard_map/ppermute | solution.py:25
  8.5 8.3 %collective-permute-start.1 = (bf16[144,256]{1,0:T(8,128)(2,1)}, bf16[144,256]{1,0:T(8,128)(2,1)S(1)}, u32[]{:S(2)}, u32[]{:S(2)}) collective-permute-start(bf16[144,256]{1,0:T(8,128)(2,1)} %get-tuple-element.23), channel_id=1, source_target_pairs={{0,16},{2,18},{4,20},{6,22},{8,24},{10,26},{12,28},{14,30},{16,0},... | collective-permute-start | bytes 221192 | tf_op jit(solution)/shard_map/ppermute | solution.py:25
  8.5 8.2 %collective-permute-start = (bf16[272,256]{1,0:T(8,128)(2,1)}, bf16[272,256]{1,0:T(8,128)(2,1)S(1)}, u32[]{:S(2)}, u32[]{:S(2)}) collective-permute-start(bf16[272,256]{1,0:T(8,128)(2,1)} %get-tuple-element.24), channel_id=1, source_target_pairs={{0,8},{2,10},{4,12},{6,14},{8,0},{10,2},{12,4},{14,6},{16,24},{18,... | collective-permute-start | bytes 417800 | tf_op jit(solution)/shard_map/ppermute | solution.py:25
  9.1 1.0 %copy-start.1 = (bf16[1,256,512]{2,1,0:T(8,128)(2,1)S(1)}, bf16[1,256,512]{2,1,0:T(8,128)(2,1)}, u32[]{:S(2)}) copy-start(bf16[1,256,512]{2,1,0:T(8,128)(2,1)} %param.8) | copy-start | bytes 786436
  10.1 1.6 %copy-start.8 = (s32[16]{0:T(128)S(1)}, s32[16]{0:T(128)}, u32[]{:S(2)}) copy-start(s32[16]{0:T(128)} %constant.93.clone) | copy-start | bytes 196
  10.1 19.7 %collective-permute-start.3 = (bf16[512,512]{1,0:T(8,128)(2,1)S(1)}, bf16[512,512]{1,0:T(8,128)(2,1)S(1)}, u32[]{:S(2)}, u32[]{:S(2)}) collective-permute-start(bf16[512,512]{1,0:T(8,128)(2,1)S(1)} %pad_maximum_fusion), channel_id=1, source_target_pairs={{0,8},{2,10},{4,12},{6,14},{8,0},{10,2},{12,4},{14,6},{16,24},{18,... | collective-permute-start | bytes 1572872 | tf_op jit(solution)/shard_map/ppermute | solution.py:25
  11.6 0.7 %copy-start.7 = (s32[1,8,16]{2,1,0:T(8,128)S(1)}, s32[1,8,16]{2,1,0:T(8,128)}, u32[]{:S(2)}) copy-start(s32[1,8,16]{2,1,0:T(8,128)} %blocks_ref.1) | copy-start | bytes 1540
  14.3 2.5 %copy-start.5 = (bf16[144,256]{1,0:T(8,128)(2,1)S(1)}, bf16[144,256]{1,0:T(8,128)(2,1)}, u32[]{:S(2)}) copy-start(bf16[144,256]{1,0:T(8,128)(2,1)} %get-tuple-element.23) | copy-start | bytes 221188
  16.9 3.6 %copy-start.6 = (bf16[128,256]{1,0:T(8,128)(2,1)S(1)}, bf16[128,256]{1,0:T(8,128)(2,1)}, u32[]{:S(2)}) copy-start(bf16[128,256]{1,0:T(8,128)(2,1)} %get-tuple-element.28) | copy-start | bytes 196612
  16.9 16.7 %collective-permute-start.6 = (bf16[4,144,256]{2,1,0:T(8,128)(2,1)S(1)}, bf16[4,144,256]{2,1,0:T(8,128)(2,1)S(1)}, u32[]{:S(2)}, u32[]{:S(2)}) collective-permute-start(bf16[4,144,256]{2,1,0:T(8,128)(2,1)S(1)} %pad_maximum_fusion.1.refs_7_.refs_11_), channel_id=1, source_target_pairs={{0,6},{2,4},{4,2},{6,0},{8,14},{10,12},{12,10},{14,8},{16,22},{18,... | collective-permute-start | bytes 884744 | tf_op jit(solution)/shard_map/ppermute | solution.py:25
  19.5 14.5 %collective-permute-start.5 = (bf16[4,144,256]{2,1,0:T(8,128)(2,1)S(1)}, bf16[4,144,256]{2,1,0:T(8,128)(2,1)S(1)}, u32[]{:S(2)}, u32[]{:S(2)}) collective-permute-start(bf16[4,144,256]{2,1,0:T(8,128)(2,1)S(1)} %pad_maximum_fusion.1.refs_7_.refs_11_), channel_id=1, source_target_pairs={{0,4},{2,6},{4,0},{6,2},{8,12},{10,14},{12,8},{14,10},{16,20},{18,... | collective-permute-start | bytes 884744 | tf_op jit(solution)/shard_map/ppermute | solution.py:25
  20.0 14.0 %collective-permute-start.4 = (bf16[4,144,256]{2,1,0:T(8,128)(2,1)S(1)}, bf16[4,144,256]{2,1,0:T(8,128)(2,1)S(1)}, u32[]{:S(2)}, u32[]{:S(2)}) collective-permute-start(bf16[4,144,256]{2,1,0:T(8,128)(2,1)S(1)} %pad_maximum_fusion.1.refs_7_.refs_11_), channel_id=1, source_target_pairs={{0,2},{2,0},{4,6},{6,4},{8,10},{10,8},{12,14},{14,12},{16,18},{18,... | collective-permute-start | bytes 884744 | tf_op jit(solution)/shard_map/ppermute | solution.py:25
  20.5 8.5 %collective-permute-start.7 = (bf16[2,128,256]{2,1,0:T(8,128)(2,1)S(1)}, bf16[2,128,256]{2,1,0:T(8,128)(2,1)S(1)}, u32[]{:S(2)}, u32[]{:S(2)}) collective-permute-start(bf16[2,128,256]{2,1,0:T(8,128)(2,1)S(1)} %pad_maximum_fusion.3), channel_id=1, source_target_pairs={{0,16},{2,18},{4,20},{6,22},{8,24},{10,26},{12,28},{14,30},{16,0},... | collective-permute-start | bytes 393224 | tf_op jit(solution)/shard_map/ppermute | solution.py:25
  29.8 10.6 %collective-permute-start.10 = (bf16[4,128,256]{2,1,0:T(8,128)(2,1)S(1)}, bf16[4,128,256]{2,1,0:T(8,128)(2,1)S(1)}, u32[]{:S(2)}, u32[]{:S(2)}) collective-permute-start(bf16[4,128,256]{2,1,0:T(8,128)(2,1)S(1)} %pad_maximum_fusion.2.refs_7_), channel_id=1, source_target_pairs={{0,6},{2,4},{4,2},{6,0},{8,14},{10,12},{12,10},{14,8},{16,22},{18,... | collective-permute-start | bytes 786440 | tf_op jit(solution)/shard_map/ppermute | solution.py:25
  32.4 11.2 %collective-permute-start.9 = (bf16[4,128,256]{2,1,0:T(8,128)(2,1)S(1)}, bf16[4,128,256]{2,1,0:T(8,128)(2,1)S(1)}, u32[]{:S(2)}, u32[]{:S(2)}) collective-permute-start(bf16[4,128,256]{2,1,0:T(8,128)(2,1)S(1)} %pad_maximum_fusion.2.refs_7_), channel_id=1, source_target_pairs={{0,4},{2,6},{4,0},{6,2},{8,12},{10,14},{12,8},{14,10},{16,20},{18,... | collective-permute-start | bytes 786440 | tf_op jit(solution)/shard_map/ppermute | solution.py:25
  33.6 10.4 %collective-permute-start.8 = (bf16[4,128,256]{2,1,0:T(8,128)(2,1)S(1)}, bf16[4,128,256]{2,1,0:T(8,128)(2,1)S(1)}, u32[]{:S(2)}, u32[]{:S(2)}) collective-permute-start(bf16[4,128,256]{2,1,0:T(8,128)(2,1)S(1)} %pad_maximum_fusion.2.refs_7_), channel_id=1, source_target_pairs={{0,2},{2,0},{4,6},{6,4},{8,10},{10,8},{12,14},{14,12},{16,18},{18,... | collective-permute-start | bytes 786440 | tf_op jit(solution)/shard_map/ppermute | solution.py:25
  39.5 9.8 %collective-permute-start.11 = (bf16[2,256,256]{2,1,0:T(8,128)(2,1)S(1)}, bf16[2,256,256]{2,1,0:T(8,128)(2,1)S(1)}, u32[]{:S(2)}, u32[]{:S(2)}) collective-permute-start(bf16[2,256,256]{2,1,0:T(8,128)(2,1)S(1)} %get-tuple-element.34), channel_id=1, source_target_pairs={{0,8},{2,10},{4,12},{6,14},{8,0},{10,2},{12,4},{14,6},{16,24},{18,... | collective-permute-start | bytes 786440 | tf_op jit(solution)/shard_map/ppermute | solution.py:25
  49.3 0.7 %copy-start.3 = (bf16[2,256,256]{2,1,0:T(8,128)(2,1)}, bf16[2,256,256]{2,1,0:T(8,128)(2,1)S(1)}, u32[]{:S(2)}) copy-start(bf16[2,256,256]{2,1,0:T(8,128)(2,1)S(1)} %collective-permute-done.11) | copy-start | bytes 786436
  50.0 1.5 %collective-permute-start.13 = (bf16[4,4,16,512]{3,2,1,0:T(8,128)(2,1)S(1)}, bf16[4,4,16,512]{3,2,1,0:T(8,128)(2,1)S(1)}, u32[]{:S(2)}, u32[]{:S(2)}) collective-permute-start(bf16[4,4,16,512]{3,2,1,0:T(8,128)(2,1)S(1)} %bitcast.60), channel_id=1, source_target_pairs={{0,1},{1,0},{2,3},{3,2},{4,5},{5,4},{6,7},{7,6},{8,9},{9,8},{10,11... | collective-permute-start | bytes 786440 | tf_op jit(solution)/shard_map/ppermute | solution.py:25
  50.0 8.7 %collective-permute-start.12 = (bf16[2,256,256]{2,1,0:T(8,128)(2,1)S(1)}, bf16[2,256,256]{2,1,0:T(8,128)(2,1)S(1)}, u32[]{:S(2)}, u32[]{:S(2)}) collective-permute-start(bf16[2,256,256]{2,1,0:T(8,128)(2,1)S(1)} %get-tuple-element.35), channel_id=1, source_target_pairs={{0,8},{2,10},{4,12},{6,14},{8,0},{10,2},{12,4},{14,6},{16,24},{18,... | collective-permute-start | bytes 786440 | tf_op jit(solution)/shard_map/ppermute | solution.py:25
  51.6 1.6 %copy-start.4 = (bf16[2,256,256]{2,1,0:T(8,128)(2,1)S(1)}, bf16[2,256,256]{2,1,0:T(8,128)(2,1)}, u32[]{:S(2)}) copy-start(bf16[2,256,256]{2,1,0:T(8,128)(2,1)} %copy-done.3) | copy-start | bytes 786436
  51.7 7.1 %collective-permute-start.14 = (bf16[4,16,512]{2,1,0:T(8,128)(2,1)S(1)}, bf16[4,16,512]{2,1,0:T(8,128)(2,1)S(1)}, u32[]{:S(2)}, u32[]{:S(2)}) collective-permute-start(bf16[4,16,512]{2,1,0:T(8,128)(2,1)S(1)} %get-tuple-element.51), channel_id=1, source_target_pairs={{0,2},{2,0},{4,6},{6,4},{8,10},{10,8},{12,14},{14,12},{16,18},{18,... | collective-permute-start | bytes 196616 | tf_op jit(solution)/shard_map/ppermute | solution.py:25
  53.3 6.7 %collective-permute-start.15 = (bf16[4,16,512]{2,1,0:T(8,128)(2,1)S(1)}, bf16[4,16,512]{2,1,0:T(8,128)(2,1)S(1)}, u32[]{:S(2)}, u32[]{:S(2)}) collective-permute-start(bf16[4,16,512]{2,1,0:T(8,128)(2,1)S(1)} %get-tuple-element.49), channel_id=1, source_target_pairs={{0,4},{2,6},{4,0},{6,2},{8,12},{10,14},{12,8},{14,10},{16,20},{18,... | collective-permute-start | bytes 196616 | tf_op jit(solution)/shard_map/ppermute | solution.py:25
  54.1 5.9 %collective-permute-start.16 = (bf16[4,16,512]{2,1,0:T(8,128)(2,1)S(1)}, bf16[4,16,512]{2,1,0:T(8,128)(2,1)S(1)}, u32[]{:S(2)}, u32[]{:S(2)}) collective-permute-start(bf16[4,16,512]{2,1,0:T(8,128)(2,1)S(1)} %get-tuple-element.50), channel_id=1, source_target_pairs={{0,6},{2,4},{4,2},{6,0},{8,14},{10,12},{12,10},{14,8},{16,22},{18,... | collective-permute-start | bytes 196616 | tf_op jit(solution)/shard_map/ppermute | solution.py:25
  60.0 4.7 %collective-permute-start.17 = (bf16[16,512]{1,0:T(8,128)(2,1)S(1)}, bf16[16,512]{1,0:T(8,128)(2,1)S(1)}, u32[]{:S(2)}, u32[]{:S(2)}) collective-permute-start(bf16[16,512]{1,0:T(8,128)(2,1)S(1)} %get-tuple-element.56), channel_id=1, source_target_pairs={{0,16},{2,18},{4,20},{6,22},{8,24},{10,26},{12,28},{14,30},{16,0},... | collective-permute-start | bytes 49160 | tf_op jit(solution)/shard_map/ppermute | solution.py:25
  62.4 5.5 %collective-permute-start.19 = (bf16[16,512]{1,0:T(8,128)(2,1)S(1)}, bf16[16,512]{1,0:T(8,128)(2,1)S(1)}, u32[]{:S(2)}, u32[]{:S(2)}) collective-permute-start(bf16[16,512]{1,0:T(8,128)(2,1)S(1)} %get-tuple-element.57), channel_id=1, source_target_pairs={{0,24},{2,26},{4,28},{6,30},{8,16},{10,18},{12,20},{14,22},{16,8},... | collective-permute-start | bytes 49160 | tf_op jit(solution)/shard_map/ppermute | solution.py:25
  63.2 4.7 %collective-permute-start.18 = (bf16[16,512]{1,0:T(8,128)(2,1)S(1)}, bf16[16,512]{1,0:T(8,128)(2,1)S(1)}, u32[]{:S(2)}, u32[]{:S(2)}) collective-permute-start(bf16[16,512]{1,0:T(8,128)(2,1)S(1)} %get-tuple-element.58), channel_id=1, source_target_pairs={{0,8},{2,10},{4,12},{6,14},{8,0},{10,2},{12,4},{14,6},{16,24},{18,... | collective-permute-start | bytes 49160 | tf_op jit(solution)/shard_map/ppermute | solution.py:25

commit v6 on v5

--- a/solution.py
+++ b/solution.py
@@ -303,6 +303,12 @@
     for part in parts:
         level = level + part.astype(F32)
 
+    taken = [swap(level[k].astype(BF16), "hist", QUAD * k) for k in range(1, n_hist // QUAD)]
+    sums = [level[0], None]
+    for index, part in enumerate(taken, 1):
+        got = part.astype(F32)
+        sums[index % PAIR] = got if sums[index % PAIR] is None else sums[index % PAIR] + got
+
     def join(index):
         own = [(out_near, dq_near)[index], (out_late, dq_late)[index]]
         back = [back_near[index], back_late[index]]
@@ -314,12 +320,7 @@
     d_targets = lax.dot_general(
         join(1), w_query, (((1,), (1,)), ((), ())), preferred_element_type=F32
     ).astype(BF16)
-    level = after(level, (attended, d_targets))
-
-    sums = [level[0], None]
-    for index in range(1, n_hist // QUAD):
-        got = swap(level[index].astype(BF16), "hist", QUAD * index).astype(F32)
-        sums[index % PAIR] = got if sums[index % PAIR] is None else sums[index % PAIR] + got
+
     d_query_weight = jnp.where(
         side == 0, jnp.concatenate(sums, axis=1), jnp.concatenate(sums[::-1], axis=1)
     )

time: 68.8 us -> 67.8 us (0.985)
  transfers between devices with their start and end apart: 20 -> 20, of which waited for: 9 -> 10; matrix products, arithmetic and copies ran while one was open for 7% -> 7% of each run, Pallas kernels for 16% -> 16%
where the time goes in v6:
time: 67.8 us; the launch traced here: 67.6 us
  starting transfers between devices  24.1 us (36%)
  waiting for transfers between devices  20.9 us (31%)
  Pallas kernels  12.8 us (19%)
  local copies, waits for them, and re-layouts  3.37 us (5%)
  matrix products  2.53 us (4%)
  other arithmetic  2.15 us (3%)
  between operations  1.71 us (3%)
    ppermute x20, starting transfers between devices, swap(): return lax.ppermute(array, axis, [(i, i ^ mask) for i in range(size)])  24.1 us
    ppermute x20, waiting for transfers between devices, swap(): return lax.ppermute(array, axis, [(i, i ^ mask) for i in range(size)])  20.9 us
    pallas_call x2, Pallas kernels, attend(): pl.pallas_call(functools.partial(attend_kernel, len(pieces) + len(summari...  10.7 us
    unnamed x18, local copies, waits for them, and re-layouts  2.32 us
    pallas_call x1, Pallas kernels, shards(): pl.pallas_call(functools.partial(select_kernel, CUT), in_specs=[pl.BlockS...  2.07 us
  transfers between devices with their start and end apart: 20, of which 10 were waited for; matrix products, arithmetic and copies ran while one was open for 7% of the time, Pallas kernels for 16%

profile of v6, /device:TPU:0, one launch (start us, length us, event | category | flops | bytes accessed | tf_op | source)
XLA Modules:
  0.0 67.6 jit_solution(5642736341061886385)
XLA Ops:
  1.4 2.1 %select.34 = (bf16[144,256]{1,0:T(8,128)(2,1)}, bf16[128,256]{1,0:T(8,128)(2,1)}, bf16[144,256]{1,0:T(8,128)(2,1)}, bf16[272,256]{1,0:T(8,128)(2,1)}) custom-call(s32[1,8,16]{2,1,0:T(8,128)} %blocks_ref.1, s32[1]{0:T(128)} %copy.19.lengths_ref, bf16[1,128,1024]{2,1,0:T(8,128)(2,1)} %keys_ref.1, bf16[1,128,1024]{2,1,0:T(8,128)(2,1)} %values_ref.1), custom_call_target="tpu_custom_call" | custom-call | tf_op jit(solution)/shard_map/select/pallas_call | solution.py:213
  3.5 5.0 %collective-permute-start.2 = (bf16[144,256]{1,0:T(8,128)(2,1)}, bf16[144,256]{1,0:T(8,128)(2,1)S(1)}, u32[]{:S(2)}, u32[]{:S(2)}) collective-permute-start(bf16[144,256]{1,0:T(8,128)(2,1)} %get-tuple-element.24), channel_id=1, source_target_pairs={{0,24},{2,26},{4,28},{6,30},{8,16},{10,18},{12,20},{14,22},{16,8},... | collective-permute-start | bytes 221192 | tf_op jit(solution)/shard_map/ppermute | solution.py:25
  8.5 0.6 collective-permute-start
  9.2 0.9 %copy-done.1 = bf16[1,256,512]{2,1,0:T(8,128)(2,1)S(1)} copy-done((bf16[1,256,512]{2,1,0:T(8,128)(2,1)S(1)}, bf16[1,256,512]{2,1,0:T(8,128)(2,1)}, u32[]{:S(2)}) %copy-start.1) | copy-done | bytes 262168
  10.1 1.5 %collective-permute-start.3 = (bf16[512,512]{1,0:T(8,128)(2,1)S(1)}, bf16[512,512]{1,0:T(8,128)(2,1)S(1)}, u32[]{:S(2)}, u32[]{:S(2)}) collective-permute-start(bf16[512,512]{1,0:T(8,128)(2,1)S(1)} %pad_maximum_fusion), channel_id=1, source_target_pairs={{0,8},{2,10},{4,12},{6,14},{8,0},{10,2},{12,4},{14,6},{16,24},{18,... | collective-permute-start | bytes 1572872 | tf_op jit(solution)/shard_map/ppermute | solution.py:25
  11.6 0.7 copy-done.7
  12.3 0.1 select_reduce_fusion
  12.5 0.1 broadcast_reduce_fusion
  12.6 0.1 mul.60
  12.8 0.1 and.82
  12.9 0.1 and.86
  13.0 0.1 add.146
  13.5 0.1 add.137
  13.6 0.4 convolution_convert_fusion.4.refs_3_
  14.0 0.3 fusion.refs_1_
  14.3 2.5 %collective-permute-done = bf16[272,256]{1,0:T(8,128)(2,1)S(1)} collective-permute-done((bf16[272,256]{1,0:T(8,128)(2,1)}, bf16[272,256]{1,0:T(8,128)(2,1)S(1)}, u32[]{:S(2)}, u32[]{:S(2)}) %collective-permute-start) | collective-permute-done | bytes 139296 | tf_op jit(solution)/shard_map/ppermute | solution.py:25
  16.9 2.6 %collective-permute-start.6 = (bf16[4,144,256]{2,1,0:T(8,128)(2,1)S(1)}, bf16[4,144,256]{2,1,0:T(8,128)(2,1)S(1)}, u32[]{:S(2)}, u32[]{:S(2)}) collective-permute-start(bf16[4,144,256]{2,1,0:T(8,128)(2,1)S(1)} %pad_maximum_fusion.1.refs_7_.refs_11_), channel_id=1, source_target_pairs={{0,6},{2,4},{4,2},{6,0},{8,14},{10,12},{12,10},{14,8},{16,22},{18,... | collective-permute-start | bytes 884744 | tf_op jit(solution)/shard_map/ppermute | solution.py:25
  19.5 0.5 collective-permute-start.5
  20.0 0.4 collective-permute-start.4
  20.5 1.6 %collective-permute-start.7 = (bf16[2,128,256]{2,1,0:T(8,128)(2,1)S(1)}, bf16[2,128,256]{2,1,0:T(8,128)(2,1)S(1)}, u32[]{:S(2)}, u32[]{:S(2)}) collective-permute-start(bf16[2,128,256]{2,1,0:T(8,128)(2,1)S(1)} %pad_maximum_fusion.3), channel_id=1, source_target_pairs={{0,16},{2,18},{4,20},{6,22},{8,24},{10,26},{12,28},{14,30},{16,0},... | collective-permute-start | bytes 393224 | tf_op jit(solution)/shard_map/ppermute | solution.py:25
  22.1 6.9 %collective-permute-done.7 = bf16[2,128,256]{2,1,0:T(8,128)(2,1)S(1)} collective-permute-done((bf16[2,128,256]{2,1,0:T(8,128)(2,1)S(1)}, bf16[2,128,256]{2,1,0:T(8,128)(2,1)S(1)}, u32[]{:S(2)}, u32[]{:S(2)}) %collective-permute-start.7) | collective-permute-done | bytes 131104 | tf_op jit(solution)/shard_map/ppermute | solution.py:25
  29.0 0.8 %collective-permute-done.3.refs_5_ = bf16[512,512]{1,0:T(8,128)(2,1)S(1)} collective-permute-done((bf16[512,512]{1,0:T(8,128)(2,1)S(1)}, bf16[512,512]{1,0:T(8,128)(2,1)S(1)}, u32[]{:S(2)}, u32[]{:S(2)}) %collective-permute-start.3) | collective-permute-done | bytes 524320 | tf_op jit(solution)/shard_map/ppermute | solution.py:25
  29.8 2.6 %collective-permute-start.10 = (bf16[4,128,256]{2,1,0:T(8,128)(2,1)S(1)}, bf16[4,128,256]{2,1,0:T(8,128)(2,1)S(1)}, u32[]{:S(2)}, u32[]{:S(2)}) collective-permute-start(bf16[4,128,256]{2,1,0:T(8,128)(2,1)S(1)} %pad_maximum_fusion.2.refs_7_), channel_id=1, source_target_pairs={{0,6},{2,4},{4,2},{6,0},{8,14},{10,12},{12,10},{14,8},{16,22},{18,... | collective-permute-start | bytes 786440 | tf_op jit(solution)/shard_map/ppermute | solution.py:25
  32.4 0.5 collective-permute-start.9
  32.9 0.3 convolution_convert_fusion.3.refs_4_
  33.3 0.3 convolution_convert_fusion.2.refs_6_
  33.6 0.4 collective-permute-start.8
  34.0 5.4 %attend.2 = (bf16[256,256]{1,0:T(8,128)(2,1)S(1)}, bf16[256,256]{1,0:T(8,128)(2,1)S(1)}, bf16[2,256,256]{2,1,0:T(8,128)(2,1)S(1)}, f32[256,512]{1,0:T(8,128)S(1)}, bf16[256,512]{1,0:T(8,128)(2,1)S(1)}) custom-call(f32[4,1,1280]{2,1,0:T(1,128)S(1)} %broadcast_in_dim.57.refs_0_, bf16[256,512]{1,0:T(8,128)(2,1)S(1)} %fusion.refs_1_, ...), custom_call_target="tpu_custom_call" | custom-call | flops 1342177280 | bytes 1835008 | tf_op jit(solution)/shard_map/attend/pallas_call | solution.py:160
  39.5 1.0 %collective-permute-start.11 = (bf16[2,256,256]{2,1,0:T(8,128)(2,1)S(1)}, bf16[2,256,256]{2,1,0:T(8,128)(2,1)S(1)}, u32[]{:S(2)}, u32[]{:S(2)}) collective-permute-start(bf16[2,256,256]{2,1,0:T(8,128)(2,1)S(1)} %get-tuple-element.33), channel_id=1, source_target_pairs={{0,8},{2,10},{4,12},{6,14},{8,0},{10,2},{12,4},{14,6},{16,24},{18,... | collective-permute-start | bytes 786440 | tf_op jit(solution)/shard_map/ppermute | solution.py:25
  40.4 3.3 %collective-permute-done.9.refs_9_ = bf16[4,128,256]{2,1,0:T(8,128)(2,1)S(1)} collective-permute-done((bf16[4,128,256]{2,1,0:T(8,128)(2,1)S(1)}, bf16[4,128,256]{2,1,0:T(8,128)(2,1)S(1)}, u32[]{:S(2)}, u32[]{:S(2)}) %collective-permute-start.9) | collective-permute-done | bytes 262176 | tf_op jit(solution)/shard_map/ppermute | solution.py:25
  43.7 0.3 collective-permute-done.8.refs_8_
  44.0 5.3 %attend.3 = (bf16[256,256]{1,0:T(8,128)(2,1)S(1)}, bf16[256,256]{1,0:T(8,128)(2,1)S(1)}, bf16[2,256,256]{2,1,0:T(8,128)(2,1)S(1)}, f32[256,512]{1,0:T(8,128)S(1)}, bf16[256,512]{1,0:T(8,128)(2,1)S(1)}) custom-call(f32[4,1,1280]{2,1,0:T(1,128)S(1)} %broadcast_in_dim.57.refs_0_, ...), custom_call_target="tpu_custom_call", output_to_operand_aliasing={{3}: (15, {}), {4}: (16, {})} | custom-call | flops 1342177280 | bytes 1835008 | tf_op jit(solution)/shard_map/attend/pallas_call | solution.py:160
  49.3 0.7 %copy-done.3 = bf16[2,256,256]{2,1,0:T(8,128)(2,1)} copy-done((bf16[2,256,256]{2,1,0:T(8,128)(2,1)}, bf16[2,256,256]{2,1,0:T(8,128)(2,1)S(1)}, u32[]{:S(2)}) %copy-start.3) | copy-done | bytes 262168
  50.1 1.5 %collective-permute-done.13 = bf16[4,4,16,512]{3,2,1,0:T(8,128)(2,1)S(1)} collective-permute-done((bf16[4,4,16,512]{3,2,1,0:T(8,128)(2,1)S(1)}, bf16[4,4,16,512]{3,2,1,0:T(8,128)(2,1)S(1)}, u32[]{:S(2)}, u32[]{:S(2)}) %collective-permute-start.13) | collective-permute-done | bytes 262176 | tf_op jit(solution)/shard_map/ppermute | solution.py:25
  51.5 0.1 fusion.37
  51.7 1.5 %collective-permute-start.15 = (bf16[4,16,512]{2,1,0:T(8,128)(2,1)S(1)}, bf16[4,16,512]{2,1,0:T(8,128)(2,1)S(1)}, u32[]{:S(2)}, u32[]{:S(2)}) collective-permute-start(bf16[4,16,512]{2,1,0:T(8,128)(2,1)S(1)} %get-tuple-element.49), channel_id=1, source_target_pairs={{0,4},{2,6},{4,0},{6,2},{8,12},{10,14},{12,8},{14,10},{16,20},{18,... | collective-permute-start | bytes 196616 | tf_op jit(solution)/shard_map/ppermute | solution.py:25
  53.2 1.5 %collective-permute-start.16 = (bf16[4,16,512]{2,1,0:T(8,128)(2,1)S(1)}, bf16[4,16,512]{2,1,0:T(8,128)(2,1)S(1)}, u32[]{:S(2)}, u32[]{:S(2)}) collective-permute-start(bf16[4,16,512]{2,1,0:T(8,128)(2,1)S(1)} %get-tuple-element.50), channel_id=1, source_target_pairs={{0,6},{2,4},{4,2},{6,0},{8,14},{10,12},{12,10},{14,8},{16,22},{18,... | collective-permute-start | bytes 196616 | tf_op jit(solution)/shard_map/ppermute | solution.py:25
  54.7 0.5 collective-permute-start.14
  55.3 0.8 %collective-permute-done.15 = bf16[4,16,512]{2,1,0:T(8,128)(2,1)S(1)} collective-permute-done((bf16[4,16,512]{2,1,0:T(8,128)(2,1)S(1)}, bf16[4,16,512]{2,1,0:T(8,128)(2,1)S(1)}, u32[]{:S(2)}, u32[]{:S(2)}) %collective-permute-start.15) | collective-permute-done | bytes 65568 | tf_op jit(solution)/shard_map/ppermute | solution.py:25
  56.0 2.6 %collective-permute-done.16 = bf16[4,16,512]{2,1,0:T(8,128)(2,1)S(1)} collective-permute-done((bf16[4,16,512]{2,1,0:T(8,128)(2,1)S(1)}, bf16[4,16,512]{2,1,0:T(8,128)(2,1)S(1)}, u32[]{:S(2)}, u32[]{:S(2)}) %collective-permute-start.16) | collective-permute-done | bytes 65568 | tf_op jit(solution)/shard_map/ppermute | solution.py:25
  58.6 0.3 collective-permute-done.14
  59.0 2.3 %collective-permute-start.17 = (bf16[16,512]{1,0:T(8,128)(2,1)S(1)}, bf16[16,512]{1,0:T(8,128)(2,1)S(1)}, u32[]{:S(2)}, u32[]{:S(2)}) collective-permute-start(bf16[16,512]{1,0:T(8,128)(2,1)S(1)} %get-tuple-element.56), channel_id=1, source_target_pairs={{0,16},{2,18},{4,20},{6,22},{8,24},{10,26},{12,28},{14,30},{16,0},... | collective-permute-start | bytes 49160 | tf_op jit(solution)/shard_map/ppermute | solution.py:25
  61.4 0.9 %collective-permute-start.19 = (bf16[16,512]{1,0:T(8,128)(2,1)S(1)}, bf16[16,512]{1,0:T(8,128)(2,1)S(1)}, u32[]{:S(2)}, u32[]{:S(2)}) collective-permute-start(bf16[16,512]{1,0:T(8,128)(2,1)S(1)} %get-tuple-element.57), channel_id=1, source_target_pairs={{0,24},{2,26},{4,28},{6,30},{8,16},{10,18},{12,20},{14,22},{16,8},... | collective-permute-start | bytes 49160 | tf_op jit(solution)/shard_map/ppermute | solution.py:25
  62.2 0.5 collective-permute-start.18
  62.7 1.2 %fusion.1 = bf16[1,256,512]{2,1,0:T(8,128)(2,1)} fusion(bf16[512,1024]{1,0:T(8,128)(2,1)S(1)} %copy-done, bf16[256,256]{1,0:T(8,128)(2,1)S(1)} %get-tuple-element.54, bf16[256,256]{1,0:T(8,128)(2,1)S(1)} %get-tuple-element.52, bf16[256,256]{1,0:T(8,128)(2,1)S(1)} %get-tuple-element.40, bf16[256,256]{1,0:T(8,128)(2,1)S(1)} %get-tuple-element.39, pred[]{:T(512)S(6)} %eq.52), kind=kOutput, calls=%fused_computation.6 | convolution fusion | flops 273022976 | bytes 1835009 | tf_op jit(solution)/shard_map/dot_general | solution.py:320
  63.9 0.9 %maximum_select_fusion = bf16[1,256,1024]{2,1,0:T(8,128)(2,1)} fusion(bf16[1,256,256]{2,1,0:T(8,128)(2,1)S(1)} %get-tuple-element.55, bf16[1,256,256]{2,1,0:T(8,128)(2,1)S(1)} %get-tuple-element.53, bf16[1,256,256]{2,1,0:T(8,128)(2,1)S(1)} %bitcast.63, bf16[1,256,256]{2,1,0:T(8,128)(2,1)S(1)} %bitcast.62, pred[]{:T(512)S(6)} %eq.52), kind=kLoop, calls=%fused_computation.9 | loop fusion | flops 4456448 | bytes 1048577 | tf_op jit(solution)/shard_map/jit(_where)/select_n | solution.py:315
  64.9 2.0 %collective-permute-done.19 = bf16[16,512]{1,0:T(8,128)(2,1)S(1)} collective-permute-done((bf16[16,512]{1,0:T(8,128)(2,1)S(1)}, bf16[16,512]{1,0:T(8,128)(2,1)S(1)}, u32[]{:S(2)}, u32[]{:S(2)}) %collective-permute-start.19) | collective-permute-done | bytes 16416 | tf_op jit(solution)/shard_map/ppermute | solution.py:25
  66.9 0.6 maximum_select_fusion.3
  (64 shorter events, 1.0 us)
Async XLA Ops:
  0.6 13.3 %copy-start = (bf16[512,1024]{1,0:T(8,128)(2,1)S(1)}, bf16[512,1024]{1,0:T(8,128)(2,1)}, u32[]{:S(2)}) copy-start(bf16[512,1024]{1,0:T(8,128)(2,1)} %param.9) | copy-start | bytes 3145732
  0.6 8.5 %copy-start.2 = (bf16[1,256,1024]{2,1,0:T(8,128)(2,1)S(1)}, bf16[1,256,1024]{2,1,0:T(8,128)(2,1)}, u32[]{:S(2)}) copy-start(bf16[1,256,1024]{2,1,0:T(8,128)(2,1)} %param.14) | copy-start | bytes 1572868
  3.5 13.3 %collective-permute-start.2 = (bf16[144,256]{1,0:T(8,128)(2,1)}, bf16[144,256]{1,0:T(8,128)(2,1)S(1)}, u32[]{:S(2)}, u32[]{:S(2)}) collective-permute-start(bf16[144,256]{1,0:T(8,128)(2,1)} %get-tuple-element.24), channel_id=1, source_target_pairs={{0,24},{2,26},{4,28},{6,30},{8,16},{10,18},{12,20},{14,22},{16,8},... | collective-permute-start | bytes 221192 | tf_op jit(solution)/shard_map/ppermute | solution.py:25
  8.5 8.3 %collective-permute-start.1 = (bf16[144,256]{1,0:T(8,128)(2,1)}, bf16[144,256]{1,0:T(8,128)(2,1)S(1)}, u32[]{:S(2)}, u32[]{:S(2)}) collective-permute-start(bf16[144,256]{1,0:T(8,128)(2,1)} %get-tuple-element.22), channel_id=1, source_target_pairs={{0,16},{2,18},{4,20},{6,22},{8,24},{10,26},{12,28},{14,30},{16,0},... | collective-permute-start | bytes 221192 | tf_op jit(solution)/shard_map/ppermute | solution.py:25
  8.5 8.2 %collective-permute-start = (bf16[272,256]{1,0:T(8,128)(2,1)}, bf16[272,256]{1,0:T(8,128)(2,1)S(1)}, u32[]{:S(2)}, u32[]{:S(2)}) collective-permute-start(bf16[272,256]{1,0:T(8,128)(2,1)} %get-tuple-element.23), channel_id=1, source_target_pairs={{0,8},{2,10},{4,12},{6,14},{8,0},{10,2},{12,4},{14,6},{16,24},{18,... | collective-permute-start | bytes 417800 | tf_op jit(solution)/shard_map/ppermute | solution.py:25
  9.1 1.0 %copy-start.1 = (bf16[1,256,512]{2,1,0:T(8,128)(2,1)S(1)}, bf16[1,256,512]{2,1,0:T(8,128)(2,1)}, u32[]{:S(2)}) copy-start(bf16[1,256,512]{2,1,0:T(8,128)(2,1)} %param.8) | copy-start | bytes 786436
  10.1 1.6 %copy-start.8 = (s32[16]{0:T(128)S(1)}, s32[16]{0:T(128)}, u32[]{:S(2)}) copy-start(s32[16]{0:T(128)} %constant.93.clone) | copy-start | bytes 196
  10.1 19.7 %collective-permute-start.3 = (bf16[512,512]{1,0:T(8,128)(2,1)S(1)}, bf16[512,512]{1,0:T(8,128)(2,1)S(1)}, u32[]{:S(2)}, u32[]{:S(2)}) collective-permute-start(bf16[512,512]{1,0:T(8,128)(2,1)S(1)} %pad_maximum_fusion), channel_id=1, source_target_pairs={{0,8},{2,10},{4,12},{6,14},{8,0},{10,2},{12,4},{14,6},{16,24},{18,... | collective-permute-start | bytes 1572872 | tf_op jit(solution)/shard_map/ppermute | solution.py:25
  11.6 0.7 %copy-start.7 = (s32[1,8,16]{2,1,0:T(8,128)S(1)}, s32[1,8,16]{2,1,0:T(8,128)}, u32[]{:S(2)}) copy-start(s32[1,8,16]{2,1,0:T(8,128)} %blocks_ref.1) | copy-start | bytes 1540
  14.3 2.5 %copy-start.5 = (bf16[144,256]{1,0:T(8,128)(2,1)S(1)}, bf16[144,256]{1,0:T(8,128)(2,1)}, u32[]{:S(2)}) copy-start(bf16[144,256]{1,0:T(8,128)(2,1)} %get-tuple-element.22) | copy-start | bytes 221188
  16.9 3.6 %copy-start.6 = (bf16[128,256]{1,0:T(8,128)(2,1)S(1)}, bf16[128,256]{1,0:T(8,128)(2,1)}, u32[]{:S(2)}) copy-start(bf16[128,256]{1,0:T(8,128)(2,1)} %get-tuple-element.27) | copy-start | bytes 196612
  16.9 16.7 %collective-permute-start.6 = (bf16[4,144,256]{2,1,0:T(8,128)(2,1)S(1)}, bf16[4,144,256]{2,1,0:T(8,128)(2,1)S(1)}, u32[]{:S(2)}, u32[]{:S(2)}) collective-permute-start(bf16[4,144,256]{2,1,0:T(8,128)(2,1)S(1)} %pad_maximum_fusion.1.refs_7_.refs_11_), channel_id=1, source_target_pairs={{0,6},{2,4},{4,2},{6,0},{8,14},{10,12},{12,10},{14,8},{16,22},{18,... | collective-permute-start | bytes 884744 | tf_op jit(solution)/shard_map/ppermute | solution.py:25
  19.5 14.5 %collective-permute-start.5 = (bf16[4,144,256]{2,1,0:T(8,128)(2,1)S(1)}, bf16[4,144,256]{2,1,0:T(8,128)(2,1)S(1)}, u32[]{:S(2)}, u32[]{:S(2)}) collective-permute-start(bf16[4,144,256]{2,1,0:T(8,128)(2,1)S(1)} %pad_maximum_fusion.1.refs_7_.refs_11_), channel_id=1, source_target_pairs={{0,4},{2,6},{4,0},{6,2},{8,12},{10,14},{12,8},{14,10},{16,20},{18,... | collective-permute-start | bytes 884744 | tf_op jit(solution)/shard_map/ppermute | solution.py:25
  20.0 14.0 %collective-permute-start.4 = (bf16[4,144,256]{2,1,0:T(8,128)(2,1)S(1)}, bf16[4,144,256]{2,1,0:T(8,128)(2,1)S(1)}, u32[]{:S(2)}, u32[]{:S(2)}) collective-permute-start(bf16[4,144,256]{2,1,0:T(8,128)(2,1)S(1)} %pad_maximum_fusion.1.refs_7_.refs_11_), channel_id=1, source_target_pairs={{0,2},{2,0},{4,6},{6,4},{8,10},{10,8},{12,14},{14,12},{16,18},{18,... | collective-permute-start | bytes 884744 | tf_op jit(solution)/shard_map/ppermute | solution.py:25
  20.5 8.5 %collective-permute-start.7 = (bf16[2,128,256]{2,1,0:T(8,128)(2,1)S(1)}, bf16[2,128,256]{2,1,0:T(8,128)(2,1)S(1)}, u32[]{:S(2)}, u32[]{:S(2)}) collective-permute-start(bf16[2,128,256]{2,1,0:T(8,128)(2,1)S(1)} %pad_maximum_fusion.3), channel_id=1, source_target_pairs={{0,16},{2,18},{4,20},{6,22},{8,24},{10,26},{12,28},{14,30},{16,0},... | collective-permute-start | bytes 393224 | tf_op jit(solution)/shard_map/ppermute | solution.py:25
  29.8 10.6 %collective-permute-start.10 = (bf16[4,128,256]{2,1,0:T(8,128)(2,1)S(1)}, bf16[4,128,256]{2,1,0:T(8,128)(2,1)S(1)}, u32[]{:S(2)}, u32[]{:S(2)}) collective-permute-start(bf16[4,128,256]{2,1,0:T(8,128)(2,1)S(1)} %pad_maximum_fusion.2.refs_7_), channel_id=1, source_target_pairs={{0,6},{2,4},{4,2},{6,0},{8,14},{10,12},{12,10},{14,8},{16,22},{18,... | collective-permute-start | bytes 786440 | tf_op jit(solution)/shard_map/ppermute | solution.py:25
  32.4 11.2 %collective-permute-start.9 = (bf16[4,128,256]{2,1,0:T(8,128)(2,1)S(1)}, bf16[4,128,256]{2,1,0:T(8,128)(2,1)S(1)}, u32[]{:S(2)}, u32[]{:S(2)}) collective-permute-start(bf16[4,128,256]{2,1,0:T(8,128)(2,1)S(1)} %pad_maximum_fusion.2.refs_7_), channel_id=1, source_target_pairs={{0,4},{2,6},{4,0},{6,2},{8,12},{10,14},{12,8},{14,10},{16,20},{18,... | collective-permute-start | bytes 786440 | tf_op jit(solution)/shard_map/ppermute | solution.py:25
  33.6 10.4 %collective-permute-start.8 = (bf16[4,128,256]{2,1,0:T(8,128)(2,1)S(1)}, bf16[4,128,256]{2,1,0:T(8,128)(2,1)S(1)}, u32[]{:S(2)}, u32[]{:S(2)}) collective-permute-start(bf16[4,128,256]{2,1,0:T(8,128)(2,1)S(1)} %pad_maximum_fusion.2.refs_7_), channel_id=1, source_target_pairs={{0,2},{2,0},{4,6},{6,4},{8,10},{10,8},{12,14},{14,12},{16,18},{18,... | collective-permute-start | bytes 786440 | tf_op jit(solution)/shard_map/ppermute | solution.py:25
  39.5 9.8 %collective-permute-start.11 = (bf16[2,256,256]{2,1,0:T(8,128)(2,1)S(1)}, bf16[2,256,256]{2,1,0:T(8,128)(2,1)S(1)}, u32[]{:S(2)}, u32[]{:S(2)}) collective-permute-start(bf16[2,256,256]{2,1,0:T(8,128)(2,1)S(1)} %get-tuple-element.33), channel_id=1, source_target_pairs={{0,8},{2,10},{4,12},{6,14},{8,0},{10,2},{12,4},{14,6},{16,24},{18,... | collective-permute-start | bytes 786440 | tf_op jit(solution)/shard_map/ppermute | solution.py:25
  49.3 0.7 %copy-start.3 = (bf16[2,256,256]{2,1,0:T(8,128)(2,1)}, bf16[2,256,256]{2,1,0:T(8,128)(2,1)S(1)}, u32[]{:S(2)}) copy-start(bf16[2,256,256]{2,1,0:T(8,128)(2,1)S(1)} %collective-permute-done.11) | copy-start | bytes 786436
  50.0 1.5 %collective-permute-start.13 = (bf16[4,4,16,512]{3,2,1,0:T(8,128)(2,1)S(1)}, bf16[4,4,16,512]{3,2,1,0:T(8,128)(2,1)S(1)}, u32[]{:S(2)}, u32[]{:S(2)}) collective-permute-start(bf16[4,4,16,512]{3,2,1,0:T(8,128)(2,1)S(1)} %bitcast.64), channel_id=1, source_target_pairs={{0,1},{1,0},{2,3},{3,2},{4,5},{5,4},{6,7},{7,6},{8,9},{9,8},{10,11... | collective-permute-start | bytes 786440 | tf_op jit(solution)/shard_map/ppermute | solution.py:25
  50.0 9.0 %collective-permute-start.12 = (bf16[2,256,256]{2,1,0:T(8,128)(2,1)S(1)}, bf16[2,256,256]{2,1,0:T(8,128)(2,1)S(1)}, u32[]{:S(2)}, u32[]{:S(2)}) collective-permute-start(bf16[2,256,256]{2,1,0:T(8,128)(2,1)S(1)} %get-tuple-element.34), channel_id=1, source_target_pairs={{0,8},{2,10},{4,12},{6,14},{8,0},{10,2},{12,4},{14,6},{16,24},{18,... | collective-permute-start | bytes 786440 | tf_op jit(solution)/shard_map/ppermute | solution.py:25
  51.6 3.6 %copy-start.4 = (bf16[2,256,256]{2,1,0:T(8,128)(2,1)S(1)}, bf16[2,256,256]{2,1,0:T(8,128)(2,1)}, u32[]{:S(2)}) copy-start(bf16[2,256,256]{2,1,0:T(8,128)(2,1)} %copy-done.3) | copy-start | bytes 786436
  51.7 4.3 %collective-permute-start.15 = (bf16[4,16,512]{2,1,0:T(8,128)(2,1)S(1)}, bf16[4,16,512]{2,1,0:T(8,128)(2,1)S(1)}, u32[]{:S(2)}, u32[]{:S(2)}) collective-permute-start(bf16[4,16,512]{2,1,0:T(8,128)(2,1)S(1)} %get-tuple-element.49), channel_id=1, source_target_pairs={{0,4},{2,6},{4,0},{6,2},{8,12},{10,14},{12,8},{14,10},{16,20},{18,... | collective-permute-start | bytes 196616 | tf_op jit(solution)/shard_map/ppermute | solution.py:25
  53.2 5.5 %collective-permute-start.16 = (bf16[4,16,512]{2,1,0:T(8,128)(2,1)S(1)}, bf16[4,16,512]{2,1,0:T(8,128)(2,1)S(1)}, u32[]{:S(2)}, u32[]{:S(2)}) collective-permute-start(bf16[4,16,512]{2,1,0:T(8,128)(2,1)S(1)} %get-tuple-element.50), channel_id=1, source_target_pairs={{0,6},{2,4},{4,2},{6,0},{8,14},{10,12},{12,10},{14,8},{16,22},{18,... | collective-permute-start | bytes 196616 | tf_op jit(solution)/shard_map/ppermute | solution.py:25
  54.7 4.3 %collective-permute-start.14 = (bf16[4,16,512]{2,1,0:T(8,128)(2,1)S(1)}, bf16[4,16,512]{2,1,0:T(8,128)(2,1)S(1)}, u32[]{:S(2)}, u32[]{:S(2)}) collective-permute-start(bf16[4,16,512]{2,1,0:T(8,128)(2,1)S(1)} %get-tuple-element.51), channel_id=1, source_target_pairs={{0,2},{2,0},{4,6},{6,4},{8,10},{10,8},{12,14},{14,12},{16,18},{18,... | collective-permute-start | bytes 196616 | tf_op jit(solution)/shard_map/ppermute | solution.py:25
  59.0 5.8 %collective-permute-start.17 = (bf16[16,512]{1,0:T(8,128)(2,1)S(1)}, bf16[16,512]{1,0:T(8,128)(2,1)S(1)}, u32[]{:S(2)}, u32[]{:S(2)}) collective-permute-start(bf16[16,512]{1,0:T(8,128)(2,1)S(1)} %get-tuple-element.56), channel_id=1, source_target_pairs={{0,16},{2,18},{4,20},{6,22},{8,24},{10,26},{12,28},{14,30},{16,0},... | collective-permute-start | bytes 49160 | tf_op jit(solution)/shard_map/ppermute | solution.py:25
  61.4 5.5 %collective-permute-start.19 = (bf16[16,512]{1,0:T(8,128)(2,1)S(1)}, bf16[16,512]{1,0:T(8,128)(2,1)S(1)}, u32[]{:S(2)}, u32[]{:S(2)}) collective-permute-start(bf16[16,512]{1,0:T(8,128)(2,1)S(1)} %get-tuple-element.57), channel_id=1, source_target_pairs={{0,24},{2,26},{4,28},{6,30},{8,16},{10,18},{12,20},{14,22},{16,8},... | collective-permute-start | bytes 49160 | tf_op jit(solution)/shard_map/ppermute | solution.py:25
  62.2 4.7 %collective-permute-start.18 = (bf16[16,512]{1,0:T(8,128)(2,1)S(1)}, bf16[16,512]{1,0:T(8,128)(2,1)S(1)}, u32[]{:S(2)}, u32[]{:S(2)}) collective-permute-start(bf16[16,512]{1,0:T(8,128)(2,1)S(1)} %get-tuple-element.58), channel_id=1, source_target_pairs={{0,8},{2,10},{4,12},{6,14},{8,0},{10,2},{12,4},{14,6},{16,24},{18,... | collective-permute-start | bytes 49160 | tf_op jit(solution)/shard_map/ppermute | solution.py:25

commit v7 on v6

--- a/solution.py
+++ b/solution.py
@@ -88,10 +88,10 @@
     out_ref, dq_ref, away_ref, keep_ref, send_ref = refs[-5:]
     head_dim = out_ref.shape[1]
     keys = jnp.concatenate(
-        [r[:, :, :head_dim].reshape(-1, head_dim) for r in piece_refs], axis=0
+        [r[..., :head_dim].reshape(-1, head_dim) for r in piece_refs], axis=0
     )
     values = jnp.concatenate(
-        [r[:, :, head_dim:].reshape(-1, head_dim) for r in piece_refs], axis=0
+        [r[..., head_dim:].reshape(-1, head_dim) for r in piece_refs], axis=0
     )
     bias = bias_ref[0]
     cols = (slice(0, fine_width), slice(fine_width, keys.shape[0]))
@@ -131,8 +131,9 @@
     half = bias.shape[0]
     width = own_side[0].shape[1]
     head_dim = width // half
-    fine_width = sum(p.shape[0] for p in pieces) * BLK
-    room = (bias.shape[-1] - fine_width) // sum(p.shape[0] for p in pieces)
+    sources = lax.axis_size("hist")
+    fine_width = sources * BLK
+    room = bias.shape[-1] // sources - BLK
     kept = depth // share
     in_specs = [pl.BlockSpec((1,) + bias.shape[1:], lambda i: (first + i, 0, 0))]
     for at in (0, own_side[1].shape[0] // rows - 1), (0, their_side[1].shape[0] // rows - 1):
@@ -141,12 +142,16 @@
             pl.BlockSpec((rows, head_dim), lambda i, at=at[1]: (at, first + i)),
             pl.BlockSpec((depth, rows), lambda i: (0, 0)),
         ]
+    rest = sources // QUAD
     in_specs += [
-        pl.BlockSpec((p.shape[0], BLK, 2 * head_dim), lambda i: (0, i, 0)) for p in pieces
+        pl.BlockSpec((rest * BLK, 2 * head_dim), lambda i: (i, 0))
+        if p.ndim == 2
+        else pl.BlockSpec((rest, BLK, 2 * head_dim), lambda i: (0, i, 0))
+        for p in pieces
     ]
     in_specs += [
-        pl.BlockSpec((p.shape[0], room, 2 * head_dim), lambda i: (0, CUT * BLK // room, 0))
-        for p in summaries
+        pl.BlockSpec((rest * room, 2 * head_dim), lambda i: (CUT * BLK // room, 0))
+        for _ in summaries
     ]
     args = [bias, *own_side, *their_side, *pieces, *summaries]
     aliases = {}
@@ -177,7 +182,7 @@
         ),
         input_output_aliases=aliases,
         compiler_params=pltpu.CompilerParams(
-            vmem_limit_bytes=min(VMEM_LIMIT, sum(p.shape[0] for p in pieces) * VMEM_SOURCE)
+            vmem_limit_bytes=min(VMEM_LIMIT, sources * VMEM_SOURCE)
         ),
         cost_estimate=pl.CostEstimate(
             flops=16 * count * rows * columns * head_dim,
@@ -233,7 +238,10 @@
             for k in range(PAIR, n_hist // QUAD)
         ]
     )
-    near = gather_quad(column_near)
+    packed = column_near[:, : CUT * BLK].reshape(-1, CUT, BLK, 2 * head_dim)
+    packed = packed.transpose(1, 0, 2, 3).reshape(-1, 2 * head_dim)
+    lines = column_near[:, CUT * BLK : CUT * BLK + count].reshape(-1, 2 * head_dim)
+    near = gather_quad(jnp.concatenate([packed, lines]))
     pair_late = after(jnp.stack([keep_late, came[near_rows:]]), column_near)
     column_late = jnp.concatenate(
         [pair_late]
@@ -259,7 +267,7 @@
     spots = jnp.arange(BLK, dtype=jnp.int32)
     live = (listed[:, :, None] >= 0) & (listed[:, :, None] * BLK + spots < lengths[0])
     fine_bias = jnp.where(live, 0.0, DEAD).astype(F32).reshape(half, -1)
-    line = jnp.arange(room, dtype=jnp.int32)
+    line = jnp.arange(count, dtype=jnp.int32)
     names = source[:, None] * blk_dev + line[None, :] % blk_dev
     own_line = (line // blk_dev)[None, :] == jnp.arange(half, dtype=jnp.int32)[:, None]
     coarse_live = own_line[:, None, :] & (names * BLK < lengths[0])[None]
@@ -282,7 +290,7 @@
 
     own_side = (project(targets[0]), grad_keep, reorder(targets[0]))
     their_side = (project(theirs[:rows]), theirs, reorder(theirs[:rows]))
-    late = gather_quad(after(column_late, theirs))
+    late = gather_quad(column_late)
     fixed = (bias, own_side, their_side, near)
     out_near, dq_near, away_near, *weight = attend(0, CUT, *fixed, near, n_batch, None)
     out_late, dq_late, away_late, kept, sent = attend(
@@ -291,7 +299,7 @@
 
     back_near = swap(away_near, "hist", QUAD)
     back_late = swap(away_late, "hist", QUAD)
-    sent = after(sent, back_near)
+    kept = after(kept, back_near)
     kept = kept.reshape(QUAD, n_hist // QUAD, share, wide)
     sent = sent.reshape(n_batch - 1, QUAD, n_hist // QUAD, share, wide)
     total = kept

time: 67.8 us -> 66.9 us (0.987)
  waiting for transfers between devices: 20.9 us -> 18 us
  starting transfers between devices: 24.1 us -> 26.4 us
    ppermute x20, waiting for transfers between devices: 20.9 us -> 18 us  [swap(): return lax.ppermute(array, axis, [(i, i ^ mask) for i in range(size)])]
    ppermute x20, starting transfers between devices: 24.1 us -> 26.4 us  [swap(): return lax.ppermute(array, axis, [(i, i ^ mask) for i in range(size)])]
    squeeze x2, local copies, waits for them, and re-layouts: 0.04 us -> 1 us  [join(): back = [back_near[index], back_late[index]]]
    unnamed x18 -> x19, local copies, waits for them, and re-layouts: 2.32 us -> 1.64 us
  transfers between devices with their start and end apart: 20 -> 20, of which waited for: 10 -> 7; matrix products, arithmetic and copies ran while one was open for 7% -> 9% of each run, Pallas kernels for 16% -> 15%
where the time goes in v7:
time: 66.9 us; the launch traced here: 66.7 us
  starting transfers between devices  26.4 us (39%)
  waiting for transfers between devices  18 us (27%)
  Pallas kernels  12.2 us (18%)
  local copies, waits for them, and re-layouts  3.69 us (6%)
  matrix products  2.54 us (4%)
  other arithmetic  2.15 us (3%)
  between operations  1.79 us (3%)
    ppermute x20, starting transfers between devices, swap(): return lax.ppermute(array, axis, [(i, i ^ mask) for i in range(size)])  26.4 us
    ppermute x20, waiting for transfers between devices, swap(): return lax.ppermute(array, axis, [(i, i ^ mask) for i in range(size)])  18 us
    pallas_call x2, Pallas kernels, attend(): pl.pallas_call(functools.partial(attend_kernel, len(pieces) + len(summari...  10.1 us
    pallas_call x1, Pallas kernels, shards(): pl.pallas_call(functools.partial(select_kernel, CUT), in_specs=[pl.BlockS...  2.07 us
    unnamed x19, local copies, waits for them, and re-layouts  1.64 us
  transfers between devices with their start and end apart: 20, of which 7 were waited for; matrix products, arithmetic and copies ran while one was open for 9% of the time, Pallas kernels for 15%

profile of v7, /device:TPU:0, one launch (start us, length us, event | category | flops | bytes accessed | tf_op | source)
XLA Modules:
  0.0 66.7 jit_solution(6050090750404057294)
XLA Ops:
  1.4 2.1 %select.34 = (bf16[144,256]{1,0:T(8,128)(2,1)}, bf16[128,256]{1,0:T(8,128)(2,1)}, bf16[144,256]{1,0:T(8,128)(2,1)}, bf16[272,256]{1,0:T(8,128)(2,1)}) custom-call(s32[1,8,16]{2,1,0:T(8,128)} %blocks_ref.1, s32[1]{0:T(128)} %copy.23.lengths_ref, bf16[1,128,1024]{2,1,0:T(8,128)(2,1)} %keys_ref.1, bf16[1,128,1024]{2,1,0:T(8,128)(2,1)} %values_ref.1), custom_call_target="tpu_custom_call" | custom-call | tf_op jit(solution)/shard_map/select/pallas_call | solution.py:218
  3.5 5.0 %collective-permute-start.2 = (bf16[144,256]{1,0:T(8,128)(2,1)}, bf16[144,256]{1,0:T(8,128)(2,1)S(1)}, u32[]{:S(2)}, u32[]{:S(2)}) collective-permute-start(bf16[144,256]{1,0:T(8,128)(2,1)} %get-tuple-element.23), channel_id=1, source_target_pairs={{0,24},{2,26},{4,28},{6,30},{8,16},{10,18},{12,20},{14,22},{16,8},... | collective-permute-start | bytes 221192 | tf_op jit(solution)/shard_map/ppermute | solution.py:25
  8.5 0.6 collective-permute-start
  9.2 0.9 %copy-done.3 = bf16[1,256,512]{2,1,0:T(8,128)(2,1)S(1)} copy-done((bf16[1,256,512]{2,1,0:T(8,128)(2,1)S(1)}, bf16[1,256,512]{2,1,0:T(8,128)(2,1)}, u32[]{:S(2)}) %copy-start.3) | copy-done | bytes 262168
  10.1 1.5 %collective-permute-start.3 = (bf16[512,512]{1,0:T(8,128)(2,1)S(1)}, bf16[512,512]{1,0:T(8,128)(2,1)S(1)}, u32[]{:S(2)}, u32[]{:S(2)}) collective-permute-start(bf16[512,512]{1,0:T(8,128)(2,1)S(1)} %pad_maximum_fusion), channel_id=1, source_target_pairs={{0,8},{2,10},{4,12},{6,14},{8,0},{10,2},{12,4},{14,6},{16,24},{18,... | collective-permute-start | bytes 1572872 | tf_op jit(solution)/shard_map/ppermute | solution.py:25
  11.6 0.7 %copy-done.7 = s32[1,8,16]{2,1,0:T(8,128)S(1)} copy-done((s32[1,8,16]{2,1,0:T(8,128)S(1)}, s32[1,8,16]{2,1,0:T(8,128)}, u32[]{:S(2)}) %copy-start.7) | copy-done | bytes 536
  12.3 0.1 select_reduce_fusion
  12.5 0.1 mul.60
  12.7 0.1 and.82
  12.8 0.1 and.86
  12.9 0.1 add.146
  13.1 0.1 add.143
  13.3 0.1 add.155
  13.5 0.1 add.137
  13.6 0.4 convolution_convert_fusion.4.refs_3_
  13.9 0.3 fusion.refs_1_
  14.3 2.5 %collective-permute-done = bf16[272,256]{1,0:T(8,128)(2,1)S(1)} collective-permute-done((bf16[272,256]{1,0:T(8,128)(2,1)}, bf16[272,256]{1,0:T(8,128)(2,1)S(1)}, u32[]{:S(2)}, u32[]{:S(2)}) %collective-permute-start) | collective-permute-done | bytes 139296 | tf_op jit(solution)/shard_map/ppermute | solution.py:25
  17.0 2.6 %collective-permute-start.6 = (bf16[544,256]{1,0:T(8,128)(2,1)S(1)}, bf16[544,256]{1,0:T(8,128)(2,1)S(1)}, u32[]{:S(2)}, u32[]{:S(2)}) collective-permute-start(bf16[544,256]{1,0:T(8,128)(2,1)S(1)} %pad_maximum_fusion.2.refs_7_.refs_11_), channel_id=1, source_target_pairs={{0,6},{2,4},{4,2},{6,0},{8,14},{10,12},{12,10},{14,8},{16,22},{18,... | collective-permute-start | bytes 835592 | tf_op jit(solution)/shard_map/ppermute | solution.py:25
  19.6 0.5 collective-permute-start.5
  20.1 0.4 collective-permute-start.4
  20.6 1.6 %collective-permute-start.7 = (bf16[2,128,256]{2,1,0:T(8,128)(2,1)S(1)}, bf16[2,128,256]{2,1,0:T(8,128)(2,1)S(1)}, u32[]{:S(2)}, u32[]{:S(2)}) collective-permute-start(bf16[2,128,256]{2,1,0:T(8,128)(2,1)S(1)} %pad_maximum_fusion.3), channel_id=1, source_target_pairs={{0,16},{2,18},{4,20},{6,22},{8,24},{10,26},{12,28},{14,30},{16,0},... | collective-permute-start | bytes 393224 | tf_op jit(solution)/shard_map/ppermute | solution.py:25
  22.2 6.8 %collective-permute-done.7 = bf16[2,128,256]{2,1,0:T(8,128)(2,1)S(1)} collective-permute-done((bf16[2,128,256]{2,1,0:T(8,128)(2,1)S(1)}, bf16[2,128,256]{2,1,0:T(8,128)(2,1)S(1)}, u32[]{:S(2)}, u32[]{:S(2)}) %collective-permute-start.7) | collective-permute-done | bytes 131104 | tf_op jit(solution)/shard_map/ppermute | solution.py:25
  28.9 2.5 %collective-permute-start.10 = (bf16[4,128,256]{2,1,0:T(8,128)(2,1)S(1)}, bf16[4,128,256]{2,1,0:T(8,128)(2,1)S(1)}, u32[]{:S(2)}, u32[]{:S(2)}) collective-permute-start(bf16[4,128,256]{2,1,0:T(8,128)(2,1)S(1)} %constant_dynamic-update-slice_fusion.refs_7_), channel_id=1, source_target_pairs={{0,6},{2,4},{4,2},{6,0},{8,14},{10,12},{12,10},{14,8},{16,22},{18,... | collective-permute-start | bytes 786440 | tf_op jit(solution)/shard_map/ppermute | solution.py:25
  31.5 0.5 collective-permute-start.9
  32.0 0.4 convolution_convert_fusion.2.refs_6_
  32.3 1.1 %collective-permute-start.8 = (bf16[4,128,256]{2,1,0:T(8,128)(2,1)S(1)}, bf16[4,128,256]{2,1,0:T(8,128)(2,1)S(1)}, u32[]{:S(2)}, u32[]{:S(2)}) collective-permute-start(bf16[4,128,256]{2,1,0:T(8,128)(2,1)S(1)} %constant_dynamic-update-slice_fusion.refs_7_), channel_id=1, source_target_pairs={{0,2},{2,0},{4,6},{6,4},{8,10},{10,8},{12,14},{14,12},{16,18},{18,... | collective-permute-start | bytes 786440 | tf_op jit(solution)/shard_map/ppermute | solution.py:25
  33.4 0.3 convolution_convert_fusion.3.refs_4_
  33.8 5.0 %attend.2 = (bf16[256,256]{1,0:T(8,128)(2,1)S(1)}, bf16[256,256]{1,0:T(8,128)(2,1)S(1)}, bf16[2,256,256]{2,1,0:T(8,128)(2,1)S(1)}, f32[256,512]{1,0:T(8,128)S(1)}, bf16[256,512]{1,0:T(8,128)(2,1)S(1)}) custom-call(f32[4,1,1152]{2,1,0:T(1,128)S(1)} %broadcast_in_dim.57.refs_0_, bf16[256,512]{1,0:T(8,128)(2,1)S(1)} %fusion.refs_1_, ...), custom_call_target="tpu_custom_call" | custom-call | flops 1207959552 | bytes 1703936 | tf_op jit(solution)/shard_map/attend/pallas_call | solution.py:165
  38.8 1.2 %collective-permute-start.11 = (bf16[2,256,256]{2,1,0:T(8,128)(2,1)S(1)}, bf16[2,256,256]{2,1,0:T(8,128)(2,1)}, u32[]{:S(2)}, u32[]{:S(2)}) collective-permute-start(bf16[2,256,256]{2,1,0:T(8,128)(2,1)S(1)} %get-tuple-element.31), channel_id=1, source_target_pairs={{0,8},{2,10},{4,12},{6,14},{8,0},{10,2},{12,4},{14,6},{16,24},{18,... | collective-permute-start | bytes 786440 | tf_op jit(solution)/shard_map/ppermute | solution.py:25
  40.0 2.7 %collective-permute-done.9.refs_9_ = bf16[4,128,256]{2,1,0:T(8,128)(2,1)S(1)} collective-permute-done((bf16[4,128,256]{2,1,0:T(8,128)(2,1)S(1)}, bf16[4,128,256]{2,1,0:T(8,128)(2,1)S(1)}, u32[]{:S(2)}, u32[]{:S(2)}) %collective-permute-start.9) | collective-permute-done | bytes 262176 | tf_op jit(solution)/shard_map/ppermute | solution.py:25
  42.7 0.1 collective-permute-done.8.refs_8_
  42.8 5.1 %attend.3 = (bf16[256,256]{1,0:T(8,128)(2,1)S(1)}, bf16[256,256]{1,0:T(8,128)(2,1)S(1)}, bf16[2,256,256]{2,1,0:T(8,128)(2,1)S(1)}, f32[256,512]{1,0:T(8,128)S(1)}, bf16[256,512]{1,0:T(8,128)(2,1)S(1)}) custom-call(f32[4,1,1152]{2,1,0:T(1,128)S(1)} %broadcast_in_dim.57.refs_0_, ...), custom_call_target="tpu_custom_call", output_to_operand_aliasing={{3}: (15, {}), {4}: (16, {})} | custom-call | flops 1207959552 | bytes 1703936 | tf_op jit(solution)/shard_map/attend/pallas_call | solution.py:165
  48.0 0.1 collective-permute-start.13
  48.0 1.1 %collective-permute-start.12 = (bf16[2,256,256]{2,1,0:T(8,128)(2,1)S(1)}, bf16[2,256,256]{2,1,0:T(8,128)(2,1)S(1)}, u32[]{:S(2)}, u32[]{:S(2)}) collective-permute-start(bf16[2,256,256]{2,1,0:T(8,128)(2,1)S(1)} %get-tuple-element.32), channel_id=1, source_target_pairs={{0,8},{2,10},{4,12},{6,14},{8,0},{10,2},{12,4},{14,6},{16,24},{18,... | collective-permute-start | bytes 786440 | tf_op jit(solution)/shard_map/ppermute | solution.py:25
  49.1 0.4 collective-permute-done.13
  49.6 0.1 fusion.37
  49.7 1.5 %collective-permute-start.15 = (bf16[4,16,512]{2,1,0:T(8,128)(2,1)S(1)}, bf16[4,16,512]{2,1,0:T(8,128)(2,1)S(1)}, u32[]{:S(2)}, u32[]{:S(2)}) collective-permute-start(bf16[4,16,512]{2,1,0:T(8,128)(2,1)S(1)} %get-tuple-element.47), channel_id=1, source_target_pairs={{0,4},{2,6},{4,0},{6,2},{8,12},{10,14},{12,8},{14,10},{16,20},{18,... | collective-permute-start | bytes 196616 | tf_op jit(solution)/shard_map/ppermute | solution.py:25
  51.2 1.5 %collective-permute-start.16 = (bf16[4,16,512]{2,1,0:T(8,128)(2,1)S(1)}, bf16[4,16,512]{2,1,0:T(8,128)(2,1)S(1)}, u32[]{:S(2)}, u32[]{:S(2)}) collective-permute-start(bf16[4,16,512]{2,1,0:T(8,128)(2,1)S(1)} %get-tuple-element.48), channel_id=1, source_target_pairs={{0,6},{2,4},{4,2},{6,0},{8,14},{10,12},{12,10},{14,8},{16,22},{18,... | collective-permute-start | bytes 196616 | tf_op jit(solution)/shard_map/ppermute | solution.py:25
  52.7 0.5 collective-permute-start.14
  53.2 1.0 %slice_bitcast_fusion.1 = (bf16[256,256]{1,0:T(8,128)(2,1)S(1)}, bf16[1,256,256]{2,1,0:T(8,128)(2,1)S(1)}) fusion(bf16[2,256,256]{2,1,0:T(8,128)(2,1)} %collective-permute-done.11), kind=kLoop, calls=%fused_computation.40 | loop fusion | bytes 524288 | tf_op jit(solution)/shard_map/squeeze | solution.py:322
  54.2 2.7 %collective-permute-done.16 = bf16[4,16,512]{2,1,0:T(8,128)(2,1)S(1)} collective-permute-done((bf16[4,16,512]{2,1,0:T(8,128)(2,1)S(1)}, bf16[4,16,512]{2,1,0:T(8,128)(2,1)S(1)}, u32[]{:S(2)}, u32[]{:S(2)}) %collective-permute-start.16) | collective-permute-done | bytes 65568 | tf_op jit(solution)/shard_map/ppermute | solution.py:25
  57.1 3.5 %collective-permute-start.17 = (bf16[16,512]{1,0:T(8,128)(2,1)S(1)}, bf16[16,512]{1,0:T(8,128)(2,1)S(1)}, u32[]{:S(2)}, u32[]{:S(2)}) collective-permute-start(bf16[16,512]{1,0:T(8,128)(2,1)S(1)} %get-tuple-element.54), channel_id=1, source_target_pairs={{0,16},{2,18},{4,20},{6,22},{8,24},{10,26},{12,28},{14,30},{16,0},... | collective-permute-start | bytes 49160 | tf_op jit(solution)/shard_map/ppermute | solution.py:25
  60.5 0.1 collective-permute-start.19
  60.6 0.5 collective-permute-start.18
  61.2 1.2 %fusion.1 = bf16[1,256,512]{2,1,0:T(8,128)(2,1)} fusion(bf16[512,1024]{1,0:T(8,128)(2,1)S(1)} %copy-done, bf16[256,256]{1,0:T(8,128)(2,1)S(1)} %get-tuple-element.52, bf16[256,256]{1,0:T(8,128)(2,1)S(1)} %get-tuple-element.50, bf16[256,256]{1,0:T(8,128)(2,1)S(1)} %get-tuple-element.38, bf16[256,256]{1,0:T(8,128)(2,1)S(1)} %copy-done.2, pred[]{:T(512)S(6)} %eq.52), kind=kOutput, calls=%fused_computation.6 | convolution fusion | flops 273022976 | bytes 1835009 | tf_op jit(solution)/shard_map/dot_general | solution.py:328
  62.4 0.9 %maximum_select_fusion = bf16[1,256,1024]{2,1,0:T(8,128)(2,1)} fusion(bf16[1,256,256]{2,1,0:T(8,128)(2,1)S(1)} %get-tuple-element.53, bf16[1,256,256]{2,1,0:T(8,128)(2,1)S(1)} %get-tuple-element.51, bf16[1,256,256]{2,1,0:T(8,128)(2,1)S(1)} %bitcast.72, bf16[1,256,256]{2,1,0:T(8,128)(2,1)S(1)} %bitcast.71, pred[]{:T(512)S(6)} %eq.52), kind=kLoop, calls=%fused_computation.9 | loop fusion | flops 4456448 | bytes 1048577 | tf_op jit(solution)/shard_map/jit(_where)/select_n | solution.py:323
  63.3 2.7 %collective-permute-done.19 = bf16[16,512]{1,0:T(8,128)(2,1)S(1)} collective-permute-done((bf16[16,512]{1,0:T(8,128)(2,1)S(1)}, bf16[16,512]{1,0:T(8,128)(2,1)S(1)}, u32[]{:S(2)}, u32[]{:S(2)}) %collective-permute-start.19) | collective-permute-done | bytes 16416 | tf_op jit(solution)/shard_map/ppermute | solution.py:25
  66.1 0.6 maximum_select_fusion.3
  (69 shorter events, 1.0 us)
Async XLA Ops:
  0.6 13.3 %copy-start = (bf16[512,1024]{1,0:T(8,128)(2,1)S(1)}, bf16[512,1024]{1,0:T(8,128)(2,1)}, u32[]{:S(2)}) copy-start(bf16[512,1024]{1,0:T(8,128)(2,1)} %param.9) | copy-start | bytes 3145732
  0.6 8.5 %copy-start.4 = (bf16[1,256,1024]{2,1,0:T(8,128)(2,1)S(1)}, bf16[1,256,1024]{2,1,0:T(8,128)(2,1)}, u32[]{:S(2)}) copy-start(bf16[1,256,1024]{2,1,0:T(8,128)(2,1)} %param.14) | copy-start | bytes 1572868
  3.5 13.3 %collective-permute-start.2 = (bf16[144,256]{1,0:T(8,128)(2,1)}, bf16[144,256]{1,0:T(8,128)(2,1)S(1)}, u32[]{:S(2)}, u32[]{:S(2)}) collective-permute-start(bf16[144,256]{1,0:T(8,128)(2,1)} %get-tuple-element.23), channel_id=1, source_target_pairs={{0,24},{2,26},{4,28},{6,30},{8,16},{10,18},{12,20},{14,22},{16,8},... | collective-permute-start | bytes 221192 | tf_op jit(solution)/shard_map/ppermute | solution.py:25
  8.5 8.3 %collective-permute-start.1 = (bf16[144,256]{1,0:T(8,128)(2,1)}, bf16[144,256]{1,0:T(8,128)(2,1)S(1)}, u32[]{:S(2)}, u32[]{:S(2)}) collective-permute-start(bf16[144,256]{1,0:T(8,128)(2,1)} %get-tuple-element.21), channel_id=1, source_target_pairs={{0,16},{2,18},{4,20},{6,22},{8,24},{10,26},{12,28},{14,30},{16,0},... | collective-permute-start | bytes 221192 | tf_op jit(solution)/shard_map/ppermute | solution.py:25
  8.5 8.2 %collective-permute-start = (bf16[272,256]{1,0:T(8,128)(2,1)}, bf16[272,256]{1,0:T(8,128)(2,1)S(1)}, u32[]{:S(2)}, u32[]{:S(2)}) collective-permute-start(bf16[272,256]{1,0:T(8,128)(2,1)} %get-tuple-element.22), channel_id=1, source_target_pairs={{0,8},{2,10},{4,12},{6,14},{8,0},{10,2},{12,4},{14,6},{16,24},{18,... | collective-permute-start | bytes 417800 | tf_op jit(solution)/shard_map/ppermute | solution.py:25
  9.1 1.0 %copy-start.3 = (bf16[1,256,512]{2,1,0:T(8,128)(2,1)S(1)}, bf16[1,256,512]{2,1,0:T(8,128)(2,1)}, u32[]{:S(2)}) copy-start(bf16[1,256,512]{2,1,0:T(8,128)(2,1)} %param.8) | copy-start | bytes 786436
  10.1 1.6 %copy-start.8 = (s32[16]{0:T(128)S(1)}, s32[16]{0:T(128)}, u32[]{:S(2)}) copy-start(s32[16]{0:T(128)} %constant.93.clone) | copy-start | bytes 196
  10.1 21.4 %collective-permute-start.3 = (bf16[512,512]{1,0:T(8,128)(2,1)S(1)}, bf16[512,512]{1,0:T(8,128)(2,1)S(1)}, u32[]{:S(2)}, u32[]{:S(2)}) collective-permute-start(bf16[512,512]{1,0:T(8,128)(2,1)S(1)} %pad_maximum_fusion), channel_id=1, source_target_pairs={{0,8},{2,10},{4,12},{6,14},{8,0},{10,2},{12,4},{14,6},{16,24},{18,... | collective-permute-start | bytes 1572872 | tf_op jit(solution)/shard_map/ppermute | solution.py:25
  11.6 0.7 %copy-start.7 = (s32[1,8,16]{2,1,0:T(8,128)S(1)}, s32[1,8,16]{2,1,0:T(8,128)}, u32[]{:S(2)}) copy-start(s32[1,8,16]{2,1,0:T(8,128)} %blocks_ref.1) | copy-start | bytes 1540
  14.3 2.5 %copy-start.5 = (bf16[144,256]{1,0:T(8,128)(2,1)S(1)}, bf16[144,256]{1,0:T(8,128)(2,1)}, u32[]{:S(2)}) copy-start(bf16[144,256]{1,0:T(8,128)(2,1)} %get-tuple-element.21) | copy-start | bytes 221188
  17.0 3.6 %copy-start.6 = (bf16[128,256]{1,0:T(8,128)(2,1)S(1)}, bf16[128,256]{1,0:T(8,128)(2,1)}, u32[]{:S(2)}) copy-start(bf16[128,256]{1,0:T(8,128)(2,1)} %get-tuple-element.26) | copy-start | bytes 196612
  17.0 15.4 %collective-permute-start.6 = (bf16[544,256]{1,0:T(8,128)(2,1)S(1)}, bf16[544,256]{1,0:T(8,128)(2,1)S(1)}, u32[]{:S(2)}, u32[]{:S(2)}) collective-permute-start(bf16[544,256]{1,0:T(8,128)(2,1)S(1)} %pad_maximum_fusion.2.refs_7_.refs_11_), channel_id=1, source_target_pairs={{0,6},{2,4},{4,2},{6,0},{8,14},{10,12},{12,10},{14,8},{16,22},{18,... | collective-permute-start | bytes 835592 | tf_op jit(solution)/shard_map/ppermute | solution.py:25
  19.6 14.2 %collective-permute-start.5 = (bf16[544,256]{1,0:T(8,128)(2,1)S(1)}, bf16[544,256]{1,0:T(8,128)(2,1)S(1)}, u32[]{:S(2)}, u32[]{:S(2)}) collective-permute-start(bf16[544,256]{1,0:T(8,128)(2,1)S(1)} %pad_maximum_fusion.2.refs_7_.refs_11_), channel_id=1, source_target_pairs={{0,4},{2,6},{4,0},{6,2},{8,12},{10,14},{12,8},{14,10},{16,20},{18,... | collective-permute-start | bytes 835592 | tf_op jit(solution)/shard_map/ppermute | solution.py:25
  20.1 13.7 %collective-permute-start.4 = (bf16[544,256]{1,0:T(8,128)(2,1)S(1)}, bf16[544,256]{1,0:T(8,128)(2,1)S(1)}, u32[]{:S(2)}, u32[]{:S(2)}) collective-permute-start(bf16[544,256]{1,0:T(8,128)(2,1)S(1)} %pad_maximum_fusion.2.refs_7_.refs_11_), channel_id=1, source_target_pairs={{0,2},{2,0},{4,6},{6,4},{8,10},{10,8},{12,14},{14,12},{16,18},{18,... | collective-permute-start | bytes 835592 | tf_op jit(solution)/shard_map/ppermute | solution.py:25
  20.6 8.4 %collective-permute-start.7 = (bf16[2,128,256]{2,1,0:T(8,128)(2,1)S(1)}, bf16[2,128,256]{2,1,0:T(8,128)(2,1)S(1)}, u32[]{:S(2)}, u32[]{:S(2)}) collective-permute-start(bf16[2,128,256]{2,1,0:T(8,128)(2,1)S(1)} %pad_maximum_fusion.3), channel_id=1, source_target_pairs={{0,16},{2,18},{4,20},{6,22},{8,24},{10,26},{12,28},{14,30},{16,0},... | collective-permute-start | bytes 393224 | tf_op jit(solution)/shard_map/ppermute | solution.py:25
  28.9 11.1 %collective-permute-start.10 = (bf16[4,128,256]{2,1,0:T(8,128)(2,1)S(1)}, bf16[4,128,256]{2,1,0:T(8,128)(2,1)S(1)}, u32[]{:S(2)}, u32[]{:S(2)}) collective-permute-start(bf16[4,128,256]{2,1,0:T(8,128)(2,1)S(1)} %constant_dynamic-update-slice_fusion.refs_7_), channel_id=1, source_target_pairs={{0,6},{2,4},{4,2},{6,0},{8,14},{10,12},{12,10},{14,8},{16,22},{18,... | collective-permute-start | bytes 786440 | tf_op jit(solution)/shard_map/ppermute | solution.py:25
  31.5 11.3 %collective-permute-start.9 = (bf16[4,128,256]{2,1,0:T(8,128)(2,1)S(1)}, bf16[4,128,256]{2,1,0:T(8,128)(2,1)S(1)}, u32[]{:S(2)}, u32[]{:S(2)}) collective-permute-start(bf16[4,128,256]{2,1,0:T(8,128)(2,1)S(1)} %constant_dynamic-update-slice_fusion.refs_7_), channel_id=1, source_target_pairs={{0,4},{2,6},{4,0},{6,2},{8,12},{10,14},{12,8},{14,10},{16,20},{18,... | collective-permute-start | bytes 786440 | tf_op jit(solution)/shard_map/ppermute | solution.py:25
  32.3 10.5 %collective-permute-start.8 = (bf16[4,128,256]{2,1,0:T(8,128)(2,1)S(1)}, bf16[4,128,256]{2,1,0:T(8,128)(2,1)S(1)}, u32[]{:S(2)}, u32[]{:S(2)}) collective-permute-start(bf16[4,128,256]{2,1,0:T(8,128)(2,1)S(1)} %constant_dynamic-update-slice_fusion.refs_7_), channel_id=1, source_target_pairs={{0,2},{2,0},{4,6},{6,4},{8,10},{10,8},{12,14},{14,12},{16,18},{18,... | collective-permute-start | bytes 786440 | tf_op jit(solution)/shard_map/ppermute | solution.py:25
  38.8 9.2 %copy-start.1 = (bf16[256,256]{1,0:T(8,128)(2,1)}, bf16[256,256]{1,0:T(8,128)(2,1)S(1)}, u32[]{:S(2)}) copy-start(bf16[256,256]{1,0:T(8,128)(2,1)S(1)} %get-tuple-element.37) | copy-start | bytes 393220
  38.8 10.3 %collective-permute-start.11 = (bf16[2,256,256]{2,1,0:T(8,128)(2,1)S(1)}, bf16[2,256,256]{2,1,0:T(8,128)(2,1)}, u32[]{:S(2)}, u32[]{:S(2)}) collective-permute-start(bf16[2,256,256]{2,1,0:T(8,128)(2,1)S(1)} %get-tuple-element.31), channel_id=1, source_target_pairs={{0,8},{2,10},{4,12},{6,14},{8,0},{10,2},{12,4},{14,6},{16,24},{18,... | collective-permute-start | bytes 786440 | tf_op jit(solution)/shard_map/ppermute | solution.py:25
  48.0 1.6 %collective-permute-start.13 = (bf16[4,4,16,512]{3,2,1,0:T(8,128)(2,1)S(1)}, bf16[4,4,16,512]{3,2,1,0:T(8,128)(2,1)S(1)}, u32[]{:S(2)}, u32[]{:S(2)}) collective-permute-start(bf16[4,4,16,512]{3,2,1,0:T(8,128)(2,1)S(1)} %bitcast.70), channel_id=1, source_target_pairs={{0,1},{1,0},{2,3},{3,2},{4,5},{5,4},{6,7},{7,6},{8,9},{9,8},{10,11... | collective-permute-start | bytes 786440 | tf_op jit(solution)/shard_map/ppermute | solution.py:25
  48.0 9.0 %collective-permute-start.12 = (bf16[2,256,256]{2,1,0:T(8,128)(2,1)S(1)}, bf16[2,256,256]{2,1,0:T(8,128)(2,1)S(1)}, u32[]{:S(2)}, u32[]{:S(2)}) collective-permute-start(bf16[2,256,256]{2,1,0:T(8,128)(2,1)S(1)} %get-tuple-element.32), channel_id=1, source_target_pairs={{0,8},{2,10},{4,12},{6,14},{8,0},{10,2},{12,4},{14,6},{16,24},{18,... | collective-permute-start | bytes 786440 | tf_op jit(solution)/shard_map/ppermute | solution.py:25
  49.7 4.5 %collective-permute-start.15 = (bf16[4,16,512]{2,1,0:T(8,128)(2,1)S(1)}, bf16[4,16,512]{2,1,0:T(8,128)(2,1)S(1)}, u32[]{:S(2)}, u32[]{:S(2)}) collective-permute-start(bf16[4,16,512]{2,1,0:T(8,128)(2,1)S(1)} %get-tuple-element.47), channel_id=1, source_target_pairs={{0,4},{2,6},{4,0},{6,2},{8,12},{10,14},{12,8},{14,10},{16,20},{18,... | collective-permute-start | bytes 196616 | tf_op jit(solution)/shard_map/ppermute | solution.py:25
  51.2 5.8 %collective-permute-start.16 = (bf16[4,16,512]{2,1,0:T(8,128)(2,1)S(1)}, bf16[4,16,512]{2,1,0:T(8,128)(2,1)S(1)}, u32[]{:S(2)}, u32[]{:S(2)}) collective-permute-start(bf16[4,16,512]{2,1,0:T(8,128)(2,1)S(1)} %get-tuple-element.48), channel_id=1, source_target_pairs={{0,6},{2,4},{4,2},{6,0},{8,14},{10,12},{12,10},{14,8},{16,22},{18,... | collective-permute-start | bytes 196616 | tf_op jit(solution)/shard_map/ppermute | solution.py:25
  52.7 4.3 %collective-permute-start.14 = (bf16[4,16,512]{2,1,0:T(8,128)(2,1)S(1)}, bf16[4,16,512]{2,1,0:T(8,128)(2,1)S(1)}, u32[]{:S(2)}, u32[]{:S(2)}) collective-permute-start(bf16[4,16,512]{2,1,0:T(8,128)(2,1)S(1)} %get-tuple-element.49), channel_id=1, source_target_pairs={{0,2},{2,0},{4,6},{6,4},{8,10},{10,8},{12,14},{14,12},{16,18},{18,... | collective-permute-start | bytes 196616 | tf_op jit(solution)/shard_map/ppermute | solution.py:25
  57.0 4.1 %copy-start.2 = (bf16[256,256]{1,0:T(8,128)(2,1)S(1)}, bf16[256,256]{1,0:T(8,128)(2,1)}, u32[]{:S(2)}) copy-start(bf16[256,256]{1,0:T(8,128)(2,1)} %copy-done.1) | copy-start | bytes 393220
  57.1 6.3 %collective-permute-start.17 = (bf16[16,512]{1,0:T(8,128)(2,1)S(1)}, bf16[16,512]{1,0:T(8,128)(2,1)S(1)}, u32[]{:S(2)}, u32[]{:S(2)}) collective-permute-start(bf16[16,512]{1,0:T(8,128)(2,1)S(1)} %get-tuple-element.54), channel_id=1, source_target_pairs={{0,16},{2,18},{4,20},{6,22},{8,24},{10,26},{12,28},{14,30},{16,0},... | collective-permute-start | bytes 49160 | tf_op jit(solution)/shard_map/ppermute | solution.py:25
  60.5 5.5 %collective-permute-start.19 = (bf16[16,512]{1,0:T(8,128)(2,1)S(1)}, bf16[16,512]{1,0:T(8,128)(2,1)S(1)}, u32[]{:S(2)}, u32[]{:S(2)}) collective-permute-start(bf16[16,512]{1,0:T(8,128)(2,1)S(1)} %get-tuple-element.55), channel_id=1, source_target_pairs={{0,24},{2,26},{4,28},{6,30},{8,16},{10,18},{12,20},{14,22},{16,8},... | collective-permute-start | bytes 49160 | tf_op jit(solution)/shard_map/ppermute | solution.py:25
  60.6 5.4 %collective-permute-start.18 = (bf16[16,512]{1,0:T(8,128)(2,1)S(1)}, bf16[16,512]{1,0:T(8,128)(2,1)S(1)}, u32[]{:S(2)}, u32[]{:S(2)}) collective-permute-start(bf16[16,512]{1,0:T(8,128)(2,1)S(1)} %get-tuple-element.56), channel_id=1, source_target_pairs={{0,8},{2,10},{4,12},{6,14},{8,0},{10,2},{12,4},{14,6},{16,24},{18,... | collective-permute-start | bytes 49160 | tf_op jit(solution)/shard_map/ppermute | solution.py:25
